TPU v7x, 256 devices: a whole 4x4x8 slice. The times are simulated.
256 devices in a mesh: pipe: 16 (over x, y), dp: 2 (over z_hi), tensor: 8 (over z_lo, core).
Axes of the slice: x: 4, y: 4, z: 8 (z_hi: 2, z_lo: 4; z = z_hi * 4 + z_lo), core: 2. Of those that a mesh axis runs over, the one named last changes fastest.
Arguments:
- section_states: bfloat16 [16, 2, 256, 8192], P('pipe', 'dp', None, 'tensor'), may hold values from -6 to 6
- key_weight: bfloat16 [16, 8192, 4096], P('pipe', 'dp', 'tensor'), may hold values from -0.0625 to 0.0625
- value_weight: bfloat16 [16, 8192, 4096], P('pipe', 'dp', 'tensor'), may hold values from -0.0625 to 0.0625
- queries: bfloat16 [16, 2, 256, 4096], P('pipe', 'dp', None, 'tensor'), may hold values from -102 to 102
- cotangent: bfloat16 [16, 2, 256, 4096], P('pipe', 'dp', None, 'tensor'), may hold values from -6 to 6
Outputs:
- context: bfloat16 [16, 2, 256, 4096], P('pipe', 'dp', None, 'tensor')
- query_grad: bfloat16 [16, 2, 256, 4096], P('pipe', 'dp', None, 'tensor')
- encoder_grad: bfloat16 [16, 2, 256, 8192], P('pipe', 'dp', None, 'tensor')
All inputs are finite; a program needn't handle non-finite values.
Results may differ from a plain program's by a relative error of at most 0.023.
The roundings to bfloat16 on the way count: a program that leaves them out, or rounds other values in their place, can miss the bound.
Values may be sent and summed in bfloat16 or wider, within the bound.
No kernel may reach another device: no remote copies, remote signals or barrier semaphores. Data moves between devices by JAX's collectives and lax.ppermute only.
A program may use at most 128 MiB of HBM per device.

v0:
```python
import jax
import jax.numpy as jnp
from jax import lax
from jax.sharding import PartitionSpec as P

HD = 128


def broadcast(array, axis, root):
    mine = lax.axis_index(axis) == root
    return lax.psum(jnp.where(mine, array, jnp.zeros_like(array)), axis)


def body(section_states, key_weight, value_weight, queries, cotangent):
    section_count = lax.axis_size("pipe")
    tensor_count = lax.axis_size("tensor")
    midpoint = section_count // 2
    section_index = lax.axis_index("pipe")
    decoder = section_index >= midpoint
    root_piece = section_states[0, 0]
    enc_len = root_piece.shape[0]
    local_width = key_weight.shape[2]
    head_count = local_width // HD
    encoded = broadcast(root_piece, "pipe", midpoint - 1)
    key_full, value_full = (
        lax.all_gather(key_weight[0], "dp", axis=0, tiled=True),
        lax.all_gather(value_weight[0], "dp", axis=0, tiled=True),
    )
    piece = lax.all_gather(encoded, "tensor", axis=1, tiled=True)
    keys_sum = jnp.dot(piece, key_full, preferred_element_type=jnp.float32)
    values_sum = jnp.dot(piece, value_full, preferred_element_type=jnp.float32)
    dec_len = queries.shape[2]
    key_heads = keys_sum.astype(jnp.bfloat16).reshape(enc_len, head_count, HD)
    value_heads = values_sum.astype(jnp.bfloat16).reshape(enc_len, head_count, HD)
    query_heads = queries[0, 0].reshape(dec_len, head_count, HD)
    grad_heads = cotangent[0, 0].reshape(dec_len, head_count, HD)
    score_scale = HD ** (-0.5)
    scores = (
        jnp.einsum("qhd,khd->hqk", query_heads, key_heads, preferred_element_type=jnp.float32)
        * score_scale
    )
    highest = jnp.max(scores, axis=-1, keepdims=True)
    exp_scores = jnp.exp(scores - highest)
    attn_probs = exp_scores / jnp.sum(exp_scores, axis=-1, keepdims=True)
    probs_low = attn_probs.astype(jnp.bfloat16)
    context = jnp.einsum(
        "hqk,khd->qhd", probs_low, value_heads, preferred_element_type=jnp.float32
    ).reshape(dec_len, local_width)
    dprobs = jnp.einsum("qhd,khd->hqk", grad_heads, value_heads, preferred_element_type=jnp.float32)
    delta = jnp.sum(attn_probs * dprobs, axis=-1, keepdims=True)
    dscores = (attn_probs * (dprobs - delta) * score_scale).astype(jnp.bfloat16)
    query_grad = jnp.einsum(
        "hqk,khd->qhd", dscores, key_heads, preferred_element_type=jnp.float32
    ).reshape(dec_len, local_width)
    key_grad = (
        jnp.einsum("hqk,qhd->khd", dscores, query_heads, preferred_element_type=jnp.float32)
        .reshape(enc_len, local_width)
        .astype(jnp.bfloat16)
    )
    value_grad = (
        jnp.einsum("hqk,qhd->khd", probs_low, grad_heads, preferred_element_type=jnp.float32)
        .reshape(enc_len, local_width)
        .astype(jnp.bfloat16)
    )
    keep_term = decoder.astype(jnp.float32)
    term_flat = jnp.einsum("eh,dh->ed", key_grad, key_full, preferred_element_type=jnp.float32)
    term_flat = term_flat + jnp.einsum(
        "eh,dh->ed", value_grad, value_full, preferred_element_type=jnp.float32
    )
    term_flat = term_flat * keep_term
    width = term_flat.shape[1]
    col_block = width // tensor_count
    row_block = enc_len // section_count
    term = term_flat.reshape(section_count, row_block, tensor_count, col_block).transpose(
        0, 2, 1, 3
    )
    term = term.reshape(section_count * tensor_count * row_block, col_block)
    block = lax.psum_scatter(term, ("pipe", "tensor"), scatter_dimension=0, tiled=True)
    gathered = lax.all_gather(block.astype(jnp.bfloat16), "pipe", axis=0, tiled=True)
    grad_out = jnp.where(section_index == midpoint - 1, gathered, jnp.zeros_like(gathered))
    context_out = jnp.where(decoder, context, 0.0).astype(jnp.bfloat16)
    query_out = jnp.where(decoder, query_grad, 0.0).astype(jnp.bfloat16)
    return (context_out[None, None], query_out[None, None], grad_out[None, None])


def solution(mesh):
    placed = (
        P("pipe", "dp", None, "tensor"),
        P("pipe", "dp", "tensor"),
        P("pipe", "dp", "tensor"),
        P("pipe", "dp", None, "tensor"),
        P("pipe", "dp", None, "tensor"),
    )
    return jax.shard_map(
        body,
        mesh=mesh,
        in_specs=placed,
        out_specs=(
            P("pipe", "dp", None, "tensor"),
            P("pipe", "dp", None, "tensor"),
            P("pipe", "dp", None, "tensor"),
        ),
        check_vma=False,
    )
```

profile of v0, /device:TPU:122, one launch (start us, length us, event | category | flops | bytes accessed | tf_op | source)
XLA Modules:
  0.0 1327.5 jit_solution(545324524460453539)
XLA Ops:
  7.2 1.9 select_bitcast_fusion.1
  9.2 97.8 %all-reduce.2.cloned.1.call-done = bf16[256,1024]{1,0:T(8,128)(2,1)} async-done(((bf16[256,1024]{1,0:T(8,128)(2,1)}), bf16[256,1024]{1,0:T(8,128)(2,1)}) %all-reduce.2.cloned.1.call-update) | async-done | bytes 524304 | tf_op jit(solution)/shard_map/psum | solution.py:11
  107.1 0.7 all-gather.10.cloned.1.call-update
  107.9 0.5 all-gather.8.cloned.1.call-update
  108.8 52.5 %all-gather.6.cloned.1.call-done = bf16[256,8192]{1,0:T(8,128)(2,1)} async-done(((bf16[256,1024]{1,0:T(8,128)(2,1)}), bf16[256,8192]{1,0:T(8,128)(2,1)}) %all-gather.6.cloned.1.call-update) | async-done | bytes 4194320 | tf_op jit(solution)/shard_map/all_gather | solution.py:29
  161.3 191.5 %all-gather.10.cloned.1.call-done = bf16[1,8192,512]{2,1,0:T(8,128)(2,1)} async-done(((bf16[1,4096,512]{2,1,0:T(8,128)(2,1)}), bf16[1,8192,512]{2,1,0:T(8,128)(2,1)}) %all-gather.10.cloned.1.call-update) | async-done | bytes 8388624 | tf_op jit(solution)/shard_map/all_gather | solution.py:26
  352.8 7.0 fusion.22
  359.9 195.6 %all-gather.8.cloned.1.call-done = bf16[1,8192,512]{2,1,0:T(8,128)(2,1)} async-done(((bf16[1,4096,512]{2,1,0:T(8,128)(2,1)}), bf16[1,8192,512]{2,1,0:T(8,128)(2,1)}) %all-gather.8.cloned.1.call-update) | async-done | bytes 8388624 | tf_op jit(solution)/shard_map/all_gather | solution.py:27
  555.5 7.0 fusion.25
  562.8 0.5 fusion.46
  563.4 0.8 convolution_convert_fusion
  564.6 5.8 fusion.3
  570.4 9.0 fusion.2
  579.4 11.1 copy.32
  590.5 1.7 bitcast_bitcast_fusion
  592.2 9.9 copy.21
  602.2 0.5 fusion.18
  602.6 0.8 copy.23
  603.5 0.8 fusion.17
  604.2 0.8 copy.22
  605.1 617.6 %reduce-scatter.2.cloned.1.call-done = f32[16,1024]{1,0:T(8,128)} async-done(((f32[2048,1024]{1,0:T(8,128)}), f32[16,1024]{1,0:T(8,128)}) %reduce-scatter.2.cloned.1.call-update) | async-done | bytes 65552 | tf_op jit(solution)/shard_map/reduce_scatter | solution.py:78
  1222.7 0.8 convert_element_type.85
  1223.5 96.7 %all_gather.15 = bf16[256,1024]{1,0:T(8,128)(2,1)S(1)} all-gather(bf16[16,1024]{1,0:T(8,128)(2,1)S(1)} %convert_element_type.85), channel_id=1, replica_groups=mesh['pipe'=16,'dp'=2,'tensor'=8] {'pipe'}, dimensions={0}, use_global_device_ids=true | all-gather | bytes 557056 | tf_op jit(solution)/shard_map/all_gather | solution.py:79
  1320.2 0.8 select_bitcast_fusion
  (17 shorter events, 1.4 us)
Async XLA Ops:
  7.2 101.3 %copy-start = (bf16[1,1,256,512]{3,2,1,0:T(8,128)(2,1)S(1)}, bf16[1,1,256,512]{3,2,1,0:T(8,128)(2,1)}, u32[]{:S(2)}) copy-start(bf16[1,1,256,512]{3,2,1,0:T(8,128)(2,1)} %param.8) | copy-start | bytes 786436
  7.2 101.4 %copy-start.1 = (bf16[1,1,256,512]{3,2,1,0:T(8,128)(2,1)S(1)}, bf16[1,1,256,512]{3,2,1,0:T(8,128)(2,1)}, u32[]{:S(2)}) copy-start(bf16[1,1,256,512]{3,2,1,0:T(8,128)(2,1)} %param.9) | copy-start | bytes 786436
  7.2 99.9 %all-reduce.2.cloned.1.call-start = ((), (), s32[]{:S(2)}) async-start(), calls=%async_computation.1 | async-start | bytes 1048576 | tf_op jit(solution)/shard_map/psum | solution.py:11
  9.2 152.1 %all-gather.6.cloned.1.call-start = ((), (), s32[]{:S(2)}) async-start(), calls=%async_computation.2 | async-start | bytes 4718592 | tf_op jit(solution)/shard_map/all_gather | solution.py:29
  107.1 245.7 %all-gather.10.cloned.1.call-start = ((), (), s32[]{:S(2)}) async-start(), calls=%async_computation.5 | async-start | bytes 12582912 | tf_op jit(solution)/shard_map/all_gather | solution.py:26
  107.8 447.7 %all-gather.8.cloned.1.call-start = ((), (), s32[]{:S(2)}) async-start(), calls=%async_computation.4 | async-start | bytes 12582912 | tf_op jit(solution)/shard_map/all_gather | solution.py:27
  108.4 1114.2 %reduce-scatter.2.cloned.1.call-start = ((), (), s32[]{:S(2)}) async-start(), calls=%async_computation.3 | async-start | bytes 8454144 | tf_op jit(solution)/shard_map/reduce_scatter | solution.py:78
Sparse Core Ops, SparseCore 0:
  11.8 95.2 all-reduce.1
  109.0 52.2 all-gather.5
  163.2 189.5 all-gather.9
  354.6 200.9 all-gather.7
  602.3 620.3 reduce-scatter.1
where the time goes:
time: 1340 us; the launch traced here: 1330 us
  waiting for transfers between devices  1160 us (87%)
  blocking collectives  96.7 us (7%)
  matrix products  32 us (2%)
  local copies, waits for them, and re-layouts  24.8 us (2%)
  between operations  13.9 us (1%)
    reduce_scatter x1, waiting for transfers between devices, body(): lax.psum_scatter(term, ('pipe', 'tensor'), scatter_dimension=0, tiled=True)  618 us
    all_gather x1, waiting for transfers between devices, body(): lax.all_gather(value_weight[0], 'dp', axis=0, tiled=True)  196 us
    all_gather x1, waiting for transfers between devices, body(): lax.all_gather(key_weight[0], 'dp', axis=0, tiled=True)  192 us
    psum x1, waiting for transfers between devices, broadcast(): return lax.psum(jnp.where(mine, array, jnp.zeros_like(array)), axis)  97.8 us
    all_gather x1, blocking collectives, body(): lax.all_gather(block.astype(jnp.bfloat16), 'pipe', axis=0, tiled=True)  96.7 us
    all_gather x1, waiting for transfers between devices, body(): piece = lax.all_gather(encoded, 'tensor', axis=1, tiled=True)  52.5 us
  transfers between devices with their start and end apart: 5, of which 5 were waited for; matrix products, arithmetic and copies ran while one was open for 1% of the time, Pallas kernels for 0%

commit v1 on v0

v1 whole, which is shorter than its diff:
```python
import jax
import jax.numpy as jnp
from jax import lax
from jax.sharding import PartitionSpec as P

HD = 128
AXES = ("pipe", "dp", "tensor")
F32 = jnp.float32
BF16 = jnp.bfloat16


def body(section_states, key_weight, value_weight, queries, cotangent):
    sections = lax.axis_size("pipe")
    replicas = lax.axis_size("dp")
    lanes = lax.axis_size("tensor")
    first = sections // 2
    count = sections - first
    root = first - 1
    section = lax.axis_index("pipe")
    replica = lax.axis_index("dp")
    lane = lax.axis_index("tensor")
    core = lane % 2
    chip = lane // 2
    chips = lanes // 2
    decoder = section >= first

    def place(s, d, t):
        return (s * replicas + d) * lanes + t

    everyone = [(k, d, t) for k in range(count) for d in range(replicas) for t in range(lanes)]

    def send(array, move):
        pairs = []
        for k, d, t in everyone:
            a, b, c = move(k, d, t)
            pairs.append((place(first + k, d, t), place(first + a, b, c)))
        return lax.ppermute(array, AXES, pairs)

    def swap_core(array):
        return send(array, lambda k, d, t: (k, d, t ^ 1))

    def swap_replica(array):
        return send(array, lambda k, d, t: (k, 1 - d, t))

    half = lanes // 2
    piece = section_states[0, 0]
    tokens, block = piece.shape
    rows = tokens // count

    local = key_weight.shape[2]

    def split(weight):
        parts = weight[0].reshape(2, 2, block, local)
        mine = lax.dynamic_index_in_dim(parts, core, 1, keepdims=False).reshape(2 * block, local)
        other = lax.dynamic_index_in_dim(parts, 1 - core, 1, keepdims=False).reshape(
            2 * block, local
        )
        return mine, other

    key_mine, key_other = split(key_weight)
    value_mine, value_other = split(value_weight)
    key_far = swap_core(key_other)
    value_far = swap_core(value_other)
    back = jnp.concatenate([key_mine, value_mine, key_far, value_far], axis=1)

    got = None
    for k in range(count):
        pairs = [
            (place(root, b, half * p + j), place(first + k, p, half * b + j))
            for b in range(replicas)
            for p in range(replicas)
            for j in range(half)
        ]
        part = lax.ppermute(piece[k * rows : (k + 1) * rows], AXES, pairs)
        got = part if got is None else got + part
    held = [got] + [
        send(got, lambda k, d, t, n=n: (k, d, t ^ (2 * n))) for n in range(1, chips)
    ]
    held = jnp.stack(held)

    def pick(array, owner):
        return lax.dynamic_index_in_dim(array, chip ^ owner, 0, keepdims=False)

    chunk = jnp.stack(
        [
            jnp.concatenate([pick(held, 2 * b), pick(held, 2 * b + 1)], axis=1)
            for b in (replica, 1 - replica)
        ]
    )
    chunks = [chunk] + [
        send(chunk, lambda k, d, t, m=m: (k ^ m, d, t)) for m in range(1, count)
    ]
    near = jnp.stack(chunks, axis=1).reshape(replicas * tokens, 2 * block)
    far = swap_core(near)

    def project(mine, other):
        out = jnp.dot(near, mine, preferred_element_type=F32)
        return out + jnp.dot(far, other, preferred_element_type=F32)

    key_part = project(key_mine, key_other)
    key_sum = key_part[:tokens] + swap_replica(key_part[tokens:])
    value_part = project(value_mine, value_other)
    value_sum = value_part[:tokens] + swap_replica(value_part[tokens:].astype(BF16)).astype(F32)

    heads = local // HD
    dec_len = queries.shape[2]
    keys = key_sum.astype(BF16).reshape(tokens, heads, HD)
    values = value_sum.astype(BF16).reshape(tokens, heads, HD)
    query = queries[0, 0].reshape(dec_len, heads, HD)
    grad = cotangent[0, 0].reshape(dec_len, heads, HD)
    scale = HD ** (-0.5)
    scores = jnp.einsum("qhd,khd->hqk", query, keys, preferred_element_type=F32) * scale
    top = jnp.max(scores, axis=-1, keepdims=True)
    weights = jnp.exp(scores - top)
    probs = weights / jnp.sum(weights, axis=-1, keepdims=True)
    low = probs.astype(BF16)
    value_grad = (
        jnp.einsum("hqk,qhd->khd", low, grad, preferred_element_type=F32)
        .reshape(tokens, local)
        .astype(BF16)
    )
    value_grad_far = swap_replica(value_grad)
    dprobs = jnp.einsum("qhd,khd->hqk", grad, values, preferred_element_type=F32)
    delta = jnp.sum(probs * dprobs, axis=-1, keepdims=True)
    dscores = (probs * (dprobs - delta) * scale).astype(BF16)
    key_grad = (
        jnp.einsum("hqk,qhd->khd", dscores, query, preferred_element_type=F32)
        .reshape(tokens, local)
        .astype(BF16)
    )
    key_grad_far = swap_replica(key_grad)
    context = jnp.einsum("hqk,khd->qhd", low, values, preferred_element_type=F32)
    context = context.reshape(dec_len, local)
    query_grad = jnp.einsum("hqk,khd->qhd", dscores, keys, preferred_element_type=F32)
    query_grad = query_grad.reshape(dec_len, local)

    here = jnp.concatenate([key_grad, value_grad], axis=1)
    there = jnp.concatenate([key_grad_far, value_grad_far], axis=1)
    grads = jnp.concatenate(
        [
            jnp.concatenate([here, swap_core(here)], axis=1),
            jnp.concatenate([there, swap_core(there)], axis=1),
        ],
        axis=0,
    )
    term = lax.dot_general(
        grads, back, (((1,), (1,)), ((), ())), preferred_element_type=F32
    )
    term = term.reshape(replicas, count, rows, 2 * block)
    total = term[:, 0]
    term_low = term.astype(BF16)
    for m in range(1, count):
        total = total + send(term_low[:, m], lambda k, d, t, m=m: (k ^ m, d, t)).astype(F32)
    total = total.reshape(replicas, rows, 2, block)

    def owned(array, owner):
        which = (owner // 2) ^ replica
        one = lax.dynamic_index_in_dim(array, which, 0, keepdims=False)
        return lax.dynamic_index_in_dim(one, owner % 2, 1, keepdims=False)

    summed = owned(total, chip)
    for n in range(1, chips):
        away = owned(total, chip ^ n).astype(BF16)
        summed = summed + send(away, lambda k, d, t, n=n: (k, d, t ^ (2 * n))).astype(F32)
    summed = summed.astype(BF16)
    out = []
    for k in range(count):
        pairs = [
            (place(first + k, p, half * b + j), place(root, b, half * p + j))
            for b in range(replicas)
            for p in range(replicas)
            for j in range(half)
        ]
        out.append(lax.ppermute(summed, AXES, pairs))
    encoder_grad = jnp.concatenate(out, axis=0)
    encoder_grad = jnp.where(section == root, encoder_grad, jnp.zeros_like(encoder_grad))
    context = jnp.where(decoder, context, 0.0).astype(BF16)
    query_grad = jnp.where(decoder, query_grad, 0.0).astype(BF16)
    return context[None, None], query_grad[None, None], encoder_grad[None, None]


def solution(mesh):
    wide = P("pipe", "dp", None, "tensor")
    tall = P("pipe", "dp", "tensor")
    return jax.shard_map(
        body,
        mesh=mesh,
        in_specs=(wide, tall, tall, wide, wide),
        out_specs=(wide, wide, wide),
        check_vma=False,
    )
```

time: 1340 us -> 271 us (0.20)
  waiting for transfers between devices: 1160 us -> 149 us
  blocking collectives: 96.7 us -> 0 us
  starting transfers between devices: 0.19 us -> 56 us
    reduce_scatter x1 -> x0, waiting for transfers between devices: 618 us -> none  [body(): lax.psum_scatter(term, ('pipe', 'tensor'), scatter_dimension=0, tiled=True)]
    all_gather x3 -> x0, waiting for transfers between devices: 440 us -> none  [the longest x1 196 us: body(): lax.all_gather(value_weight[0], 'dp', axis=0, tiled=True)]
    ppermute x0 -> x45, waiting for transfers between devices: none -> 149 us  [the longest x8 136 us: body(): out.append(lax.ppermute(summed, AXES, pairs))]
    psum x1 -> x0, waiting for transfers between devices: 97.8 us -> none  [broadcast(): return lax.psum(jnp.where(mine, array, jnp.zeros_like(array)), axis)]
    all_gather x1 -> x0, blocking collectives: 96.7 us -> none  [body(): lax.all_gather(block.astype(jnp.bfloat16), 'pipe', axis=0, tiled=True)]
    ppermute x0 -> x45, starting transfers between devices: none -> 56 us  [the longest x29 29.6 us: send(): return lax.ppermute(array, AXES, pairs)]
    dot_general x9 -> x10, matrix products: 31.5 us -> 28.9 us  [the longest x2 7.78 us: project(): return out + jnp.dot(far, other, preferred_element_type=F32)]
  transfers between devices with their start and end apart: 5 -> 45, of which waited for: 5 -> 13; matrix products, arithmetic and copies ran while one was open for 1% -> 14% of each run, Pallas kernels for 0% -> 0%
where the time goes in v1:
time: 271 us; the launch traced here: 269 us
  waiting for transfers between devices  149 us (55%)
  starting transfers between devices  56 us (21%)
  matrix products  31.4 us (12%)
  local copies, waits for them, and re-layouts  22.6 us (8%)
  other arithmetic  8.52 us (3%)
    ppermute x8, waiting for transfers between devices, body(): out.append(lax.ppermute(summed, AXES, pairs))  136 us
    ppermute x29, starting transfers between devices, send(): return lax.ppermute(array, AXES, pairs)  29.6 us
    ppermute x8, starting transfers between devices, body(): part = lax.ppermute(piece[k * rows:(k + 1) * rows], AXES, pairs)  16.1 us
    ppermute x8, waiting for transfers between devices, body(): part = lax.ppermute(piece[k * rows:(k + 1) * rows], AXES, pairs)  13.3 us
    ppermute x8, starting transfers between devices, body(): out.append(lax.ppermute(summed, AXES, pairs))  10.3 us
    unnamed x44, local copies, waits for them, and re-layouts  9.79 us
    dot_general x2, matrix products, project(): return out + jnp.dot(far, other, preferred_element_type=F32)  7.78 us
    dot_general x1, matrix products, body(): lax.dot_general(grads, back, (((1,), (1,)), ((), ())), preferred_element_...  6.96 us
  transfers between devices with their start and end apart: 45, of which 13 were waited for; matrix products, arithmetic and copies ran while one was open for 14% of the time, Pallas kernels for 0%

profile of v1, /device:TPU:122, one launch (start us, length us, event | category | flops | bytes accessed | tf_op | source)
XLA Modules:
  0.0 269.2 jit_solution(7532969992369969217)
XLA Ops:
  1.7 7.1 %collective-permute-start.7 = (bf16[32,1024]{1,0:T(8,128)(2,1)S(1)}, bf16[32,1024]{1,0:T(8,128)(2,1)S(1)}, u32[]{:S(2)}, u32[]{:S(2)}) collective-permute-start(bf16[32,1024]{1,0:T(8,128)(2,1)S(1)} %get-tuple-element.38), channel_id=1, source_target_pairs={{112,240},{113,241},{114,242},{115,243},{116,248},{117,249},{118,2... | collective-permute-start | bytes 196616 | tf_op jit(solution)/shard_map/ppermute | solution.py:74
  14.0 7.8 %collective-permute-done.7 = bf16[32,1024]{1,0:T(8,128)(2,1)S(1)} collective-permute-done((bf16[32,1024]{1,0:T(8,128)(2,1)S(1)}, bf16[32,1024]{1,0:T(8,128)(2,1)S(1)}, u32[]{:S(2)}, u32[]{:S(2)}) %collective-permute-start.7) | collective-permute-done | bytes 65568 | tf_op jit(solution)/shard_map/ppermute | solution.py:74
  26.1 1.4 collective-permute-done.3
  44.0 2.1 collective-permute-start.18
  46.1 6.2 %constant_dynamic-slice_fusion.2 = (bf16[2,1,1024,512]{3,2,1,0:T(8,128)(2,1)S(1)}, bf16[2,1,1024,512]{3,2,1,0:T(8,128)(2,1)}, bf16[2,1,1024,512]{3,2,1,0:T(8,128)(2,1)}, bf16[2,1,1024,512]{3,2,1,0:T(8,128)(2,1)S(1)}) fusion(bf16[2,2,1024,512]{3,2,1,0:T(8,128)(2,1)} %bitcast.187, s32[]{:T(128)S(6)} %select_n.155, s32[]{:T(128)S(6)} %select_n.156, ...), kind=kLoop, calls=%fused_computation.114 | loop fusion | bytes 16777224 | tf_op jit(solution)/shard_map/jit(dynamic_index_in_dim)/dynamic_slice | solution.py:54
  52.4 4.3 %fusion.58 = f32[512,512]{0,1:T(8,128)S(1)} fusion(bf16[512,2048]{1,0:T(8,128)(2,1)} %collective-permute-done.18, bf16[2048,512]{1,0:T(8,128)(2,1)} %bitcast.36), kind=kOutput, calls=%fused_computation.126 | convolution fusion | flops 1073741824 | bytes 5242880 | tf_op jit(solution)/shard_map/dot_general | solution.py:98
  56.6 2.9 %convolution_add_fusion.1 = f32[512,512]{0,1:T(8,128)S(1)} fusion(f32[512,512]{0,1:T(8,128)S(1)} %fusion.58, bf16[512,2048]{1,0:T(8,128)(2,1)} %bitcast.33, bf16[2048,512]{1,0:T(8,128)(2,1)S(1)} %bitcast.191), kind=kOutput, calls=%fused_computation.30 | convolution fusion | flops 1074003968 | bytes 6291456 | tf_op jit(solution)/shard_map/dot_general | solution.py:97
  61.7 3.5 %fusion.59 = f32[512,512]{0,1:T(8,128)S(1)} fusion(bf16[512,2048]{1,0:T(8,128)(2,1)} %collective-permute-done.18, bf16[2048,512]{1,0:T(8,128)(2,1)} %bitcast.40), kind=kOutput, calls=%fused_computation.127 | convolution fusion | flops 1073741824 | bytes 5242880 | tf_op jit(solution)/shard_map/dot_general | solution.py:98
  65.2 2.9 %convolution_add_fusion = f32[512,512]{0,1:T(8,128)S(1)} fusion(f32[512,512]{0,1:T(8,128)S(1)} %fusion.59, bf16[512,2048]{1,0:T(8,128)(2,1)} %bitcast.33, bf16[2048,512]{1,0:T(8,128)(2,1)S(1)} %bitcast.189), kind=kOutput, calls=%fused_computation.29 | convolution fusion | flops 1074003968 | bytes 6291456 | tf_op jit(solution)/shard_map/dot_general | solution.py:97
  69.9 1.4 collective-permute-start.20
  71.4 2.1 collective-permute-start.26
  73.4 2.0 collective-permute-start.25
  78.9 1.8 fusion.41
  80.7 2.5 fusion.57
  83.2 2.5 convolution_convert_fusion
  87.1 2.8 %convolution_convert_fusion.1 = bf16[4,256,128]{1,2,0:T(8,128)(2,1)} fusion(bf16[256,4,128]{0,2,1:T(8,128)(2,1)} %bitcast.205, f32[4,256,256]{1,2,0:T(8,128)S(1)} %convolution_bitcast_fusion, f32[4,256,256]{1,2,0:T(8,128)} %get-tuple-element.45, f32[4,256]{1,0:T(4,128)S(1)} %get-tuple-element.44), kind=kOutput, calls=%fused_computation.37 | convolution fusion | flops 69076224 | bytes 2625536 | tf_op jit(solution)/shard_map/hqk,qhd->khd/dot_general | solution.py:127
  94.3 7.0 %fusion.2 = f32[512,2048]{1,0:T(8,128)S(1)} fusion(bf16[2048,512]{1,0:T(8,128)(2,1)} %collective-permute-done.26, bf16[2048,512]{1,0:T(8,128)(2,1)} %collective-permute-done.25, bf16[2048,512]{1,0:T(8,128)(2,1)S(1)} %bitcast.192, bf16[2048,512]{1,0:T(8,128)(2,1)S(1)} %bitcast.190, bf16[256,1024]{0,1:T(8,128)(2,1)S(1)} %collective-permute-done.24, ...), kind=kOutput, calls=%fused_computation.2 | convolution fusion | flops 4341104640 | bytes 14680064 | tf_op jit(solution)/shard_map/dot_general | solution.py:146
  101.3 1.9 copy-done.2
  113.3 1.9 fusion.40
  119.6 2.0 fusion.29
  128.5 122.0 %collective-permute-done.37 = bf16[32,1024]{1,0:T(8,128)(2,1)S(1)} collective-permute-done((bf16[32,1024]{1,0:T(8,128)(2,1)S(1)}, bf16[32,1024]{1,0:T(8,128)(2,1)S(1)}, u32[]{:S(2)}, u32[]{:S(2)}) %collective-permute-start.37) | collective-permute-done | bytes 65568 | tf_op jit(solution)/shard_map/ppermute | solution.py:174
  251.8 4.6 %collective-permute-done.38 = bf16[32,1024]{1,0:T(8,128)(2,1)S(1)} collective-permute-done((bf16[32,1024]{1,0:T(8,128)(2,1)S(1)}, bf16[32,1024]{1,0:T(8,128)(2,1)S(1)}, u32[]{:S(2)}, u32[]{:S(2)}) %collective-permute-start.38) | collective-permute-done | bytes 65568 | tf_op jit(solution)/shard_map/ppermute | solution.py:174
  259.1 4.5 %collective-permute-done.42 = bf16[32,1024]{1,0:T(8,128)(2,1)S(1)} collective-permute-done((bf16[32,1024]{1,0:T(8,128)(2,1)S(1)}, bf16[32,1024]{1,0:T(8,128)(2,1)S(1)}, u32[]{:S(2)}, u32[]{:S(2)}) %collective-permute-start.42) | collective-permute-done | bytes 65568 | tf_op jit(solution)/shard_map/ppermute | solution.py:174
  263.6 4.4 %collective-permute-done.43 = bf16[32,1024]{1,0:T(8,128)(2,1)S(1)} collective-permute-done((bf16[32,1024]{1,0:T(8,128)(2,1)S(1)}, bf16[32,1024]{1,0:T(8,128)(2,1)S(1)}, u32[]{:S(2)}, u32[]{:S(2)}) %collective-permute-start.43) | collective-permute-done | bytes 65568 | tf_op jit(solution)/shard_map/ppermute | solution.py:174
  (146 shorter events, 66.3 us)
Async XLA Ops:
  1.7 20.0 %collective-permute-start.7 = (bf16[32,1024]{1,0:T(8,128)(2,1)S(1)}, bf16[32,1024]{1,0:T(8,128)(2,1)S(1)}, u32[]{:S(2)}, u32[]{:S(2)}) collective-permute-start(bf16[32,1024]{1,0:T(8,128)(2,1)S(1)} %get-tuple-element.38), channel_id=1, source_target_pairs={{112,240},{113,241},{114,242},{115,243},{116,248},{117,249},{118,2... | collective-permute-start | bytes 196616 | tf_op jit(solution)/shard_map/ppermute | solution.py:74
  8.8 14.5 %collective-permute-start.6 = (bf16[32,1024]{1,0:T(8,128)(2,1)S(1)}, bf16[32,1024]{1,0:T(8,128)(2,1)S(1)}, u32[]{:S(2)}, u32[]{:S(2)}) collective-permute-start(bf16[32,1024]{1,0:T(8,128)(2,1)S(1)} %get-tuple-element.39), channel_id=1, source_target_pairs={{112,224},{113,225},{114,226},{115,227},{116,232},{117,233},{118,2... | collective-permute-start | bytes 196616 | tf_op jit(solution)/shard_map/ppermute | solution.py:74
  10.1 14.6 %collective-permute-start.5 = (bf16[32,1024]{1,0:T(8,128)(2,1)S(1)}, bf16[32,1024]{1,0:T(8,128)(2,1)S(1)}, u32[]{:S(2)}, u32[]{:S(2)}) collective-permute-start(bf16[32,1024]{1,0:T(8,128)(2,1)S(1)} %get-tuple-element.33), channel_id=1, source_target_pairs={{112,208},{113,209},{114,210},{115,211},{116,216},{117,217},{118,2... | collective-permute-start | bytes 196616 | tf_op jit(solution)/shard_map/ppermute | solution.py:74
  11.4 14.7 %collective-permute-start.4 = (bf16[32,1024]{1,0:T(8,128)(2,1)S(1)}, bf16[32,1024]{1,0:T(8,128)(2,1)S(1)}, u32[]{:S(2)}, u32[]{:S(2)}) collective-permute-start(bf16[32,1024]{1,0:T(8,128)(2,1)S(1)} %get-tuple-element.34), channel_id=1, source_target_pairs={{112,192},{113,193},{114,194},{115,195},{116,200},{117,201},{118,2... | collective-permute-start | bytes 196616 | tf_op jit(solution)/shard_map/ppermute | solution.py:74
  12.7 14.8 %collective-permute-start.3 = (bf16[32,1024]{1,0:T(8,128)(2,1)S(1)}, bf16[32,1024]{1,0:T(8,128)(2,1)S(1)}, u32[]{:S(2)}, u32[]{:S(2)}) collective-permute-start(bf16[32,1024]{1,0:T(8,128)(2,1)S(1)} %get-tuple-element.35), channel_id=1, source_target_pairs={{112,176},{113,177},{114,178},{115,179},{116,184},{117,185},{118,1... | collective-permute-start | bytes 196616 | tf_op jit(solution)/shard_map/ppermute | solution.py:74
  21.8 7.2 %collective-permute-start.2 = (bf16[32,1024]{1,0:T(8,128)(2,1)S(1)}, bf16[32,1024]{1,0:T(8,128)(2,1)S(1)}, u32[]{:S(2)}, u32[]{:S(2)}) collective-permute-start(bf16[32,1024]{1,0:T(8,128)(2,1)S(1)} %get-tuple-element.36), channel_id=1, source_target_pairs={{112,160},{113,161},{114,162},{115,163},{116,168},{117,169},{118,1... | collective-permute-start | bytes 196616 | tf_op jit(solution)/shard_map/ppermute | solution.py:74
  23.3 7.0 %collective-permute-start = (bf16[32,1024]{1,0:T(8,128)(2,1)S(1)}, bf16[32,1024]{1,0:T(8,128)(2,1)S(1)}, u32[]{:S(2)}, u32[]{:S(2)}) collective-permute-start(bf16[32,1024]{1,0:T(8,128)(2,1)S(1)} %get-tuple-element.37), channel_id=1, source_target_pairs={{112,128},{113,129},{114,130},{115,131},{116,136},{117,137},{118,1... | collective-permute-start | bytes 196616 | tf_op jit(solution)/shard_map/ppermute | solution.py:74
  24.7 6.5 %collective-permute-start.1 = (bf16[32,1024]{1,0:T(8,128)(2,1)S(1)}, bf16[32,1024]{1,0:T(8,128)(2,1)S(1)}, u32[]{:S(2)}, u32[]{:S(2)}) collective-permute-start(bf16[32,1024]{1,0:T(8,128)(2,1)S(1)} %get-tuple-element.32), channel_id=1, source_target_pairs={{112,144},{113,145},{114,146},{115,147},{116,152},{117,153},{118,1... | collective-permute-start | bytes 196616 | tf_op jit(solution)/shard_map/ppermute | solution.py:74
  44.0 8.3 %collective-permute-start.18 = (bf16[512,2048]{1,0:T(8,128)(2,1)}, bf16[512,2048]{1,0:T(8,128)(2,1)}, u32[]{:S(2)}, u32[]{:S(2)}) collective-permute-start(bf16[512,2048]{1,0:T(8,128)(2,1)} %bitcast.33), channel_id=1, source_target_pairs={{128,129},{129,128},{130,131},{131,130},{132,133},{133,132},{134,1... | collective-permute-start | bytes 6291464 | tf_op jit(solution)/shard_map/ppermute | solution.py:37
  60.3 17.1 %collective-permute-start.19 = (bf16[256,512]{0,1:T(8,128)(2,1)}, bf16[256,512]{0,1:T(8,128)(2,1)}, u32[]{:S(2)}, u32[]{:S(2)}) collective-permute-start(bf16[256,512]{0,1:T(8,128)(2,1)} %slice.162), channel_id=1, source_target_pairs={{128,136},{129,137},{130,138},{131,139},{132,140},{133,141},{134,1... | collective-permute-start | bytes 786440 | tf_op jit(solution)/shard_map/ppermute | solution.py:37
  69.9 8.9 %collective-permute-start.20 = (f32[256,512]{0,1:T(8,128)}, f32[256,512]{0,1:T(8,128)}, u32[]{:S(2)}, u32[]{:S(2)}) collective-permute-start(f32[256,512]{0,1:T(8,128)} %slice.116), channel_id=1, source_target_pairs={{128,136},{129,137},{130,138},{131,139},{132,140},{133,141},{134,1... | collective-permute-start | bytes 1572872 | tf_op jit(solution)/shard_map/ppermute | solution.py:37
  71.4 22.9 %collective-permute-start.26 = (bf16[2048,512]{1,0:T(8,128)(2,1)}, bf16[2048,512]{1,0:T(8,128)(2,1)}, u32[]{:S(2)}, u32[]{:S(2)}) collective-permute-start(bf16[2048,512]{1,0:T(8,128)(2,1)} %bitcast.36), channel_id=1, source_target_pairs={{128,129},{129,128},{130,131},{131,130},{132,133},{133,132},{134,1... | collective-permute-start | bytes 6291464 | tf_op jit(solution)/shard_map/ppermute | solution.py:37
  73.4 20.9 %collective-permute-start.25 = (bf16[2048,512]{1,0:T(8,128)(2,1)}, bf16[2048,512]{1,0:T(8,128)(2,1)}, u32[]{:S(2)}, u32[]{:S(2)}) collective-permute-start(bf16[2048,512]{1,0:T(8,128)(2,1)} %bitcast.40), channel_id=1, source_target_pairs={{128,129},{129,128},{130,131},{131,130},{132,133},{133,132},{134,1... | collective-permute-start | bytes 6291464 | tf_op jit(solution)/shard_map/ppermute | solution.py:37
  85.7 6.7 %collective-permute-start.23 = (bf16[256,512]{0,1:T(8,128)(2,1)}, bf16[256,512]{0,1:T(8,128)(2,1)}, u32[]{:S(2)}, u32[]{:S(2)}) collective-permute-start(bf16[256,512]{0,1:T(8,128)(2,1)} %bitcast.209), channel_id=1, source_target_pairs={{128,136},{129,137},{130,138},{131,139},{132,140},{133,141},{134,1... | collective-permute-start | bytes 786440 | tf_op jit(solution)/shard_map/ppermute | solution.py:37
  104.9 8.3 %collective-permute-start.31 = (bf16[2,32,2048]{2,1,0:T(8,128)(2,1)S(1)}, bf16[2,32,2048]{2,1,0:T(8,128)(2,1)}, u32[]{:S(2)}, u32[]{:S(2)}) collective-permute-start(bf16[2,32,2048]{2,1,0:T(8,128)(2,1)S(1)} %get-tuple-element.25), channel_id=1, source_target_pairs={{128,208},{129,209},{130,210},{131,211},{132,212},{133,213},{134,2... | collective-permute-start | bytes 786440 | tf_op jit(solution)/shard_map/ppermute | solution.py:37
  106.3 7.0 %collective-permute-start.30 = (bf16[2,32,2048]{2,1,0:T(8,128)(2,1)S(1)}, bf16[2,32,2048]{2,1,0:T(8,128)(2,1)}, u32[]{:S(2)}, u32[]{:S(2)}) collective-permute-start(bf16[2,32,2048]{2,1,0:T(8,128)(2,1)S(1)} %get-tuple-element.26), channel_id=1, source_target_pairs={{128,192},{129,193},{130,194},{131,195},{132,196},{133,197},{134,1... | collective-permute-start | bytes 786440 | tf_op jit(solution)/shard_map/ppermute | solution.py:37
  118.3 132.2 %collective-permute-start.37 = (bf16[32,1024]{1,0:T(8,128)(2,1)S(1)}, bf16[32,1024]{1,0:T(8,128)(2,1)S(1)}, u32[]{:S(2)}, u32[]{:S(2)}) collective-permute-start(bf16[32,1024]{1,0:T(8,128)(2,1)S(1)} %fusion.49), channel_id=1, source_target_pairs={{128,112},{129,113},{130,114},{131,115},{136,116},{137,117},{138,1... | collective-permute-start | bytes 196616 | tf_op jit(solution)/shard_map/ppermute | solution.py:174
  123.3 133.1 %collective-permute-start.38 = (bf16[32,1024]{1,0:T(8,128)(2,1)S(1)}, bf16[32,1024]{1,0:T(8,128)(2,1)S(1)}, u32[]{:S(2)}, u32[]{:S(2)}) collective-permute-start(bf16[32,1024]{1,0:T(8,128)(2,1)S(1)} %fusion.49), channel_id=1, source_target_pairs={{144,112},{145,113},{146,114},{147,115},{152,116},{153,117},{154,1... | collective-permute-start | bytes 196616 | tf_op jit(solution)/shard_map/ppermute | solution.py:174
  124.6 133.1 %collective-permute-start.39 = (bf16[32,1024]{1,0:T(8,128)(2,1)S(1)}, bf16[32,1024]{1,0:T(8,128)(2,1)S(1)}, u32[]{:S(2)}, u32[]{:S(2)}) collective-permute-start(bf16[32,1024]{1,0:T(8,128)(2,1)S(1)} %fusion.49), channel_id=1, source_target_pairs={{160,112},{161,113},{162,114},{163,115},{168,116},{169,117},{170,1... | collective-permute-start | bytes 196616 | tf_op jit(solution)/shard_map/ppermute | solution.py:174
  125.9 133.2 %collective-permute-start.40 = (bf16[32,1024]{1,0:T(8,128)(2,1)S(1)}, bf16[32,1024]{1,0:T(8,128)(2,1)S(1)}, u32[]{:S(2)}, u32[]{:S(2)}) collective-permute-start(bf16[32,1024]{1,0:T(8,128)(2,1)S(1)} %fusion.49), channel_id=1, source_target_pairs={{176,112},{177,113},{178,114},{179,115},{184,116},{185,117},{186,1... | collective-permute-start | bytes 196616 | tf_op jit(solution)/shard_map/ppermute | solution.py:174
  127.2 131.9 %collective-permute-start.41 = (bf16[32,1024]{1,0:T(8,128)(2,1)S(1)}, bf16[32,1024]{1,0:T(8,128)(2,1)S(1)}, u32[]{:S(2)}, u32[]{:S(2)}) collective-permute-start(bf16[32,1024]{1,0:T(8,128)(2,1)S(1)} %fusion.49), channel_id=1, source_target_pairs={{192,112},{193,113},{194,114},{195,115},{200,116},{201,117},{202,1... | collective-permute-start | bytes 196616 | tf_op jit(solution)/shard_map/ppermute | solution.py:174
  250.5 13.1 %collective-permute-start.42 = (bf16[32,1024]{1,0:T(8,128)(2,1)S(1)}, bf16[32,1024]{1,0:T(8,128)(2,1)S(1)}, u32[]{:S(2)}, u32[]{:S(2)}) collective-permute-start(bf16[32,1024]{1,0:T(8,128)(2,1)S(1)} %fusion.49), channel_id=1, source_target_pairs={{208,112},{209,113},{210,114},{211,115},{216,116},{217,117},{218,1... | collective-permute-start | bytes 196616 | tf_op jit(solution)/shard_map/ppermute | solution.py:174
  256.4 11.6 %collective-permute-start.43 = (bf16[32,1024]{1,0:T(8,128)(2,1)S(1)}, bf16[32,1024]{1,0:T(8,128)(2,1)S(1)}, u32[]{:S(2)}, u32[]{:S(2)}) collective-permute-start(bf16[32,1024]{1,0:T(8,128)(2,1)S(1)} %fusion.49), channel_id=1, source_target_pairs={{224,112},{225,113},{226,114},{227,115},{232,116},{233,117},{234,1... | collective-permute-start | bytes 196616 | tf_op jit(solution)/shard_map/ppermute | solution.py:174
  257.7 10.7 %collective-permute-start.44 = (bf16[32,1024]{1,0:T(8,128)(2,1)S(1)}, bf16[32,1024]{1,0:T(8,128)(2,1)S(1)}, u32[]{:S(2)}, u32[]{:S(2)}) collective-permute-start(bf16[32,1024]{1,0:T(8,128)(2,1)S(1)} %fusion.49), channel_id=1, source_target_pairs={{240,112},{241,113},{242,114},{243,115},{248,116},{249,117},{250,1... | collective-permute-start | bytes 196616 | tf_op jit(solution)/shard_map/ppermute | solution.py:174
  (34 other events, 138.5 us)

commit v2 on v1

v2 whole, which is shorter than its diff:
```python
import functools

import jax
import jax.numpy as jnp
from jax import lax
from jax.experimental import pallas as pl
from jax.experimental.pallas import tpu as pltpu
from jax.sharding import PartitionSpec as P

HD = 128
AXES = ("pipe", "dp", "tensor")
F32 = jnp.float32
BF16 = jnp.bfloat16
SCALE = HD ** (-0.5)
VMEM = 20 * 1024 * 1024
VMEM_BACK = 48 * 1024 * 1024
BACK_COST = 8 << 20
NT = (((1,), (1,)), ((), ()))
TN = (((0,), (0,)), ((), ()))


def params():
    return pltpu.CompilerParams(vmem_limit_bytes=VMEM)


def like(shape, dtype):
    return jax.ShapeDtypeStruct(shape, dtype)


def dot(a, b, dims=(((1,), (0,)), ((), ()))):
    return lax.dot_general(a, b, dims, preferred_element_type=F32)


def cost(moved=1):
    return pl.CostEstimate(flops=1, bytes_accessed=moved, transcendentals=0)


def whole(count):
    return [pl.BlockSpec(memory_space=pltpu.VMEM)] * count


def scalar():
    return [pl.BlockSpec(memory_space=pltpu.SMEM)]


def rows_of(weight, index, size):
    return weight[pl.ds(pl.multiple_of(index * size, size), size), :]


def product_near(core, near, key_weight, value_weight, block):
    count, sequences, rows, width = near.shape
    tokens = count * sequences * rows
    cols = key_weight.shape[1]
    step = block // 2

    def kernel(core_ref, x_ref, wk, wv, ok, ov):
        x = x_ref[...].reshape(tokens, step)
        shape = (count, sequences, rows, cols)

        @pl.when(pl.program_id(0) == 0)
        def _():
            ok[...] = dot(x, wk[...]).reshape(shape)
            ov[...] = dot(x, wv[...]).reshape(shape)

        @pl.when(pl.program_id(0) > 0)
        def _():
            ok[...] += dot(x, wk[...]).reshape(shape)
            ov[...] += dot(x, wv[...]).reshape(shape)

    def place(i, c):
        return ((i // 2 * 2 + c[0]) * 2 + i % 2, 0)

    return pl.pallas_call(
        kernel,
        grid_spec=pltpu.PrefetchScalarGridSpec(
            num_scalar_prefetch=1,
            grid=(width // step,),
            in_specs=[
                pl.BlockSpec((count, sequences, rows, step), lambda i, c: (0, 0, 0, i)),
                pl.BlockSpec((step, cols), place),
                pl.BlockSpec((step, cols), place),
            ],
            out_specs=[
                pl.BlockSpec((count, sequences, rows, cols), lambda i, c: (0, 0, 0, 0))
            ]
            * 2,
        ),
        out_shape=[like((count, sequences, rows, cols), F32)] * 2,
        cost_estimate=cost(),
        compiler_params=params(),
    )(core, near, key_weight, value_weight)


def product_far(core, far, weights, parts, block, which, sent):
    count, sequences, rows, width = far.shape
    tokens = count * rows
    cols = weights[0].shape[1]
    many = len(weights)

    def kernel(core_ref, x_ref, *refs):
        ws, ps, outs = (refs[n * many : (n + 1) * many] for n in range(3))
        c = 1 - core_ref[0]
        for w, p, out in zip(ws, ps, outs):
            total = p[:, which].reshape(tokens, cols)
            for j in range(2):
                x = x_ref[:, which, :, j * block : (j + 1) * block].reshape(tokens, block)
                total = total + dot(x, rows_of(w, 2 * j + c, block))
            out[...] = total.astype(out.dtype)

    return pl.pallas_call(
        kernel,
        in_specs=scalar() + whole(1 + 2 * many),
        out_specs=whole(many),
        out_shape=[like((tokens, cols), t) for t in sent],
        cost_estimate=cost(),
        compiler_params=params(),
    )(core, far, *weights, *parts)


def other_rows(core, key_weight, value_weight, block, after):
    height, cols = key_weight.shape
    step = block // 2

    def kernel(core_ref, wk, wv, after_ref, out):
        out[0] = wk[...]
        out[1] = wv[...]

    def place(i, c):
        return ((i // 2 * 2 + 1 - c[0]) * 2 + i % 2, 0)

    return pl.pallas_call(
        kernel,
        grid_spec=pltpu.PrefetchScalarGridSpec(
            num_scalar_prefetch=1,
            grid=(4,),
            in_specs=[pl.BlockSpec((step, cols), place)] * 2
            + [pl.BlockSpec(memory_space=pl.ANY)],
            out_specs=pl.BlockSpec((2, step, cols), lambda i, c: (0, i, 0)),
        ),
        out_shape=like((2, height // 2, cols), BF16),
        cost_estimate=cost(),
        compiler_params=params(),
    )(core, key_weight, value_weight, after)


def attend(key_own, key_in, value_own, value_in, query, grad):
    tokens, local = key_own.shape
    dec = query.shape[0]
    heads = local // HD

    def kernel(ka, kb, va, vb, q, g, keys, values, low, dscores, grads):
        for h in range(heads):
            at = slice(h * HD, (h + 1) * HD)
            k = (ka[:, at] + kb[:, at]).astype(BF16)
            v = (va[:, at] + vb[:, at].astype(F32)).astype(BF16)
            keys[:, at] = k
            values[:, at] = v
            scores = dot(q[:, at], k, NT) * SCALE
            top = jnp.max(scores, axis=-1, keepdims=True)
            e = jnp.exp(scores - top)
            p = e / jnp.sum(e, axis=-1, keepdims=True)
            rounded = p.astype(BF16)
            low[h] = rounded
            dprobs = dot(g[:, at], v, NT)
            delta = jnp.sum(p * dprobs, axis=-1, keepdims=True)
            ds = (p * (dprobs - delta) * SCALE).astype(BF16)
            dscores[h] = ds
            grads[:, at] = dot(ds, q[:, at], TN).astype(BF16)
            start = local + h * HD
            grads[:, start : start + HD] = dot(rounded, g[:, at], TN).astype(BF16)

    return pl.pallas_call(
        kernel,
        in_specs=whole(6),
        out_specs=whole(5),
        out_shape=[
            like((tokens, local), BF16),
            like((tokens, local), BF16),
            like((heads, dec, tokens), BF16),
            like((heads, dec, tokens), BF16),
            like((tokens, 2 * local), BF16),
        ],
        cost_estimate=cost(),
        compiler_params=params(),
    )(key_own, key_in, value_own, value_in, query, grad)


def attend_out(keep, low, values, dscores, keys):
    tokens, local = values.shape
    heads, dec = low.shape[:2]

    def kernel(keep_ref, p, v, ds, k, context, query_grad):
        on = keep_ref[0] > 0
        for h in range(heads):
            at = slice(h * HD, (h + 1) * HD)
            context[:, at] = jnp.where(on, dot(p[h], v[:, at]), 0.0).astype(BF16)
            query_grad[:, at] = jnp.where(on, dot(ds[h], k[:, at]), 0.0).astype(BF16)

    return pl.pallas_call(
        kernel,
        in_specs=scalar() + whole(4),
        out_specs=whole(2),
        out_shape=[like((dec, local), BF16)] * 2,
        cost_estimate=cost(),
        compiler_params=params(),
    )(keep, low, values, dscores, keys)


def back_product_near(core, mine, others, key_weight, value_weight, weights_far, block, count):
    tokens = mine[0].shape[0]
    cols = key_weight.shape[1]
    width = 2 * block
    step = block // 2
    rows = tokens // count
    split = len(mine), len(mine) + len(others)

    def kernel(core_ref, *refs):
        wk, wv, far, low = refs[split[1] :]
        c = core_ref[0]

        def pair(arrays):
            if len(arrays) == 1:
                return arrays[0][:, :cols], arrays[0][:, cols:]
            return arrays[0][...], arrays[1][...]

        (kg, vg), (kh, vh) = pair(refs[: split[0]]), pair(refs[split[0] : split[1]])
        for i in range(width // step):
            at = (i // 2 * 2 + c) * 2 + i % 2
            total = dot(kg, rows_of(wk, at, step), NT)
            total += dot(vg, rows_of(wv, at, step), NT)
            total += dot(kh, far[0, i * step : (i + 1) * step, :], NT)
            total += dot(vh, far[1, i * step : (i + 1) * step, :], NT)
            low[:, :, i * step : (i + 1) * step] = total.reshape(count, rows, step).astype(BF16)

    return pl.pallas_call(
        kernel,
        in_specs=scalar() + whole(split[1] + 3),
        out_specs=whole(1)[0],
        out_shape=like((count, rows, width), BF16),
        cost_estimate=cost(),
        compiler_params=params(),
    )(core, *mine, *others, key_weight, value_weight, weights_far)


def back_product(core, mine, others, key_weight, value_weight, weights_far, block, count):
    tokens = mine[0].shape[0]
    cols = key_weight.shape[1]
    width = 2 * block
    step = block // 2
    rows = tokens // count
    split = len(mine), len(mine) + len(others)

    def kernel(core_ref, *refs):
        wk, wv, fk, fv, low = refs[split[1] :]

        def pair(arrays):
            if len(arrays) == 1:
                return arrays[0][:, :cols], arrays[0][:, cols:]
            return arrays[0][...], arrays[1][...]

        (kg, vg), (kh, vh) = pair(refs[: split[0]]), pair(refs[split[0] : split[1]])
        total = dot(kg, wk[...], NT)
        total += dot(vg, wv[...], NT)
        total += dot(kh, fk[0], NT)
        total += dot(vh, fv[0], NT)
        low[...] = total.reshape(count, rows, step).astype(BF16)

    def place(i, c):
        return ((i // 2 * 2 + c[0]) * 2 + i % 2, 0)

    return pl.pallas_call(
        kernel,
        grid_spec=pltpu.PrefetchScalarGridSpec(
            num_scalar_prefetch=1,
            grid=(width // step,),
            in_specs=[pl.BlockSpec(a.shape, lambda i, c: (0, 0)) for a in (*mine, *others)]
            + [pl.BlockSpec((step, cols), place)] * 2
            + [
                pl.BlockSpec((1, step, cols), lambda i, c: (0, i, 0)),
                pl.BlockSpec((1, step, cols), lambda i, c: (1, i, 0)),
            ],
            out_specs=pl.BlockSpec((count, rows, step), lambda i, c: (0, 0, i)),
        ),
        out_shape=like((count, rows, width), BF16),
        cost_estimate=cost(BACK_COST),
        compiler_params=pltpu.CompilerParams(vmem_limit_bytes=VMEM_BACK),
    )(core, *mine, *others, key_weight, value_weight, weights_far, weights_far)


def body(section_states, key_weight, value_weight, queries, cotangent):
    sections = lax.axis_size("pipe")
    replicas = lax.axis_size("dp")
    lanes = lax.axis_size("tensor")
    first = sections // 2
    count = sections - first
    root = first - 1
    section = lax.axis_index("pipe")
    replica = lax.axis_index("dp")
    lane = lax.axis_index("tensor")
    core = lane % 2
    chip = lane // 2
    chips = lanes // 2
    decoder = section >= first
    half = lanes // 2

    def place(s, d, t):
        return (s * replicas + d) * lanes + t

    everyone = [(k, d, t) for k in range(count) for d in range(replicas) for t in range(lanes)]

    def send(array, move):
        pairs = []
        for k, d, t in everyone:
            a, b, c = move(k, d, t)
            pairs.append((place(first + k, d, t), place(first + a, b, c)))
        return lax.ppermute(array, AXES, pairs)

    def swap_core(array):
        return send(array, lambda k, d, t: (k, d, t ^ 1))

    def swap_replica(array):
        return send(array, lambda k, d, t: (k, 1 - d, t))

    def beside(k, d, t):
        return place((k + count // 2) % count, d, t)

    def lend(array):
        pairs = [(place(first + k, d, t), beside(k, d, t)) for k, d, t in everyone]
        return lax.ppermute(array, AXES, pairs)

    def swap_replica_lent(array):
        pairs = [(beside(k, d, t), place(first + k, 1 - d, t)) for k, d, t in everyone]
        return lax.ppermute(array, AXES, pairs)

    groups = [list(range(first)), list(range(first, sections))]

    def exchange(array):
        return lax.all_to_all(array, "pipe", 0, 0, axis_index_groups=groups)

    def cross(k, d, t, n):
        owner = 2 * d + (t % half) // 2
        return (k, t // half, 2 * (owner ^ n) + t % 2)

    def cross_back(k, d, t, n):
        owner = (t // 2) ^ n
        return (k, owner // 2, half * d + 2 * (owner % 2) + t % 2)

    piece = section_states[0, 0]
    key_weight, value_weight = key_weight[0], value_weight[0]
    tokens, block = piece.shape
    rows = tokens // count
    local = key_weight.shape[1]
    core_index = core.astype(jnp.int32).reshape(1)

    got = None
    for k in range(count):
        pairs = [
            (place(root, d, t), place(first + k, d, t))
            for d in range(replicas)
            for t in range(lanes)
        ]
        part = lax.ppermute(piece[k * rows : (k + 1) * rows], AXES, pairs)
        got = part if got is None else got + part
    held = jnp.stack(
        [send(got, functools.partial(cross, n=n)) for n in range(chips)]
    )

    def pick(owner):
        return lax.dynamic_index_in_dim(held, chip ^ owner, 0, keepdims=False)

    chunk = jnp.stack(
        [
            jnp.concatenate([pick(2 * b), pick(2 * b + 1)], axis=1)
            for b in (replica, 1 - replica)
        ]
    )
    near = exchange(jnp.broadcast_to(chunk[None], (count,) + chunk.shape))
    far = swap_core(near)
    key_part, value_part = product_near(core_index, near, key_weight, value_weight, block)
    weights = [key_weight, value_weight]
    far_product = functools.partial(product_far, core_index, far, weights)
    key_out, value_out = far_product([key_part, value_part], block, 1, [F32, BF16])
    key_in = swap_replica(key_out)
    lent = lend(value_out)
    value_in = swap_replica_lent(lent)
    key_part, value_part, lent = lax.optimization_barrier((key_part, value_part, lent))
    key_own, value_own = far_product([key_part, value_part], block, 0, [F32, F32])

    query, grad = queries[0, 0], cotangent[0, 0]
    keys, values, low, dscores, grads = attend(
        key_own, key_in, value_own, value_in, query, grad
    )
    grads_in = swap_replica(grads)
    keep = decoder.astype(jnp.int32).reshape(1)
    context, query_grad = attend_out(keep, low, values, dscores, keys)

    weights_far = swap_core(other_rows(core_index, key_weight, value_weight, block, grads))

    def reduce(term):
        return jnp.sum(exchange(term).astype(F32), axis=0)

    own_total = reduce(
        back_product_near(
            core_index, [grads], [swap_core(grads)], *weights, weights_far, block, count
        )
    )
    other_term = back_product(
        core_index, [grads_in], [swap_core(grads_in)], *weights, weights_far, block, count
    )
    other_term, own_total = lax.optimization_barrier((other_term, own_total))
    other_total = reduce(other_term)
    total = jnp.stack([own_total, other_total])
    total = total.reshape(replicas, rows, 2, block)

    def owned(owner):
        one = lax.dynamic_index_in_dim(total, (owner // 2) ^ replica, 0, keepdims=False)
        return lax.dynamic_index_in_dim(one, owner % 2, 1, keepdims=False)

    summed = None
    for n in reversed(range(chips)):
        part = send(owned(chip ^ n).astype(BF16), functools.partial(cross_back, n=n))
        part = part.astype(F32)
        summed = part if summed is None else summed + part
    summed = summed.astype(BF16)
    out = []
    for k in range(count):
        pairs = [
            (place(first + k, d, t), place(root, d, t))
            for d in range(replicas)
            for t in range(lanes)
        ]
        out.append(lax.ppermute(summed, AXES, pairs))
    out = lax.optimization_barrier(out)
    encoder_grad = jnp.concatenate(out, axis=0)
    encoder_grad = jnp.where(section == root, encoder_grad, jnp.zeros_like(encoder_grad))
    return context[None, None], query_grad[None, None], encoder_grad[None, None]


def solution(mesh):
    wide = P("pipe", "dp", None, "tensor")
    tall = P("pipe", "dp", "tensor")
    return jax.shard_map(
        body,
        mesh=mesh,
        in_specs=(wide, tall, tall, wide, wide),
        out_specs=(wide, wide, wide),
        check_vma=False,
    )
```

time: 271 us -> 224 us (0.83)
  waiting for transfers between devices: 149 us -> 110 us
  matrix products: 31.4 us -> 0 us
  blocking collectives: 0 us -> 29.2 us
  Pallas kernels: 0 us -> 21.9 us
  local copies, waits for them, and re-layouts: 22.6 us -> 8.8 us
  starting transfers between devices: 56 us -> 49.4 us
  other arithmetic: 8.52 us -> 2.5 us
    ppermute x8, waiting for transfers between devices: 136 us -> 57.7 us  [body(): out.append(lax.ppermute(summed, AXES, pairs))]
    ppermute x0 -> x2, waiting for transfers between devices: none -> 31.1 us  [the longest x1 26 us: lend(): return lax.ppermute(array, AXES, pairs)]
    all_to_all x0 -> x1, blocking collectives: none -> 29.2 us  [exchange(): return lax.all_to_all(array, 'pipe', 0, 0, axis_index_groups=groups)]
    dot_general x10 -> x0, matrix products: 28.9 us -> none  [the longest x2 7.78 us: project(): return out + jnp.dot(far, other, preferred_element_type=F32)]
    pallas_call x0 -> x8, Pallas kernels: none -> 21.9 us  [the longest x1 6.35 us: back_product(): pl.pallas_call(kernel, grid_spec=pltpu.PrefetchScalarGridSpec(num_scalar_...]
    ppermute x29 -> x14, starting transfers between devices: 29.6 us -> 9.93 us  [send(): return lax.ppermute(array, AXES, pairs)]
    all_to_all x0 -> x2, waiting for transfers between devices: none -> 18.9 us  [exchange(): return lax.all_to_all(array, 'pipe', 0, 0, axis_index_groups=groups)]
    all_to_all x0 -> x2, starting transfers between devices: none -> 12.3 us  [exchange(): return lax.all_to_all(array, 'pipe', 0, 0, axis_index_groups=groups)]
  transfers between devices with their start and end apart: 45 -> 34, of which waited for: 13 -> 9; matrix products, arithmetic and copies ran while one was open for 14% -> 0% of each run, Pallas kernels for 0% -> 8%
where the time goes in v2:
time: 224 us; the launch traced here: 223 us
  waiting for transfers between devices  110 us (49%)
  starting transfers between devices  49.4 us (22%)
  blocking collectives  29.2 us (13%)
  Pallas kernels  21.9 us (10%)
  local copies, waits for them, and re-layouts  8.8 us (4%)
  other arithmetic  2.5 us (1%)
    ppermute x8, waiting for transfers between devices, body(): out.append(lax.ppermute(summed, AXES, pairs))  57.7 us
    all_to_all x1, blocking collectives, exchange(): return lax.all_to_all(array, 'pipe', 0, 0, axis_index_groups=groups)  29.2 us
    ppermute x1, waiting for transfers between devices, lend(): return lax.ppermute(array, AXES, pairs)  26 us
    all_to_all x2, waiting for transfers between devices, exchange(): return lax.all_to_all(array, 'pipe', 0, 0, axis_index_groups=groups)  18.9 us
    ppermute x8, starting transfers between devices, body(): part = lax.ppermute(piece[k * rows:(k + 1) * rows], AXES, pairs)  13.1 us
    all_to_all x2, starting transfers between devices, exchange(): return lax.all_to_all(array, 'pipe', 0, 0, axis_index_groups=groups)  12.3 us
    ppermute x8, starting transfers between devices, body(): out.append(lax.ppermute(summed, AXES, pairs))  10.3 us
    ppermute x14, starting transfers between devices, send(): return lax.ppermute(array, AXES, pairs)  9.93 us
  transfers between devices with their start and end apart: 34, of which 9 were waited for; matrix products, arithmetic and copies ran while one was open for 0% of the time, Pallas kernels for 8%

profile of v2, /device:TPU:122, one launch (start us, length us, event | category | flops | bytes accessed | tf_op | source)
XLA Modules:
  0.0 223.0 jit_solution(15736258531626351604)
XLA Ops:
  1.7 4.0 %collective-permute-start.7 = (bf16[32,1024]{1,0:T(8,128)(2,1)S(1)}, bf16[32,1024]{1,0:T(8,128)(2,1)S(1)}, u32[]{:S(2)}, u32[]{:S(2)}) collective-permute-start(bf16[32,1024]{1,0:T(8,128)(2,1)S(1)} %get-tuple-element.59), channel_id=1, source_target_pairs={{112,240},{113,241},{114,242},{115,243},{116,244},{117,245},{118,2... | collective-permute-start | bytes 196616 | tf_op jit(solution)/shard_map/ppermute | solution.py:362
  5.8 1.3 collective-permute-start.6
  7.1 1.3 collective-permute-start.5
  8.4 1.3 collective-permute-start.4
  9.7 1.3 collective-permute-start.3
  20.2 29.2 %all_to_all.15.x_ref = bf16[8,2,32,2048]{3,2,1,0:T(8,128)(2,1)} all-to-all(bf16[8,2,32,2048]{3,2,1,0:T(8,128)(2,1)S(1)} %broadcast_in_dim.16), channel_id=1, replica_groups={{0,16,32,48,64,80,96,112},{128,144,160,176,192,208,224,240},{1,17,33,49..., dimensions={0} | all-to-all | bytes 4194304 | tf_op jit(solution)/shard_map/all_to_all | solution.py:338
  50.2 2.2 copy-done
  52.4 2.2 copy-done.2
  54.6 5.3 %shard_map.76 = (f32[8,2,32,512]{3,2,1,0:T(8,128)S(1)}, f32[8,2,32,512]{3,2,1,0:T(8,128)S(1)}) custom-call(s32[1]{0:T(128)} %bitcast.1.core_ref, bf16[8,2,32,2048]{3,2,1,0:T(8,128)(2,1)} %all_to_all.15.x_ref, bf16[4096,512]{1,0:T(8,128)(2,1)S(1)} %bitcast.69, bf16[4096,512]{1,0:T(8,128)(2,1)S(1)} %bitcast.75), custom_call_target="tpu_custom_call" | custom-call | flops 1 | bytes 1 | tf_op jit(solution)/shard_map/pallas_call | solution.py:73
  63.4 26.0 %collective-permute-done.13 = bf16[256,512]{1,0:T(8,128)(2,1)S(1)} collective-permute-done((bf16[256,512]{1,0:T(8,128)(2,1)S(1)}, bf16[256,512]{1,0:T(8,128)(2,1)S(1)}, u32[]{:S(2)}, u32[]{:S(2)}) %collective-permute-start.13) | collective-permute-done | bytes 262176 | tf_op jit(solution)/shard_map/ppermute | solution.py:329
  89.4 2.5 %collective-permute-start.15 = (bf16[256,512]{1,0:T(8,128)(2,1)S(1)}, bf16[256,512]{1,0:T(8,128)(2,1)S(1)}, u32[]{:S(2)}, u32[]{:S(2)}) collective-permute-start(bf16[256,512]{1,0:T(8,128)(2,1)S(1)} %collective-permute-done.13), channel_id=1, source_target_pairs={{64,136},{65,137},{66,138},{67,139},{68,140},{69,141},{70,142},{71... | collective-permute-start | bytes 786440 | tf_op jit(solution)/shard_map/ppermute | solution.py:333
  91.8 1.3 shard_map.78
  93.2 5.1 %collective-permute-done.15.vb = bf16[256,512]{1,0:T(8,128)(2,1)S(1)} collective-permute-done((bf16[256,512]{1,0:T(8,128)(2,1)S(1)}, bf16[256,512]{1,0:T(8,128)(2,1)S(1)}, u32[]{:S(2)}, u32[]{:S(2)}) %collective-permute-start.15) | collective-permute-done | bytes 262176 | tf_op jit(solution)/shard_map/ppermute | solution.py:333
  98.3 2.4 %shard_map.79 = (bf16[256,512]{1,0:T(8,128)(2,1)S(1)}, bf16[256,512]{1,0:T(8,128)(2,1)S(1)}, bf16[4,256,256]{2,1,0:T(8,128)(2,1)S(1)}, bf16[4,256,256]{2,1,0:T(8,128)(2,1)S(1)}, bf16[256,1024]{1,0:T(8,128)(2,1)S(1)}) custom-call(f32[256,512]{1,0:T(8,128)S(1)} %get-tuple-element.33.ka, f32[256,512]{1,0:T(8,128)S(1)} %collective-permute-done.14.kb, ...), custom_call_target="tpu_custom_call" | custom-call | flops 1 | bytes 1 | tf_op jit(solution)/shard_map/pallas_call | solution.py:172
  103.7 3.4 %shard_map.83 = bf16[8,32,2048]{2,1,0:T(8,128)(2,1)} custom-call(s32[1]{0:T(128)} %bitcast.1.core_ref, bf16[256,1024]{1,0:T(8,128)(2,1)S(1)} %get-tuple-element.42.after_ref.refs_0_, bf16[256,1024]{1,0:T(8,128)(2,1)S(1)} %collective-permute-done.19.refs_1_, bf16[4096,512]{1,0:T(8,128)(2,1)S(1)} %bitcast.73, bf16[4096,512]{1,0:T(8,128)(2,1)S(1)} %bitcast.79, ...), custom_call_target="tpu_custom_call" | custom-call | flops 1 | bytes 1 | tf_op jit(solution)/shard_map/pallas_call | solution.py:235
  107.1 2.0 copy-done.4
  109.1 6.9 %all-to-all-start.1 = ((bf16[8,32,2048]{2,1,0:T(8,128)(2,1)}), bf16[8,32,2048]{2,1,0:T(8,128)(2,1)}, u32[]{:S(2)}, u32[]{:S(2)}) async-start(bf16[8,32,2048]{2,1,0:T(8,128)(2,1)} %shard_map.83), calls=%async_computation.1 | async-start | bytes 2097152 | tf_op jit(solution)/shard_map/all_to_all | solution.py:338
  116.7 6.4 %shard_map.82 = bf16[8,32,2048]{2,1,0:T(8,128)(2,1)} custom-call(s32[1]{0:T(128)} %bitcast.1.core_ref, bf16[256,1024]{1,0:T(8,128)(2,1)S(1)} %collective-permute-done.16.refs_0_, bf16[256,1024]{1,0:T(8,128)(2,1)S(1)} %collective-permute-done.17.refs_1_, bf16[4096,512]{1,0:T(8,128)(2,1)} %bitcast.68, bf16[4096,512]{1,0:T(8,128)(2,1)} %bitcast.74, ...), custom_call_target="tpu_custom_call" | custom-call | flops 1 | bytes 8388608 | tf_op jit(solution)/shard_map/pallas_call | solution.py:271
  123.0 5.9 %all-to-all-done.1 = bf16[8,32,2048]{2,1,0:T(8,128)(2,1)} async-done(((bf16[8,32,2048]{2,1,0:T(8,128)(2,1)}), bf16[8,32,2048]{2,1,0:T(8,128)(2,1)}, u32[]{:S(2)}, u32[]{:S(2)}) %all-to-all-start.1) | async-done | bytes 1048608 | tf_op jit(solution)/shard_map/all_to_all | solution.py:338
  128.9 1.4 convert_reduce_fusion.1
  130.3 5.4 %all-to-all-start.2 = ((bf16[8,32,2048]{2,1,0:T(8,128)(2,1)}), bf16[8,32,2048]{2,1,0:T(8,128)(2,1)S(1)}, u32[]{:S(2)}, u32[]{:S(2)}) async-start(bf16[8,32,2048]{2,1,0:T(8,128)(2,1)} %shard_map.82), calls=%async_computation.2 | async-start | bytes 2097152 | tf_op jit(solution)/shard_map/all_to_all | solution.py:338
  135.9 13.0 %all-to-all-done.2 = bf16[8,32,2048]{2,1,0:T(8,128)(2,1)S(1)} async-done(((bf16[8,32,2048]{2,1,0:T(8,128)(2,1)}), bf16[8,32,2048]{2,1,0:T(8,128)(2,1)S(1)}, u32[]{:S(2)}, u32[]{:S(2)}) %all-to-all-start.2) | async-done | bytes 1048608 | tf_op jit(solution)/shard_map/all_to_all | solution.py:338
  159.2 52.5 %collective-permute-done.24 = bf16[32,1024]{1,0:T(8,128)(2,1)S(1)} collective-permute-done((bf16[32,1024]{1,0:T(8,128)(2,1)S(1)}, bf16[32,1024]{1,0:T(8,128)(2,1)S(1)}, u32[]{:S(2)}, u32[]{:S(2)}) %collective-permute-start.24) | collective-permute-done | bytes 65568 | tf_op jit(solution)/shard_map/ppermute | solution.py:432
  216.9 4.9 %collective-permute-done.29 = bf16[32,1024]{1,0:T(8,128)(2,1)S(1)} collective-permute-done((bf16[32,1024]{1,0:T(8,128)(2,1)S(1)}, bf16[32,1024]{1,0:T(8,128)(2,1)S(1)}, u32[]{:S(2)}, u32[]{:S(2)}) %collective-permute-start.29) | collective-permute-done | bytes 65568 | tf_op jit(solution)/shard_map/ppermute | solution.py:432
  (95 shorter events, 34.5 us)
Async XLA Ops:
  1.7 9.2 %collective-permute-start.7 = (bf16[32,1024]{1,0:T(8,128)(2,1)S(1)}, bf16[32,1024]{1,0:T(8,128)(2,1)S(1)}, u32[]{:S(2)}, u32[]{:S(2)}) collective-permute-start(bf16[32,1024]{1,0:T(8,128)(2,1)S(1)} %get-tuple-element.59), channel_id=1, source_target_pairs={{112,240},{113,241},{114,242},{115,243},{116,244},{117,245},{118,2... | collective-permute-start | bytes 196616 | tf_op jit(solution)/shard_map/ppermute | solution.py:362
  5.8 6.5 %collective-permute-start.6 = (bf16[32,1024]{1,0:T(8,128)(2,1)S(1)}, bf16[32,1024]{1,0:T(8,128)(2,1)S(1)}, u32[]{:S(2)}, u32[]{:S(2)}) collective-permute-start(bf16[32,1024]{1,0:T(8,128)(2,1)S(1)} %get-tuple-element.60), channel_id=1, source_target_pairs={{112,224},{113,225},{114,226},{115,227},{116,228},{117,229},{118,2... | collective-permute-start | bytes 196616 | tf_op jit(solution)/shard_map/ppermute | solution.py:362
  7.1 6.5 %collective-permute-start.5 = (bf16[32,1024]{1,0:T(8,128)(2,1)S(1)}, bf16[32,1024]{1,0:T(8,128)(2,1)S(1)}, u32[]{:S(2)}, u32[]{:S(2)}) collective-permute-start(bf16[32,1024]{1,0:T(8,128)(2,1)S(1)} %get-tuple-element.54), channel_id=1, source_target_pairs={{112,208},{113,209},{114,210},{115,211},{116,212},{117,213},{118,2... | collective-permute-start | bytes 196616 | tf_op jit(solution)/shard_map/ppermute | solution.py:362
  8.4 6.5 %collective-permute-start.4 = (bf16[32,1024]{1,0:T(8,128)(2,1)S(1)}, bf16[32,1024]{1,0:T(8,128)(2,1)S(1)}, u32[]{:S(2)}, u32[]{:S(2)}) collective-permute-start(bf16[32,1024]{1,0:T(8,128)(2,1)S(1)} %get-tuple-element.55), channel_id=1, source_target_pairs={{112,192},{113,193},{114,194},{115,195},{116,196},{117,197},{118,1... | collective-permute-start | bytes 196616 | tf_op jit(solution)/shard_map/ppermute | solution.py:362
  9.7 5.2 %collective-permute-start.3 = (bf16[32,1024]{1,0:T(8,128)(2,1)S(1)}, bf16[32,1024]{1,0:T(8,128)(2,1)S(1)}, u32[]{:S(2)}, u32[]{:S(2)}) collective-permute-start(bf16[32,1024]{1,0:T(8,128)(2,1)S(1)} %get-tuple-element.56), channel_id=1, source_target_pairs={{112,176},{113,177},{114,178},{115,179},{116,180},{117,181},{118,1... | collective-permute-start | bytes 196616 | tf_op jit(solution)/shard_map/ppermute | solution.py:362
  11.0 3.9 %collective-permute-start.2 = (bf16[32,1024]{1,0:T(8,128)(2,1)S(1)}, bf16[32,1024]{1,0:T(8,128)(2,1)S(1)}, u32[]{:S(2)}, u32[]{:S(2)}) collective-permute-start(bf16[32,1024]{1,0:T(8,128)(2,1)S(1)} %get-tuple-element.57), channel_id=1, source_target_pairs={{112,160},{113,161},{114,162},{115,163},{116,164},{117,165},{118,1... | collective-permute-start | bytes 196616 | tf_op jit(solution)/shard_map/ppermute | solution.py:362
  12.3 3.9 %collective-permute-start = (bf16[32,1024]{1,0:T(8,128)(2,1)S(1)}, bf16[32,1024]{1,0:T(8,128)(2,1)S(1)}, u32[]{:S(2)}, u32[]{:S(2)}) collective-permute-start(bf16[32,1024]{1,0:T(8,128)(2,1)S(1)} %get-tuple-element.58), channel_id=1, source_target_pairs={{112,128},{113,129},{114,130},{115,131},{116,132},{117,133},{118,1... | collective-permute-start | bytes 196616 | tf_op jit(solution)/shard_map/ppermute | solution.py:362
  13.6 3.3 %collective-permute-start.1 = (bf16[32,1024]{1,0:T(8,128)(2,1)S(1)}, bf16[32,1024]{1,0:T(8,128)(2,1)S(1)}, u32[]{:S(2)}, u32[]{:S(2)}) collective-permute-start(bf16[32,1024]{1,0:T(8,128)(2,1)S(1)} %get-tuple-element.53), channel_id=1, source_target_pairs={{112,144},{113,145},{114,146},{115,147},{116,148},{117,149},{118,1... | collective-permute-start | bytes 196616 | tf_op jit(solution)/shard_map/ppermute | solution.py:362
  49.4 10.5 %collective-permute-start.12 = (bf16[8,2,32,2048]{3,2,1,0:T(8,128)(2,1)}, bf16[8,2,32,2048]{3,2,1,0:T(8,128)(2,1)S(1)}, u32[]{:S(2)}, u32[]{:S(2)}) collective-permute-start(bf16[8,2,32,2048]{3,2,1,0:T(8,128)(2,1)} %all_to_all.15.x_ref), channel_id=1, source_target_pairs={{128,129},{129,128},{130,131},{131,130},{132,133},{133,132},{134,1... | collective-permute-start | bytes 6291464 | tf_op jit(solution)/shard_map/ppermute | solution.py:316
  61.2 28.2 %collective-permute-start.13 = (bf16[256,512]{1,0:T(8,128)(2,1)S(1)}, bf16[256,512]{1,0:T(8,128)(2,1)S(1)}, u32[]{:S(2)}, u32[]{:S(2)}) collective-permute-start(bf16[256,512]{1,0:T(8,128)(2,1)S(1)} %get-tuple-element.30), channel_id=1, source_target_pairs={{128,64},{129,65},{130,66},{131,67},{132,68},{133,69},{134,70},{13... | collective-permute-start | bytes 786440 | tf_op jit(solution)/shard_map/ppermute | solution.py:329
  62.5 30.6 %collective-permute-start.14 = (f32[256,512]{1,0:T(8,128)S(1)}, f32[256,512]{1,0:T(8,128)S(1)}, u32[]{:S(2)}, u32[]{:S(2)}) collective-permute-start(f32[256,512]{1,0:T(8,128)S(1)} %get-tuple-element.34), channel_id=1, source_target_pairs={{128,136},{129,137},{130,138},{131,139},{132,140},{133,141},{134,1... | collective-permute-start | bytes 1572872 | tf_op jit(solution)/shard_map/ppermute | solution.py:316
  89.4 8.9 %collective-permute-start.15 = (bf16[256,512]{1,0:T(8,128)(2,1)S(1)}, bf16[256,512]{1,0:T(8,128)(2,1)S(1)}, u32[]{:S(2)}, u32[]{:S(2)}) collective-permute-start(bf16[256,512]{1,0:T(8,128)(2,1)S(1)} %collective-permute-done.13), channel_id=1, source_target_pairs={{64,136},{65,137},{66,138},{67,139},{68,140},{69,141},{70,142},{71... | collective-permute-start | bytes 786440 | tf_op jit(solution)/shard_map/ppermute | solution.py:333
  103.0 13.0 %collective-permute-start.16 = (bf16[256,1024]{1,0:T(8,128)(2,1)S(1)}, bf16[256,1024]{1,0:T(8,128)(2,1)S(1)}, u32[]{:S(2)}, u32[]{:S(2)}) collective-permute-start(bf16[256,1024]{1,0:T(8,128)(2,1)S(1)} %get-tuple-element.42.after_ref.refs_0_), channel_id=1, source_target_pairs={{128,136},{129,137},{130,138},{131,139},{132,140},{133,141},{134,1... | collective-permute-start | bytes 1572872 | tf_op jit(solution)/shard_map/ppermute | solution.py:316
  109.1 19.9 %all-to-all-start.1 = ((bf16[8,32,2048]{2,1,0:T(8,128)(2,1)}), bf16[8,32,2048]{2,1,0:T(8,128)(2,1)}, u32[]{:S(2)}, u32[]{:S(2)}) async-start(bf16[8,32,2048]{2,1,0:T(8,128)(2,1)} %shard_map.83), calls=%async_computation.1 | async-start | bytes 2097152 | tf_op jit(solution)/shard_map/all_to_all | solution.py:338
  130.3 18.6 %all-to-all-start.2 = ((bf16[8,32,2048]{2,1,0:T(8,128)(2,1)}), bf16[8,32,2048]{2,1,0:T(8,128)(2,1)S(1)}, u32[]{:S(2)}, u32[]{:S(2)}) async-start(bf16[8,32,2048]{2,1,0:T(8,128)(2,1)} %shard_map.82), calls=%async_computation.2 | async-start | bytes 2097152 | tf_op jit(solution)/shard_map/all_to_all | solution.py:338
  149.9 2.8 %collective-permute-start.23 = (bf16[32,1024]{1,0:T(8,128)(2,1)S(1)}, bf16[32,1024]{1,0:T(8,128)(2,1)S(1)}, u32[]{:S(2)}, u32[]{:S(2)}) collective-permute-start(bf16[32,1024]{1,0:T(8,128)(2,1)S(1)} %bitcast.82), channel_id=1, source_target_pairs={{128,128},{129,129},{130,130},{131,131},{132,136},{133,137},{134,1... | collective-permute-start | bytes 196616 | tf_op jit(solution)/shard_map/ppermute | solution.py:316
  152.7 59.0 %collective-permute-start.24 = (bf16[32,1024]{1,0:T(8,128)(2,1)S(1)}, bf16[32,1024]{1,0:T(8,128)(2,1)S(1)}, u32[]{:S(2)}, u32[]{:S(2)}) collective-permute-start(bf16[32,1024]{1,0:T(8,128)(2,1)S(1)} %add_convert_fusion), channel_id=1, source_target_pairs={{128,112},{129,113},{130,114},{131,115},{132,116},{133,117},{134,1... | collective-permute-start | bytes 196616 | tf_op jit(solution)/shard_map/ppermute | solution.py:432
  154.0 59.0 %collective-permute-start.25 = (bf16[32,1024]{1,0:T(8,128)(2,1)S(1)}, bf16[32,1024]{1,0:T(8,128)(2,1)S(1)}, u32[]{:S(2)}, u32[]{:S(2)}) collective-permute-start(bf16[32,1024]{1,0:T(8,128)(2,1)S(1)} %add_convert_fusion), channel_id=1, source_target_pairs={{144,112},{145,113},{146,114},{147,115},{148,116},{149,117},{150,1... | collective-permute-start | bytes 196616 | tf_op jit(solution)/shard_map/ppermute | solution.py:432
  155.3 59.0 %collective-permute-start.26 = (bf16[32,1024]{1,0:T(8,128)(2,1)S(1)}, bf16[32,1024]{1,0:T(8,128)(2,1)S(1)}, u32[]{:S(2)}, u32[]{:S(2)}) collective-permute-start(bf16[32,1024]{1,0:T(8,128)(2,1)S(1)} %add_convert_fusion), channel_id=1, source_target_pairs={{160,112},{161,113},{162,114},{163,115},{164,116},{165,117},{166,1... | collective-permute-start | bytes 196616 | tf_op jit(solution)/shard_map/ppermute | solution.py:432
  156.6 60.2 %collective-permute-start.27 = (bf16[32,1024]{1,0:T(8,128)(2,1)S(1)}, bf16[32,1024]{1,0:T(8,128)(2,1)S(1)}, u32[]{:S(2)}, u32[]{:S(2)}) collective-permute-start(bf16[32,1024]{1,0:T(8,128)(2,1)S(1)} %add_convert_fusion), channel_id=1, source_target_pairs={{176,112},{177,113},{178,114},{179,115},{180,116},{181,117},{182,1... | collective-permute-start | bytes 196616 | tf_op jit(solution)/shard_map/ppermute | solution.py:432
  157.9 59.0 %collective-permute-start.28 = (bf16[32,1024]{1,0:T(8,128)(2,1)S(1)}, bf16[32,1024]{1,0:T(8,128)(2,1)S(1)}, u32[]{:S(2)}, u32[]{:S(2)}) collective-permute-start(bf16[32,1024]{1,0:T(8,128)(2,1)S(1)} %add_convert_fusion), channel_id=1, source_target_pairs={{192,112},{193,113},{194,114},{195,115},{196,116},{197,117},{198,1... | collective-permute-start | bytes 196616 | tf_op jit(solution)/shard_map/ppermute | solution.py:432
  211.8 10.1 %collective-permute-start.29 = (bf16[32,1024]{1,0:T(8,128)(2,1)S(1)}, bf16[32,1024]{1,0:T(8,128)(2,1)S(1)}, u32[]{:S(2)}, u32[]{:S(2)}) collective-permute-start(bf16[32,1024]{1,0:T(8,128)(2,1)S(1)} %add_convert_fusion), channel_id=1, source_target_pairs={{208,112},{209,113},{210,114},{211,115},{212,116},{213,117},{214,1... | collective-permute-start | bytes 196616 | tf_op jit(solution)/shard_map/ppermute | solution.py:432
  213.1 8.8 %collective-permute-start.30 = (bf16[32,1024]{1,0:T(8,128)(2,1)S(1)}, bf16[32,1024]{1,0:T(8,128)(2,1)S(1)}, u32[]{:S(2)}, u32[]{:S(2)}) collective-permute-start(bf16[32,1024]{1,0:T(8,128)(2,1)S(1)} %add_convert_fusion), channel_id=1, source_target_pairs={{224,112},{225,113},{226,114},{227,115},{228,116},{229,117},{230,1... | collective-permute-start | bytes 196616 | tf_op jit(solution)/shard_map/ppermute | solution.py:432
  214.4 7.7 %collective-permute-start.31 = (bf16[32,1024]{1,0:T(8,128)(2,1)S(1)}, bf16[32,1024]{1,0:T(8,128)(2,1)S(1)}, u32[]{:S(2)}, u32[]{:S(2)}) collective-permute-start(bf16[32,1024]{1,0:T(8,128)(2,1)S(1)} %add_convert_fusion), channel_id=1, source_target_pairs={{240,112},{241,113},{242,114},{243,115},{244,116},{245,117},{246,1... | collective-permute-start | bytes 196616 | tf_op jit(solution)/shard_map/ppermute | solution.py:432
  (17 other events, 104.1 us)

commit v3 on v2

v3 whole, which is shorter than its diff:
```python
import functools

import jax
import jax.numpy as jnp
from jax import lax
from jax.experimental import pallas as pl
from jax.experimental.pallas import tpu as pltpu
from jax.sharding import PartitionSpec as P

HD = 128
AXES = ("pipe", "dp", "tensor")
F32 = jnp.float32
BF16 = jnp.bfloat16
SCALE = HD ** (-0.5)
VMEM = 20 * 1024 * 1024
VMEM_BACK = 48 * 1024 * 1024
NT = (((1,), (1,)), ((), ()))
TN = (((0,), (0,)), ((), ()))


def params():
    return pltpu.CompilerParams(vmem_limit_bytes=VMEM)


def like(shape, dtype):
    return jax.ShapeDtypeStruct(shape, dtype)


def dot(a, b, dims=(((1,), (0,)), ((), ()))):
    return lax.dot_general(a, b, dims, preferred_element_type=F32)


def cost():
    return pl.CostEstimate(flops=1, bytes_accessed=1, transcendentals=0)


def whole(count):
    return [pl.BlockSpec(memory_space=pltpu.VMEM)] * count


def scalar():
    return [pl.BlockSpec(memory_space=pltpu.SMEM)]


def rows_of(weight, index, size):
    return weight[pl.ds(pl.multiple_of(index * size, size), size), :]


def product_near(near, weights, block):
    count, rows, width = near.shape
    tokens = count * rows
    cols = weights[0].shape[1]
    many = len(weights)

    def kernel(x_ref, *refs):
        x = x_ref[...].reshape(tokens, block)
        first = pl.program_id(0) == 0
        for w, out in zip(refs[:many], refs[many:]):

            @pl.when(first)
            def _():
                out[...] = dot(x, w[...])

            @pl.when(jnp.logical_not(first))
            def _():
                out[...] += dot(x, w[...])

    return pl.pallas_call(
        kernel,
        grid=(width // block,),
        in_specs=[pl.BlockSpec((count, rows, block), lambda i: (0, 0, i))]
        + [pl.BlockSpec((block, cols), lambda i: (i, 0))] * many,
        out_specs=[pl.BlockSpec((tokens, cols), lambda i: (0, 0))] * many,
        out_shape=[like((tokens, cols), F32)] * many,
        cost_estimate=cost(),
        compiler_params=params(),
    )(near, *weights)


def product_far(same, far, weights, parts):
    count, rows, width = far.shape
    tokens = count * rows
    cols = weights[0].shape[1]

    def kernel(same_ref, x_ref, wk, wv, pk, pv, key_out, value_out, key_own, value_own):
        same_here = same_ref[0] > 0
        x = x_ref[...].reshape(tokens, width)
        for w, p, out, own in ((wk, pk, key_out, key_own), (wv, pv, value_out, value_own)):
            total = dot(x, w[...])
            part = p[...]
            out[...] = jnp.where(same_here, total, part).astype(out.dtype)
            own[...] = jnp.where(same_here, part, total)

    return pl.pallas_call(
        kernel,
        in_specs=scalar() + whole(5),
        out_specs=whole(4),
        out_shape=[like((tokens, cols), t) for t in (F32, BF16, F32, F32)],
        cost_estimate=cost(),
        compiler_params=params(),
    )(same, far, *weights, *parts)


def other_rows(core, key_weight, value_weight, block, after):
    height, cols = key_weight.shape
    step = block // 2

    def kernel(core_ref, wk, wv, after_ref, out):
        out[0] = wk[...]
        out[1] = wv[...]

    def place(i, c):
        return ((i // 2 * 2 + 1 - c[0]) * 2 + i % 2, 0)

    return pl.pallas_call(
        kernel,
        grid_spec=pltpu.PrefetchScalarGridSpec(
            num_scalar_prefetch=1,
            grid=(4,),
            in_specs=[pl.BlockSpec((step, cols), place)] * 2
            + [pl.BlockSpec(memory_space=pl.ANY)],
            out_specs=pl.BlockSpec((2, step, cols), lambda i, c: (0, i, 0)),
        ),
        out_shape=like((2, height // 2, cols), BF16),
        cost_estimate=cost(),
        compiler_params=params(),
    )(core, key_weight, value_weight, after)


def attend(key_own, key_in, value_own, value_in, query, grad):
    tokens, local = key_own.shape
    dec = query.shape[0]
    heads = local // HD

    def kernel(ka, kb, va, vb, q, g, keys, values, low, dscores, grads):
        for h in range(heads):
            at = slice(h * HD, (h + 1) * HD)
            k = (ka[:, at] + kb[:, at]).astype(BF16)
            v = (va[:, at] + vb[:, at].astype(F32)).astype(BF16)
            keys[:, at] = k
            values[:, at] = v
            scores = dot(q[:, at], k, NT) * SCALE
            top = jnp.max(scores, axis=-1, keepdims=True)
            e = jnp.exp(scores - top)
            p = e / jnp.sum(e, axis=-1, keepdims=True)
            rounded = p.astype(BF16)
            low[h] = rounded
            dprobs = dot(g[:, at], v, NT)
            delta = jnp.sum(p * dprobs, axis=-1, keepdims=True)
            ds = (p * (dprobs - delta) * SCALE).astype(BF16)
            dscores[h] = ds
            grads[:, at] = dot(ds, q[:, at], TN).astype(BF16)
            start = local + h * HD
            grads[:, start : start + HD] = dot(rounded, g[:, at], TN).astype(BF16)

    return pl.pallas_call(
        kernel,
        in_specs=whole(6),
        out_specs=whole(5),
        out_shape=[
            like((tokens, local), BF16),
            like((tokens, local), BF16),
            like((heads, dec, tokens), BF16),
            like((heads, dec, tokens), BF16),
            like((tokens, 2 * local), BF16),
        ],
        cost_estimate=cost(),
        compiler_params=params(),
    )(key_own, key_in, value_own, value_in, query, grad)


def attend_out(keep, low, values, dscores, keys):
    tokens, local = values.shape
    heads, dec = low.shape[:2]

    def kernel(keep_ref, p, v, ds, k, context, query_grad):
        on = keep_ref[0] > 0
        for h in range(heads):
            at = slice(h * HD, (h + 1) * HD)
            context[:, at] = jnp.where(on, dot(p[h], v[:, at]), 0.0).astype(BF16)
            query_grad[:, at] = jnp.where(on, dot(ds[h], k[:, at]), 0.0).astype(BF16)

    return pl.pallas_call(
        kernel,
        in_specs=scalar() + whole(4),
        out_specs=whole(2),
        out_shape=[like((dec, local), BF16)] * 2,
        cost_estimate=cost(),
        compiler_params=params(),
    )(keep, low, values, dscores, keys)


def back_product_near(core, mine, others, key_weight, value_weight, weights_far, block, count):
    tokens = mine.shape[0]
    cols = key_weight.shape[1]
    width = 2 * block
    step = block // 2
    rows = tokens // count

    def kernel(core_ref, g, h, wk, wv, far, out, low, sems):
        c = core_ref[0]
        copies = []
        for i in range(width // step):
            at = (i // 2 * 2 + c) * 2 + i % 2
            total = dot(g[:, :cols], rows_of(wk, at, step), NT)
            total += dot(g[:, cols:], rows_of(wv, at, step), NT)
            total += dot(h[:, :cols], far[0, i * step : (i + 1) * step, :], NT)
            total += dot(h[:, cols:], far[1, i * step : (i + 1) * step, :], NT)
            low[i] = total.reshape(count, rows, step).astype(BF16)
            copy = pltpu.make_async_copy(
                low.at[i], out.at[:, :, pl.ds(i * step, step)], sems.at[i]
            )
            copy.start()
            copies.append(copy)
        for copy in copies:
            copy.wait()

    return pl.pallas_call(
        kernel,
        in_specs=scalar() + whole(5),
        out_specs=pl.BlockSpec(memory_space=pltpu.HBM),
        out_shape=like((count, rows, width), BF16),
        scratch_shapes=[
            pltpu.VMEM((width // step, count, rows, step), BF16),
            pltpu.SemaphoreType.DMA((width // step,)),
        ],
        cost_estimate=cost(),
        compiler_params=params(),
    )(core, mine, others, key_weight, value_weight, weights_far)


def back_product(core, mine, others, key_weight, value_weight, weights_far, block, count):
    tokens = mine.shape[0]
    cols = key_weight.shape[1]
    width = 2 * block
    step = block // 2
    steps = width // step
    rows = tokens // count

    def kernel(core_ref, g, h, wk, wv, far, out, held, low, in_sems, out_sems):
        c = core_ref[0]
        loads = []
        for i in range(steps):
            at = pl.ds(pl.multiple_of(((i // 2 * 2 + c) * 2 + i % 2) * step, step), step)
            sources = [wk.at[at], wv.at[at]]
            sources += [far.at[n, pl.ds(i * step, step)] for n in range(2)]
            loads.append(
                [
                    pltpu.make_async_copy(source, held.at[i, n], in_sems.at[i, n])
                    for n, source in enumerate(sources)
                ]
            )
        for group in loads:
            for load in group:
                load.start()
        stores = []
        for i in range(steps):
            total = None
            for n, a in enumerate((g, g, h, h)):
                loads[i][n].wait()
                term = dot(a[:, n % 2 * cols : (n % 2 + 1) * cols], held[i, n], NT)
                total = term if total is None else total + term
            low[i] = total.reshape(count, rows, step).astype(BF16)
            store = pltpu.make_async_copy(
                low.at[i], out.at[:, :, pl.ds(i * step, step)], out_sems.at[i]
            )
            store.start()
            stores.append(store)
        for store in stores:
            store.wait()

    return pl.pallas_call(
        kernel,
        in_specs=scalar() + whole(2) + [pl.BlockSpec(memory_space=pl.ANY)] * 3,
        out_specs=pl.BlockSpec(memory_space=pl.ANY),
        out_shape=like((count, rows, width), BF16),
        scratch_shapes=[
            pltpu.VMEM((steps, 4, step, cols), BF16),
            pltpu.VMEM((steps, count, rows, step), BF16),
            pltpu.SemaphoreType.DMA((steps, 4)),
            pltpu.SemaphoreType.DMA((steps,)),
        ],
        cost_estimate=cost(),
        compiler_params=pltpu.CompilerParams(vmem_limit_bytes=VMEM_BACK),
    )(core, mine, others, key_weight, value_weight, weights_far)


def body(section_states, key_weight, value_weight, queries, cotangent):
    sections = lax.axis_size("pipe")
    replicas = lax.axis_size("dp")
    lanes = lax.axis_size("tensor")
    first = sections // 2
    count = sections - first
    root = first - 1
    section = lax.axis_index("pipe")
    replica = lax.axis_index("dp")
    lane = lax.axis_index("tensor")
    core = lane % 2
    chip = lane // 2
    chips = lanes // 2
    decoder = section >= first
    half = lanes // 2

    def place(s, d, t):
        return (s * replicas + d) * lanes + t

    everyone = [(k, d, t) for k in range(count) for d in range(replicas) for t in range(lanes)]

    def send(array, move):
        pairs = []
        for k, d, t in everyone:
            a, b, c = move(k, d, t)
            pairs.append((place(first + k, d, t), place(first + a, b, c)))
        return lax.ppermute(array, AXES, pairs)

    def swap_core(array):
        return send(array, lambda k, d, t: (k, d, t ^ 1))

    def swap_replica(array):
        return send(array, lambda k, d, t: (k, 1 - d, t))

    def beside(k, d, t):
        return place((k + count // 2) % count, d, t)

    def lend(array):
        pairs = [(place(first + k, d, t), beside(k, d, t)) for k, d, t in everyone]
        return lax.ppermute(array, AXES, pairs)

    def swap_replica_lent(array):
        pairs = [(beside(k, d, t), place(first + k, 1 - d, t)) for k, d, t in everyone]
        return lax.ppermute(array, AXES, pairs)

    groups = [list(range(first)), list(range(first, sections))]

    def exchange(array):
        return lax.all_to_all(array, "pipe", 0, 0, axis_index_groups=groups)

    def cross(k, d, t, n):
        over = 2 * (t % 2) + (n ^ (t % half) // 2)
        return (k, t // half, 2 * over + d)

    def cross_back(k, d, t, n):
        owner = (t // 2) ^ n
        return (k, owner // 2, half * d + 2 * (owner % 2) + t % 2)

    def in_order(mine, others):
        return jnp.where(core == 0, mine, others), jnp.where(core == 0, others, mine)

    piece = section_states[0, 0]
    key_weight, value_weight = key_weight[0], value_weight[0]
    tokens, block = piece.shape
    rows = tokens // count
    local = key_weight.shape[1]
    core_index = core.astype(jnp.int32).reshape(1)

    got = None
    for k in range(count):
        pairs = [
            (place(root, d, t), place(first + k, d, t))
            for d in range(replicas)
            for t in range(lanes)
        ]
        part = lax.ppermute(piece[k * rows : (k + 1) * rows], AXES, pairs)
        got = part if got is None else got + part
    both = jnp.concatenate(in_order(got, swap_core(got)), axis=1)
    held = [send(both, functools.partial(cross, n=n)) for n in range(2)]
    even = chip % 2 == 0
    chunk = jnp.concatenate(
        [jnp.where(even, held[0], held[1]), jnp.where(even, held[1], held[0])], axis=1
    )
    weights = [key_weight, value_weight]
    near = exchange(jnp.broadcast_to(chunk[None], (count,) + chunk.shape))
    far = swap_core(near)
    parts = product_near(near, weights, block)
    same = (core == replica).astype(jnp.int32).reshape(1)
    key_out, value_out, key_own, value_own = product_far(same, far, weights, parts)
    key_in = swap_replica(key_out)
    value_in = swap_replica_lent(lend(value_out))

    query, grad = queries[0, 0], cotangent[0, 0]
    keys, values, low, dscores, grads = attend(
        key_own, key_in, value_own, value_in, query, grad
    )
    grads_in = swap_replica(grads)
    keep = decoder.astype(jnp.int32).reshape(1)
    context, query_grad = attend_out(keep, low, values, dscores, keys)


    weights_far = swap_core(other_rows(core_index, key_weight, value_weight, block, grads))

    def reduce(term):
        return jnp.sum(exchange(term).astype(F32), axis=0)

    grads_over = swap_core(grads)
    own_total = reduce(
        back_product_near(
            core_index, grads, grads_over, *weights, weights_far, block, count
        )
    )
    other_term = back_product(
        core_index, grads_in, swap_core(grads_in), *weights, weights_far, block, count
    )
    other_term, own_total = lax.optimization_barrier((other_term, own_total))
    other_total = reduce(other_term)
    total = jnp.stack([own_total, other_total]).reshape(replicas, rows, 2, block)

    def owned(owner):
        one = lax.dynamic_index_in_dim(total, (owner // 2) ^ replica, 0, keepdims=False)
        return lax.dynamic_index_in_dim(one, owner % 2, 1, keepdims=False)

    summed = None
    for n in range(chips):
        part = send(owned(chip ^ n).astype(BF16), functools.partial(cross_back, n=n))
        part = part.astype(F32)
        summed = part if summed is None else summed + part
    summed = summed.astype(BF16)
    pairs = [
        (place(first + k, d, t), place(first + k - 1, d, t)) for k, d, t in everyone if k % 2
    ]
    summed = jnp.concatenate([summed, lax.ppermute(summed, AXES, pairs)], axis=0)
    out = []
    for k in range(0, count, 2):
        pairs = [
            (place(first + k, d, t), place(root, d, t))
            for d in range(replicas)
            for t in range(lanes)
        ]
        out.append(lax.ppermute(summed, AXES, pairs))
    encoder_grad = jnp.concatenate(out, axis=0)
    encoder_grad = jnp.where(section == root, encoder_grad, jnp.zeros_like(encoder_grad))
    return context[None, None], query_grad[None, None], encoder_grad[None, None]


def solution(mesh):
    wide = P("pipe", "dp", None, "tensor")
    tall = P("pipe", "dp", "tensor")
    return jax.shard_map(
        body,
        mesh=mesh,
        in_specs=(wide, tall, tall, wide, wide),
        out_specs=(wide, wide, wide),
        check_vma=False,
    )
```

time: 224 us -> 218 us (0.973)
  waiting for transfers between devices: 110 us -> 104 us
    ppermute x8 -> x4, waiting for transfers between devices: 57.7 us -> 45.5 us  [body(): out.append(lax.ppermute(summed, AXES, pairs))]
    ppermute x1, waiting for transfers between devices: 5.11 us -> 11 us  [swap_replica_lent(): return lax.ppermute(array, AXES, pairs)]
    ppermute x8 -> x4, starting transfers between devices: 10.3 us -> 5.17 us  [body(): out.append(lax.ppermute(summed, AXES, pairs))]
    ppermute x1, starting transfers between devices: 2.46 us -> 6.53 us  [swap_replica_lent(): return lax.ppermute(array, AXES, pairs)]
    pallas_call x5 -> x4, Pallas kernels: 17.6 us -> 16.9 us  [the longest x1 5.88 us: back_product(): pl.pallas_call(kernel, in_specs=scalar() + whole(2) + [pl.BlockSpec(memor...]
    ppermute x14 -> x13, starting transfers between devices: 9.93 us -> 10.6 us  [send(): return lax.ppermute(array, AXES, pairs)]
    unnamed x26 -> x19, local copies, waits for them, and re-layouts: 6.59 us -> 6.56 us
  transfers between devices with their start and end apart: 34 -> 30, of which waited for: 9 -> 9; matrix products, arithmetic and copies ran while one was open for 0% -> 0% of each run, Pallas kernels for 8% -> 6%
where the time goes in v3:
time: 218 us; the launch traced here: 217 us
  waiting for transfers between devices  104 us (48%)
  starting transfers between devices  50 us (23%)
  blocking collectives  29.1 us (13%)
  Pallas kernels  21.2 us (10%)
  local copies, waits for them, and re-layouts  8.72 us (4%)
  other arithmetic  2.56 us (1%)
    ppermute x4, waiting for transfers between devices, body(): out.append(lax.ppermute(summed, AXES, pairs))  45.5 us
    all_to_all x1, blocking collectives, exchange(): return lax.all_to_all(array, 'pipe', 0, 0, axis_index_groups=groups)  29.1 us
    ppermute x1, waiting for transfers between devices, lend(): return lax.ppermute(array, AXES, pairs)  26 us
    all_to_all x2, waiting for transfers between devices, exchange(): return lax.all_to_all(array, 'pipe', 0, 0, axis_index_groups=groups)  19.6 us
    ppermute x8, starting transfers between devices, body(): part = lax.ppermute(piece[k * rows:(k + 1) * rows], AXES, pairs)  13.1 us
    all_to_all x2, starting transfers between devices, exchange(): return lax.all_to_all(array, 'pipe', 0, 0, axis_index_groups=groups)  12.7 us
    ppermute x1, waiting for transfers between devices, swap_replica_lent(): return lax.ppermute(array, AXES, pairs)  11 us
    ppermute x13, starting transfers between devices, send(): return lax.ppermute(array, AXES, pairs)  10.6 us
  transfers between devices with their start and end apart: 30, of which 9 were waited for; matrix products, arithmetic and copies ran while one was open for 0% of the time, Pallas kernels for 6%

profile of v3, /device:TPU:122, one launch (start us, length us, event | category | flops | bytes accessed | tf_op | source)
XLA Modules:
  0.0 217.0 jit_solution(16718362256309338552)
XLA Ops:
  1.7 4.0 %collective-permute-start.7 = (bf16[32,1024]{1,0:T(8,128)(2,1)S(1)}, bf16[32,1024]{1,0:T(8,128)(2,1)S(1)}, u32[]{:S(2)}, u32[]{:S(2)}) collective-permute-start(bf16[32,1024]{1,0:T(8,128)(2,1)S(1)} %get-tuple-element.39), channel_id=1, source_target_pairs={{112,240},{113,241},{114,242},{115,243},{116,244},{117,245},{118,2... | collective-permute-start | bytes 196616 | tf_op jit(solution)/shard_map/ppermute | solution.py:363
  5.8 1.3 collective-permute-start.6
  7.1 1.3 collective-permute-start.5
  19.4 29.1 %all_to_all.15.x_ref = bf16[8,32,4096]{2,1,0:T(8,128)(2,1)S(1)} all-to-all(bf16[8,32,4096]{2,1,0:T(8,128)(2,1)S(1)} %broadcast_in_dim.16), channel_id=1, replica_groups={{0,16,32,48,64,80,96,112},{128,144,160,176,192,208,224,240},{1,17,33,49..., dimensions={0} | all-to-all | bytes 4194304 | tf_op jit(solution)/shard_map/all_to_all | solution.py:336
  48.6 2.0 collective-permute-start.11
  50.6 2.2 %copy-done = bf16[1,4096,512]{2,1,0:T(8,128)(2,1)S(1)} copy-done((bf16[1,4096,512]{2,1,0:T(8,128)(2,1)S(1)}, bf16[1,4096,512]{2,1,0:T(8,128)(2,1)}, u32[]{:S(2)}) %copy-start) | copy-done | bytes 4194328
  52.8 2.2 %copy-done.2 = bf16[1,4096,512]{2,1,0:T(8,128)(2,1)S(1)} copy-done((bf16[1,4096,512]{2,1,0:T(8,128)(2,1)S(1)}, bf16[1,4096,512]{2,1,0:T(8,128)(2,1)}, u32[]{:S(2)}) %copy-start.2) | copy-done | bytes 4194328
  55.0 3.8 %shard_map.76 = (f32[256,512]{1,0:T(8,128)S(1)}, f32[256,512]{1,0:T(8,128)S(1)}) custom-call(bf16[8,32,4096]{2,1,0:T(8,128)(2,1)S(1)} %all_to_all.15.x_ref, bf16[4096,512]{1,0:T(8,128)(2,1)S(1)} %bitcast.42, bf16[4096,512]{1,0:T(8,128)(2,1)S(1)} %bitcast.47), custom_call_target="tpu_custom_call" | custom-call | flops 1 | bytes 1 | tf_op jit(solution)/shard_map/pallas_call | solution.py:68
  58.9 4.1 %shard_map.77 = (f32[256,512]{1,0:T(8,128)S(1)}, bf16[256,512]{1,0:T(8,128)(2,1)S(1)}, f32[256,512]{1,0:T(8,128)S(1)}, f32[256,512]{1,0:T(8,128)S(1)}) custom-call(s32[1]{0:T(128)} %bitcast.1.same_ref, bf16[8,32,4096]{2,1,0:T(8,128)(2,1)} %collective-permute-done.11.x_ref, bf16[4096,512]{1,0:T(8,128)(2,1)S(1)} %bitcast.43, bf16[4096,512]{1,0:T(8,128)(2,1)S(1)} %bitcast.48, ...), custom_call_target="tpu_custom_call" | custom-call | flops 1 | bytes 1 | tf_op jit(solution)/shard_map/pallas_call | solution.py:94
  64.9 26.0 %collective-permute-done.13 = bf16[256,512]{1,0:T(8,128)(2,1)S(1)} collective-permute-done((bf16[256,512]{1,0:T(8,128)(2,1)S(1)}, bf16[256,512]{1,0:T(8,128)(2,1)S(1)}, u32[]{:S(2)}, u32[]{:S(2)}) %collective-permute-start.13) | collective-permute-done | bytes 262176 | tf_op jit(solution)/shard_map/ppermute | solution.py:327
  90.9 6.5 %collective-permute-start.14 = (bf16[256,512]{1,0:T(8,128)(2,1)S(1)}, bf16[256,512]{1,0:T(8,128)(2,1)S(1)}, u32[]{:S(2)}, u32[]{:S(2)}) collective-permute-start(bf16[256,512]{1,0:T(8,128)(2,1)S(1)} %collective-permute-done.13), channel_id=1, source_target_pairs={{64,136},{65,137},{66,138},{67,139},{68,140},{69,141},{70,142},{71... | collective-permute-start | bytes 786440 | tf_op jit(solution)/shard_map/ppermute | solution.py:331
  97.5 11.0 %collective-permute-done.14.vb = bf16[256,512]{1,0:T(8,128)(2,1)S(1)} collective-permute-done((bf16[256,512]{1,0:T(8,128)(2,1)S(1)}, bf16[256,512]{1,0:T(8,128)(2,1)S(1)}, u32[]{:S(2)}, u32[]{:S(2)}) %collective-permute-start.14) | collective-permute-done | bytes 262176 | tf_op jit(solution)/shard_map/ppermute | solution.py:331
  108.5 2.4 %shard_map.78 = (bf16[256,512]{1,0:T(8,128)(2,1)S(1)}, bf16[256,512]{1,0:T(8,128)(2,1)S(1)}, bf16[4,256,256]{2,1,0:T(8,128)(2,1)S(1)}, bf16[4,256,256]{2,1,0:T(8,128)(2,1)S(1)}, bf16[256,1024]{1,0:T(8,128)(2,1)S(1)}) custom-call(f32[256,512]{1,0:T(8,128)S(1)} %get-tuple-element.20.ka, f32[256,512]{1,0:T(8,128)S(1)} %collective-permute-done.12.kb, ...), custom_call_target="tpu_custom_call" | custom-call | flops 1 | bytes 1 | tf_op jit(solution)/shard_map/pallas_call | solution.py:156
  113.9 3.2 %shard_map.82 = bf16[8,32,2048]{2,1,0:T(8,128)(2,1)} custom-call(s32[1]{0:T(128)} %bitcast.16.core_ref, bf16[256,1024]{1,0:T(8,128)(2,1)S(1)} %get-tuple-element.30.after_ref.g, bf16[256,1024]{1,0:T(8,128)(2,1)S(1)} %collective-permute-done.18.h, bf16[4096,512]{1,0:T(8,128)(2,1)S(1)} %bitcast.45, bf16[4096,512]{1,0:T(8,128)(2,1)S(1)} %bitcast.50, ...), custom_call_target="tpu_custom_call" | custom-call | flops 1 | bytes 1 | tf_op jit(solution)/shard_map/pallas_call | solution.py:218
  117.1 2.0 copy-done.4
  119.1 7.2 %all-to-all-start.1 = ((bf16[8,32,2048]{2,1,0:T(8,128)(2,1)}), bf16[8,32,2048]{2,1,0:T(8,128)(2,1)}, u32[]{:S(2)}, u32[]{:S(2)}) async-start(bf16[8,32,2048]{2,1,0:T(8,128)(2,1)} %shard_map.82), calls=%async_computation.1 | async-start | bytes 2097152 | tf_op jit(solution)/shard_map/all_to_all | solution.py:336
  127.2 5.9 %shard_map.81 = bf16[8,32,2048]{2,1,0:T(8,128)(2,1)} custom-call(s32[1]{0:T(128)} %bitcast.16.core_ref, bf16[256,1024]{1,0:T(8,128)(2,1)S(1)} %collective-permute-done.15.g, bf16[256,1024]{1,0:T(8,128)(2,1)S(1)} %collective-permute-done.16.h, bf16[4096,512]{1,0:T(8,128)(2,1)} %bitcast.41, bf16[4096,512]{1,0:T(8,128)(2,1)} %bitcast.46, ...), custom_call_target="tpu_custom_call" | custom-call | flops 1 | bytes 1 | tf_op jit(solution)/shard_map/pallas_call | solution.py:272
  133.1 6.6 %all-to-all-done.1 = bf16[8,32,2048]{2,1,0:T(8,128)(2,1)} async-done(((bf16[8,32,2048]{2,1,0:T(8,128)(2,1)}), bf16[8,32,2048]{2,1,0:T(8,128)(2,1)}, u32[]{:S(2)}, u32[]{:S(2)}) %all-to-all-start.1) | async-done | bytes 1048608 | tf_op jit(solution)/shard_map/all_to_all | solution.py:336
  139.7 1.4 convert_reduce_fusion.1
  141.0 5.4 %all-to-all-start.2 = ((bf16[8,32,2048]{2,1,0:T(8,128)(2,1)}), bf16[8,32,2048]{2,1,0:T(8,128)(2,1)S(1)}, u32[]{:S(2)}, u32[]{:S(2)}) async-start(bf16[8,32,2048]{2,1,0:T(8,128)(2,1)} %shard_map.81), calls=%async_computation.2 | async-start | bytes 2097152 | tf_op jit(solution)/shard_map/all_to_all | solution.py:336
  146.6 13.0 %all-to-all-done.2 = bf16[8,32,2048]{2,1,0:T(8,128)(2,1)S(1)} async-done(((bf16[8,32,2048]{2,1,0:T(8,128)(2,1)}), bf16[8,32,2048]{2,1,0:T(8,128)(2,1)S(1)}, u32[]{:S(2)}, u32[]{:S(2)}) %all-to-all-start.2) | async-done | bytes 1048608 | tf_op jit(solution)/shard_map/all_to_all | solution.py:336
  170.6 41.6 %collective-permute-done.27 = bf16[64,1024]{1,0:T(8,128)(2,1)S(1)} collective-permute-done((bf16[64,1024]{1,0:T(8,128)(2,1)S(1)}, bf16[64,1024]{1,0:T(8,128)(2,1)S(1)}, u32[]{:S(2)}, u32[]{:S(2)}) %collective-permute-start.27) | collective-permute-done | bytes 131104 | tf_op jit(solution)/shard_map/ppermute | solution.py:428
  212.2 2.5 %collective-permute-done.26 = bf16[64,1024]{1,0:T(8,128)(2,1)S(1)} collective-permute-done((bf16[64,1024]{1,0:T(8,128)(2,1)S(1)}, bf16[64,1024]{1,0:T(8,128)(2,1)S(1)}, u32[]{:S(2)}, u32[]{:S(2)}) %collective-permute-start.26) | collective-permute-done | bytes 131104 | tf_op jit(solution)/shard_map/ppermute | solution.py:428
  214.8 1.3 collective-permute-done.24
  (79 shorter events, 29.6 us)
Async XLA Ops:
  1.7 9.2 %collective-permute-start.7 = (bf16[32,1024]{1,0:T(8,128)(2,1)S(1)}, bf16[32,1024]{1,0:T(8,128)(2,1)S(1)}, u32[]{:S(2)}, u32[]{:S(2)}) collective-permute-start(bf16[32,1024]{1,0:T(8,128)(2,1)S(1)} %get-tuple-element.39), channel_id=1, source_target_pairs={{112,240},{113,241},{114,242},{115,243},{116,244},{117,245},{118,2... | collective-permute-start | bytes 196616 | tf_op jit(solution)/shard_map/ppermute | solution.py:363
  5.8 6.5 %collective-permute-start.6 = (bf16[32,1024]{1,0:T(8,128)(2,1)S(1)}, bf16[32,1024]{1,0:T(8,128)(2,1)S(1)}, u32[]{:S(2)}, u32[]{:S(2)}) collective-permute-start(bf16[32,1024]{1,0:T(8,128)(2,1)S(1)} %get-tuple-element.40), channel_id=1, source_target_pairs={{112,224},{113,225},{114,226},{115,227},{116,228},{117,229},{118,2... | collective-permute-start | bytes 196616 | tf_op jit(solution)/shard_map/ppermute | solution.py:363
  7.1 6.5 %collective-permute-start.5 = (bf16[32,1024]{1,0:T(8,128)(2,1)S(1)}, bf16[32,1024]{1,0:T(8,128)(2,1)S(1)}, u32[]{:S(2)}, u32[]{:S(2)}) collective-permute-start(bf16[32,1024]{1,0:T(8,128)(2,1)S(1)} %get-tuple-element.34), channel_id=1, source_target_pairs={{112,208},{113,209},{114,210},{115,211},{116,212},{117,213},{118,2... | collective-permute-start | bytes 196616 | tf_op jit(solution)/shard_map/ppermute | solution.py:363
  8.4 6.5 %collective-permute-start.4 = (bf16[32,1024]{1,0:T(8,128)(2,1)S(1)}, bf16[32,1024]{1,0:T(8,128)(2,1)S(1)}, u32[]{:S(2)}, u32[]{:S(2)}) collective-permute-start(bf16[32,1024]{1,0:T(8,128)(2,1)S(1)} %get-tuple-element.35), channel_id=1, source_target_pairs={{112,192},{113,193},{114,194},{115,195},{116,196},{117,197},{118,1... | collective-permute-start | bytes 196616 | tf_op jit(solution)/shard_map/ppermute | solution.py:363
  9.7 5.2 %collective-permute-start.3 = (bf16[32,1024]{1,0:T(8,128)(2,1)S(1)}, bf16[32,1024]{1,0:T(8,128)(2,1)S(1)}, u32[]{:S(2)}, u32[]{:S(2)}) collective-permute-start(bf16[32,1024]{1,0:T(8,128)(2,1)S(1)} %get-tuple-element.36), channel_id=1, source_target_pairs={{112,176},{113,177},{114,178},{115,179},{116,180},{117,181},{118,1... | collective-permute-start | bytes 196616 | tf_op jit(solution)/shard_map/ppermute | solution.py:363
  11.0 3.9 %collective-permute-start.2 = (bf16[32,1024]{1,0:T(8,128)(2,1)S(1)}, bf16[32,1024]{1,0:T(8,128)(2,1)S(1)}, u32[]{:S(2)}, u32[]{:S(2)}) collective-permute-start(bf16[32,1024]{1,0:T(8,128)(2,1)S(1)} %get-tuple-element.37), channel_id=1, source_target_pairs={{112,160},{113,161},{114,162},{115,163},{116,164},{117,165},{118,1... | collective-permute-start | bytes 196616 | tf_op jit(solution)/shard_map/ppermute | solution.py:363
  12.3 3.9 %collective-permute-start = (bf16[32,1024]{1,0:T(8,128)(2,1)S(1)}, bf16[32,1024]{1,0:T(8,128)(2,1)S(1)}, u32[]{:S(2)}, u32[]{:S(2)}) collective-permute-start(bf16[32,1024]{1,0:T(8,128)(2,1)S(1)} %get-tuple-element.38), channel_id=1, source_target_pairs={{112,128},{113,129},{114,130},{115,131},{116,132},{117,133},{118,1... | collective-permute-start | bytes 196616 | tf_op jit(solution)/shard_map/ppermute | solution.py:363
  13.6 3.3 %collective-permute-start.1 = (bf16[32,1024]{1,0:T(8,128)(2,1)S(1)}, bf16[32,1024]{1,0:T(8,128)(2,1)S(1)}, u32[]{:S(2)}, u32[]{:S(2)}) collective-permute-start(bf16[32,1024]{1,0:T(8,128)(2,1)S(1)} %get-tuple-element.33), channel_id=1, source_target_pairs={{112,144},{113,145},{114,146},{115,147},{116,148},{117,149},{118,1... | collective-permute-start | bytes 196616 | tf_op jit(solution)/shard_map/ppermute | solution.py:363
  48.6 10.2 %collective-permute-start.11 = (bf16[8,32,4096]{2,1,0:T(8,128)(2,1)S(1)}, bf16[8,32,4096]{2,1,0:T(8,128)(2,1)}, u32[]{:S(2)}, u32[]{:S(2)}) collective-permute-start(bf16[8,32,4096]{2,1,0:T(8,128)(2,1)S(1)} %all_to_all.15.x_ref), channel_id=1, source_target_pairs={{128,129},{129,128},{130,131},{131,130},{132,133},{133,132},{134,1... | collective-permute-start | bytes 6291464 | tf_op jit(solution)/shard_map/ppermute | solution.py:314
  62.9 34.6 %collective-permute-start.12 = (f32[256,512]{1,0:T(8,128)S(1)}, f32[256,512]{1,0:T(8,128)S(1)}, u32[]{:S(2)}, u32[]{:S(2)}) collective-permute-start(f32[256,512]{1,0:T(8,128)S(1)} %get-tuple-element.21), channel_id=1, source_target_pairs={{128,136},{129,137},{130,138},{131,139},{132,140},{133,141},{134,1... | collective-permute-start | bytes 1572872 | tf_op jit(solution)/shard_map/ppermute | solution.py:314
  63.6 27.3 %collective-permute-start.13 = (bf16[256,512]{1,0:T(8,128)(2,1)S(1)}, bf16[256,512]{1,0:T(8,128)(2,1)S(1)}, u32[]{:S(2)}, u32[]{:S(2)}) collective-permute-start(bf16[256,512]{1,0:T(8,128)(2,1)S(1)} %get-tuple-element.23), channel_id=1, source_target_pairs={{128,64},{129,65},{130,66},{131,67},{132,68},{133,69},{134,70},{13... | collective-permute-start | bytes 786440 | tf_op jit(solution)/shard_map/ppermute | solution.py:327
  90.9 17.6 %collective-permute-start.14 = (bf16[256,512]{1,0:T(8,128)(2,1)S(1)}, bf16[256,512]{1,0:T(8,128)(2,1)S(1)}, u32[]{:S(2)}, u32[]{:S(2)}) collective-permute-start(bf16[256,512]{1,0:T(8,128)(2,1)S(1)} %collective-permute-done.13), channel_id=1, source_target_pairs={{64,136},{65,137},{66,138},{67,139},{68,140},{69,141},{70,142},{71... | collective-permute-start | bytes 786440 | tf_op jit(solution)/shard_map/ppermute | solution.py:331
  111.6 2.4 %collective-permute-start.17 = (bf16[2,2048,512]{2,1,0:T(8,128)(2,1)S(1)}, bf16[2,2048,512]{2,1,0:T(8,128)(2,1)S(1)}, u32[]{:S(2)}, u32[]{:S(2)}) collective-permute-start(bf16[2,2048,512]{2,1,0:T(8,128)(2,1)S(1)} %shard_map.80), channel_id=1, source_target_pairs={{128,129},{129,128},{130,131},{131,130},{132,133},{133,132},{134,1... | collective-permute-start | bytes 12582920 | tf_op jit(solution)/shard_map/ppermute | solution.py:314
  112.5 1.4 collective-permute-start.18
  113.2 13.1 %collective-permute-start.15 = (bf16[256,1024]{1,0:T(8,128)(2,1)S(1)}, bf16[256,1024]{1,0:T(8,128)(2,1)S(1)}, u32[]{:S(2)}, u32[]{:S(2)}) collective-permute-start(bf16[256,1024]{1,0:T(8,128)(2,1)S(1)} %get-tuple-element.30.after_ref.g), channel_id=1, source_target_pairs={{128,136},{129,137},{130,138},{131,139},{132,140},{133,141},{134,1... | collective-permute-start | bytes 1572872 | tf_op jit(solution)/shard_map/ppermute | solution.py:314
  119.1 20.6 %all-to-all-start.1 = ((bf16[8,32,2048]{2,1,0:T(8,128)(2,1)}), bf16[8,32,2048]{2,1,0:T(8,128)(2,1)}, u32[]{:S(2)}, u32[]{:S(2)}) async-start(bf16[8,32,2048]{2,1,0:T(8,128)(2,1)} %shard_map.82), calls=%async_computation.1 | async-start | bytes 2097152 | tf_op jit(solution)/shard_map/all_to_all | solution.py:336
  141.0 18.6 %all-to-all-start.2 = ((bf16[8,32,2048]{2,1,0:T(8,128)(2,1)}), bf16[8,32,2048]{2,1,0:T(8,128)(2,1)S(1)}, u32[]{:S(2)}, u32[]{:S(2)}) async-start(bf16[8,32,2048]{2,1,0:T(8,128)(2,1)} %shard_map.81), calls=%async_computation.2 | async-start | bytes 2097152 | tf_op jit(solution)/shard_map/all_to_all | solution.py:336
  160.6 2.8 %collective-permute-start.22 = (bf16[32,1024]{1,0:T(8,128)(2,1)S(1)}, bf16[32,1024]{1,0:T(8,128)(2,1)S(1)}, u32[]{:S(2)}, u32[]{:S(2)}) collective-permute-start(bf16[32,1024]{1,0:T(8,128)(2,1)S(1)} %bitcast.57), channel_id=1, source_target_pairs={{128,138},{129,139},{130,136},{131,137},{132,130},{133,131},{134,1... | collective-permute-start | bytes 196616 | tf_op jit(solution)/shard_map/ppermute | solution.py:314
  161.3 2.1 collective-permute-start.21
  162.0 1.4 collective-permute-start.20
  164.2 48.0 %collective-permute-start.27 = (bf16[64,1024]{1,0:T(8,128)(2,1)S(1)}, bf16[64,1024]{1,0:T(8,128)(2,1)S(1)}, u32[]{:S(2)}, u32[]{:S(2)}) collective-permute-start(bf16[64,1024]{1,0:T(8,128)(2,1)S(1)} %pad_maximum_fusion.2), channel_id=1, source_target_pairs={{224,112},{225,113},{226,114},{227,115},{228,116},{229,117},{230,1... | collective-permute-start | bytes 393224 | tf_op jit(solution)/shard_map/ppermute | solution.py:428
  165.5 49.3 %collective-permute-start.26 = (bf16[64,1024]{1,0:T(8,128)(2,1)S(1)}, bf16[64,1024]{1,0:T(8,128)(2,1)S(1)}, u32[]{:S(2)}, u32[]{:S(2)}) collective-permute-start(bf16[64,1024]{1,0:T(8,128)(2,1)S(1)} %pad_maximum_fusion.2), channel_id=1, source_target_pairs={{192,112},{193,113},{194,114},{195,115},{196,116},{197,117},{198,1... | collective-permute-start | bytes 393224 | tf_op jit(solution)/shard_map/ppermute | solution.py:428
  166.8 48.0 %collective-permute-start.25 = (bf16[64,1024]{1,0:T(8,128)(2,1)S(1)}, bf16[64,1024]{1,0:T(8,128)(2,1)S(1)}, u32[]{:S(2)}, u32[]{:S(2)}) collective-permute-start(bf16[64,1024]{1,0:T(8,128)(2,1)S(1)} %pad_maximum_fusion.2), channel_id=1, source_target_pairs={{160,112},{161,113},{162,114},{163,115},{164,116},{165,117},{166,1... | collective-permute-start | bytes 393224 | tf_op jit(solution)/shard_map/ppermute | solution.py:428
  168.1 48.0 %collective-permute-start.24 = (bf16[64,1024]{1,0:T(8,128)(2,1)S(1)}, bf16[64,1024]{1,0:T(8,128)(2,1)S(1)}, u32[]{:S(2)}, u32[]{:S(2)}) collective-permute-start(bf16[64,1024]{1,0:T(8,128)(2,1)S(1)} %pad_maximum_fusion.2), channel_id=1, source_target_pairs={{128,112},{129,113},{130,114},{131,115},{132,116},{133,117},{134,1... | collective-permute-start | bytes 393224 | tf_op jit(solution)/shard_map/ppermute | solution.py:428
  (13 other events, 118.5 us)

commit v4 on v3

--- a/solution.py
+++ b/solution.py
@@ -46,85 +46,105 @@
     return weight[pl.ds(pl.multiple_of(index * size, size), size), :]
 
 
-def product_near(near, weights, block):
+def product_near(near, weight):
     count, rows, width = near.shape
     tokens = count * rows
-    cols = weights[0].shape[1]
-    many = len(weights)
-
-    def kernel(x_ref, *refs):
-        x = x_ref[...].reshape(tokens, block)
-        first = pl.program_id(0) == 0
-        for w, out in zip(refs[:many], refs[many:]):
-
-            @pl.when(first)
-            def _():
-                out[...] = dot(x, w[...])
-
-            @pl.when(jnp.logical_not(first))
-            def _():
-                out[...] += dot(x, w[...])
-
-    return pl.pallas_call(
-        kernel,
-        grid=(width // block,),
-        in_specs=[pl.BlockSpec((count, rows, block), lambda i: (0, 0, i))]
-        + [pl.BlockSpec((block, cols), lambda i: (i, 0))] * many,
-        out_specs=[pl.BlockSpec((tokens, cols), lambda i: (0, 0))] * many,
-        out_shape=[like((tokens, cols), F32)] * many,
-        cost_estimate=cost(),
-        compiler_params=params(),
-    )(near, *weights)
-
-
-def product_far(same, far, weights, parts):
+    cols = weight.shape[1]
+
+    def kernel(x_ref, w, out):
+        out[...] = dot(x_ref[...].reshape(tokens, width), w[...])
+
+    return pl.pallas_call(
+        kernel,
+        in_specs=whole(2),
+        out_specs=whole(1)[0],
+        out_shape=like((tokens, cols), F32),
+        cost_estimate=cost(),
+        compiler_params=params(),
+    )(near, weight)
+
+
+def product_far(same, far, weights, parts, block):
     count, rows, width = far.shape
     tokens = count * rows
     cols = weights[0].shape[1]
-
-    def kernel(same_ref, x_ref, wk, wv, pk, pv, key_out, value_out, key_own, value_own):
+    steps = width // block
+
+    def kernel(same_ref, far_ref, wk, wv, pk, pv, key_out, value_out, key_own, value_own, x, sems):
         same_here = same_ref[0] > 0
-        x = x_ref[...].reshape(tokens, width)
-        for w, p, out, own in ((wk, pk, key_out, key_own), (wv, pv, value_out, value_own)):
-            total = dot(x, w[...])
+        loads = []
+        for i in range(steps):
+            at = pl.ds(i * block, block)
+            loads.append(
+                pltpu.make_async_copy(far_ref.at[:, :, at], x.at[:, :, at], sems.at[i])
+            )
+        for load in loads:
+            load.start()
+        totals = [None, None]
+        for i in range(steps):
+            loads[i].wait()
+            at = slice(i * block, (i + 1) * block)
+            here = x[:, :, at].reshape(tokens, block)
+            for n, w in enumerate((wk, wv)):
+                term = dot(here, w[at, :])
+                totals[n] = term if i == 0 else totals[n] + term
+        for total, p, out, own in (
+            (totals[0], pk, key_out, key_own),
+            (totals[1], pv, value_out, value_own),
+        ):
             part = p[...]
             out[...] = jnp.where(same_here, total, part).astype(out.dtype)
             own[...] = jnp.where(same_here, part, total)
 
     return pl.pallas_call(
         kernel,
-        in_specs=scalar() + whole(5),
+        in_specs=scalar() + [pl.BlockSpec(memory_space=pl.ANY)] + whole(4),
         out_specs=whole(4),
         out_shape=[like((tokens, cols), t) for t in (F32, BF16, F32, F32)],
+        scratch_shapes=[
+            pltpu.VMEM((count, rows, width), BF16),
+            pltpu.SemaphoreType.DMA((steps,)),
+        ],
         cost_estimate=cost(),
         compiler_params=params(),
     )(same, far, *weights, *parts)
 
 
-def other_rows(core, key_weight, value_weight, block, after):
+def settle(array, after):
+    def kernel(source, after_ref, out):
+        out[...] = source[...]
+
+    return pl.pallas_call(
+        kernel,
+        in_specs=whole(1) + [pl.BlockSpec(memory_space=pl.ANY)],
+        out_specs=whole(1)[0],
+        out_shape=like(array.shape, array.dtype),
+        cost_estimate=cost(),
+        compiler_params=params(),
+    )(array, after)
+
+
+def other_rows(core, key_weight, value_weight, grads, block):
     height, cols = key_weight.shape
-    step = block // 2
-
-    def kernel(core_ref, wk, wv, after_ref, out):
-        out[0] = wk[...]
-        out[1] = wv[...]
-
-    def place(i, c):
-        return ((i // 2 * 2 + 1 - c[0]) * 2 + i % 2, 0)
-
-    return pl.pallas_call(
-        kernel,
-        grid_spec=pltpu.PrefetchScalarGridSpec(
-            num_scalar_prefetch=1,
-            grid=(4,),
-            in_specs=[pl.BlockSpec((step, cols), place)] * 2
-            + [pl.BlockSpec(memory_space=pl.ANY)],
-            out_specs=pl.BlockSpec((2, step, cols), lambda i, c: (0, i, 0)),
-        ),
-        out_shape=like((2, height // 2, cols), BF16),
-        cost_estimate=cost(),
-        compiler_params=params(),
-    )(core, key_weight, value_weight, after)
+    tokens = grads.shape[0]
+
+    def kernel(core_ref, wk, wv, g, out):
+        c = 1 - core_ref[0]
+        for n, w in enumerate((wk, wv)):
+            for j in range(2):
+                at = (2 * n + j) * block
+                out[at : at + block, :] = rows_of(w, 2 * j + c, block)
+            at = 2 * height // 2 + n * tokens
+            out[at : at + tokens, :] = g[:, n * cols : (n + 1) * cols]
+
+    return pl.pallas_call(
+        kernel,
+        in_specs=scalar() + whole(3),
+        out_specs=whole(1)[0],
+        out_shape=like((height + 2 * tokens, cols), BF16),
+        cost_estimate=cost(),
+        compiler_params=params(),
+    )(core, key_weight, value_weight, grads)
 
 
 def attend(key_own, key_in, value_own, value_in, query, grad):
@@ -190,22 +210,24 @@
     )(keep, low, values, dscores, keys)
 
 
-def back_product_near(core, mine, others, key_weight, value_weight, weights_far, block, count):
+def back_product_near(core, mine, key_weight, value_weight, packet, block, count):
     tokens = mine.shape[0]
     cols = key_weight.shape[1]
     width = 2 * block
     step = block // 2
     rows = tokens // count
 
-    def kernel(core_ref, g, h, wk, wv, far, out, low, sems):
+    def kernel(core_ref, g, wk, wv, far, out, low, sems):
         c = core_ref[0]
         copies = []
         for i in range(width // step):
             at = (i // 2 * 2 + c) * 2 + i % 2
             total = dot(g[:, :cols], rows_of(wk, at, step), NT)
             total += dot(g[:, cols:], rows_of(wv, at, step), NT)
-            total += dot(h[:, :cols], far[0, i * step : (i + 1) * step, :], NT)
-            total += dot(h[:, cols:], far[1, i * step : (i + 1) * step, :], NT)
+            for n in range(2):
+                weight = far[n * width + i * step : n * width + (i + 1) * step, :]
+                at = 2 * width + n * tokens
+                total += dot(far[at : at + tokens, :], weight, NT)
             low[i] = total.reshape(count, rows, step).astype(BF16)
             copy = pltpu.make_async_copy(
                 low.at[i], out.at[:, :, pl.ds(i * step, step)], sems.at[i]
@@ -217,7 +239,7 @@
 
     return pl.pallas_call(
         kernel,
-        in_specs=scalar() + whole(5),
+        in_specs=scalar() + whole(4),
         out_specs=pl.BlockSpec(memory_space=pltpu.HBM),
         out_shape=like((count, rows, width), BF16),
         scratch_shapes=[
@@ -226,10 +248,10 @@
         ],
         cost_estimate=cost(),
         compiler_params=params(),
-    )(core, mine, others, key_weight, value_weight, weights_far)
-
-
-def back_product(core, mine, others, key_weight, value_weight, weights_far, block, count):
+    )(core, mine, key_weight, value_weight, packet)
+
+
+def back_product(core, mine, others, key_weight, value_weight, packet, block, count):
     tokens = mine.shape[0]
     cols = key_weight.shape[1]
     width = 2 * block
@@ -243,7 +265,7 @@
         for i in range(steps):
             at = pl.ds(pl.multiple_of(((i // 2 * 2 + c) * 2 + i % 2) * step, step), step)
             sources = [wk.at[at], wv.at[at]]
-            sources += [far.at[n, pl.ds(i * step, step)] for n in range(2)]
+            sources += [far.at[pl.ds(n * width + i * step, step)] for n in range(2)]
             loads.append(
                 [
                     pltpu.make_async_copy(source, held.at[i, n], in_sems.at[i, n])
@@ -282,7 +304,7 @@
         ],
         cost_estimate=cost(),
         compiler_params=pltpu.CompilerParams(vmem_limit_bytes=VMEM_BACK),
-    )(core, mine, others, key_weight, value_weight, weights_far)
+    )(core, mine, others, key_weight, value_weight, packet)
 
 
 def body(section_states, key_weight, value_weight, queries, cotangent):
@@ -371,11 +393,13 @@
     weights = [key_weight, value_weight]
     near = exchange(jnp.broadcast_to(chunk[None], (count,) + chunk.shape))
     far = swap_core(near)
-    parts = product_near(near, weights, block)
+    parts = [product_near(near, weight) for weight in weights]
     same = (core == replica).astype(jnp.int32).reshape(1)
-    key_out, value_out, key_own, value_own = product_far(same, far, weights, parts)
+    key_out, value_out, key_own, value_own = product_far(same, far, weights, parts, block)
     key_in = swap_replica(key_out)
-    value_in = swap_replica_lent(lend(value_out))
+    lent = lend(value_out)
+    value_in = swap_replica_lent(lent)
+    key_own = settle(key_own, lent)
 
     query, grad = queries[0, 0], cotangent[0, 0]
     keys, values, low, dscores, grads = attend(
@@ -386,22 +410,18 @@
     context, query_grad = attend_out(keep, low, values, dscores, keys)
 
 
-    weights_far = swap_core(other_rows(core_index, key_weight, value_weight, block, grads))
-
-    def reduce(term):
-        return jnp.sum(exchange(term).astype(F32), axis=0)
-
-    grads_over = swap_core(grads)
-    own_total = reduce(
-        back_product_near(
-            core_index, grads, grads_over, *weights, weights_far, block, count
-        )
+    packet = swap_core(other_rows(core_index, *weights, grads, block))
+
+    own_terms = exchange(
+        back_product_near(core_index, grads, *weights, packet, block, count)
     )
     other_term = back_product(
-        core_index, grads_in, swap_core(grads_in), *weights, weights_far, block, count
-    )
-    other_term, own_total = lax.optimization_barrier((other_term, own_total))
-    other_total = reduce(other_term)
+        core_index, grads_in, swap_core(grads_in), *weights, packet, block, count
+    )
+    other_term, own_terms = lax.optimization_barrier((other_term, own_terms))
+    own_total, other_total = (
+        jnp.sum(terms.astype(F32), axis=0) for terms in (own_terms, exchange(other_term))
+    )
     total = jnp.stack([own_total, other_total]).reshape(replicas, rows, 2, block)
 
     def owned(owner):

time: 218 us -> 214 us (0.982)
  starting transfers between devices: 50 us -> 45.1 us
  waiting for transfers between devices: 104 us -> 107 us
    ppermute x4, waiting for transfers between devices: 45.5 us -> 51 us  [body(): out.append(lax.ppermute(summed, AXES, pairs))]
    ppermute x1, starting transfers between devices: 6.53 us -> 2.29 us  [swap_replica_lent(): return lax.ppermute(array, AXES, pairs)]
    pallas_call x4 -> x6, Pallas kernels: 11.7 us -> 9.84 us  [the longest x1 3.79 us: product_far(): pl.pallas_call(kernel, in_specs=scalar() + [pl.BlockSpec(memory_space=pl....]
    ppermute x13 -> x12, starting transfers between devices: 10.6 us -> 9.9 us  [send(): return lax.ppermute(array, AXES, pairs)]
    unnamed x19 -> x17, local copies, waits for them, and re-layouts: 6.56 us -> 6.38 us
  transfers between devices with their start and end apart: 30 -> 29, of which waited for: 9 -> 9; matrix products, arithmetic and copies ran while one was open for 0% -> 1% of each run, Pallas kernels for 6% -> 6%
where the time goes in v4:
time: 214 us; the launch traced here: 213 us
  waiting for transfers between devices  107 us (50%)
  starting transfers between devices  45.1 us (21%)
  blocking collectives  29.1 us (14%)
  Pallas kernels  19.3 us (9%)
  local copies, waits for them, and re-layouts  8.54 us (4%)
  other arithmetic  2.56 us (1%)
    ppermute x4, waiting for transfers between devices, body(): out.append(lax.ppermute(summed, AXES, pairs))  51 us
    all_to_all x1, blocking collectives, exchange(): return lax.all_to_all(array, 'pipe', 0, 0, axis_index_groups=groups)  29.1 us
    ppermute x1, waiting for transfers between devices, lend(): return lax.ppermute(array, AXES, pairs)  24.1 us
    all_to_all x2, waiting for transfers between devices, exchange(): return lax.all_to_all(array, 'pipe', 0, 0, axis_index_groups=groups)  18.3 us
    ppermute x8, starting transfers between devices, body(): part = lax.ppermute(piece[k * rows:(k + 1) * rows], AXES, pairs)  13.1 us
    all_to_all x2, starting transfers between devices, exchange(): return lax.all_to_all(array, 'pipe', 0, 0, axis_index_groups=groups)  12.7 us
    ppermute x1, waiting for transfers between devices, swap_replica_lent(): return lax.ppermute(array, AXES, pairs)  11.5 us
    ppermute x12, starting transfers between devices, send(): return lax.ppermute(array, AXES, pairs)  9.9 us
  transfers between devices with their start and end apart: 29, of which 9 were waited for; matrix products, arithmetic and copies ran while one was open for 1% of the time, Pallas kernels for 6%

profile of v4, /device:TPU:122, one launch (start us, length us, event | category | flops | bytes accessed | tf_op | source)
XLA Modules:
  0.0 212.7 jit_solution(11711054722205906071)
XLA Ops:
  1.7 4.0 %collective-permute-start.7 = (bf16[32,1024]{1,0:T(8,128)(2,1)S(1)}, bf16[32,1024]{1,0:T(8,128)(2,1)S(1)}, u32[]{:S(2)}, u32[]{:S(2)}) collective-permute-start(bf16[32,1024]{1,0:T(8,128)(2,1)S(1)} %get-tuple-element.35), channel_id=1, source_target_pairs={{112,240},{113,241},{114,242},{115,243},{116,244},{117,245},{118,2... | collective-permute-start | bytes 196616 | tf_op jit(solution)/shard_map/ppermute | solution.py:385
  5.8 1.3 collective-permute-start.6
  7.1 1.3 collective-permute-start.5
  9.7 1.3 collective-permute-start.3
  11.0 1.3 collective-permute-start.2
  19.4 29.1 %all_to_all.15.x_ref = bf16[8,32,4096]{2,1,0:T(8,128)(2,1)S(1)} all-to-all(bf16[8,32,4096]{2,1,0:T(8,128)(2,1)S(1)} %broadcast_in_dim.16), channel_id=1, replica_groups={{0,16,32,48,64,80,96,112},{128,144,160,176,192,208,224,240},{1,17,33,49..., dimensions={0} | all-to-all | bytes 4194304 | tf_op jit(solution)/shard_map/all_to_all | solution.py:358
  48.6 2.0 collective-permute-start.11
  50.6 2.2 %copy-done = bf16[1,4096,512]{2,1,0:T(8,128)(2,1)S(1)} copy-done((bf16[1,4096,512]{2,1,0:T(8,128)(2,1)S(1)}, bf16[1,4096,512]{2,1,0:T(8,128)(2,1)}, u32[]{:S(2)}) %copy-start) | copy-done | bytes 4194328
  57.2 3.8 %shard_map.78 = (f32[256,512]{1,0:T(8,128)S(1)}, bf16[256,512]{1,0:T(8,128)(2,1)S(1)}, f32[256,512]{1,0:T(8,128)S(1)}, f32[256,512]{1,0:T(8,128)S(1)}) custom-call(s32[1]{0:T(128)} %bitcast.1.same_ref, bf16[8,32,4096]{2,1,0:T(8,128)(2,1)} %collective-permute-done.11.far_ref, bf16[4096,512]{1,0:T(8,128)(2,1)S(1)} %bitcast.43, bf16[4096,512]{1,0:T(8,128)(2,1)S(1)} %bitcast.48, ...), custom_call_target="tpu_custom_call" | custom-call | flops 1 | bytes 1 | tf_op jit(solution)/shard_map/pallas_call | solution.py:99
  63.0 24.1 %collective-permute-done.12.after_ref = bf16[256,512]{1,0:T(8,128)(2,1)S(1)} collective-permute-done((bf16[256,512]{1,0:T(8,128)(2,1)S(1)}, bf16[256,512]{1,0:T(8,128)(2,1)S(1)}, u32[]{:S(2)}, u32[]{:S(2)}) %collective-permute-start.12) | collective-permute-done | bytes 262176 | tf_op jit(solution)/shard_map/ppermute | solution.py:349
  87.0 2.3 %collective-permute-start.14 = (bf16[256,512]{1,0:T(8,128)(2,1)S(1)}, bf16[256,512]{1,0:T(8,128)(2,1)S(1)}, u32[]{:S(2)}, u32[]{:S(2)}) collective-permute-start(bf16[256,512]{1,0:T(8,128)(2,1)S(1)} %collective-permute-done.12.after_ref), channel_id=1, source_target_pairs={{64,136},{65,137},{66,138},{67,139},{68,140},{69,141},{70,142},{71... | collective-permute-start | bytes 786440 | tf_op jit(solution)/shard_map/ppermute | solution.py:353
  89.4 11.5 %collective-permute-done.14.vb = bf16[256,512]{1,0:T(8,128)(2,1)S(1)} collective-permute-done((bf16[256,512]{1,0:T(8,128)(2,1)S(1)}, bf16[256,512]{1,0:T(8,128)(2,1)S(1)}, u32[]{:S(2)}, u32[]{:S(2)}) %collective-permute-start.14) | collective-permute-done | bytes 262176 | tf_op jit(solution)/shard_map/ppermute | solution.py:353
  100.9 2.4 %shard_map.80 = (bf16[256,512]{1,0:T(8,128)(2,1)S(1)}, bf16[256,512]{1,0:T(8,128)(2,1)S(1)}, bf16[4,256,256]{2,1,0:T(8,128)(2,1)S(1)}, bf16[4,256,256]{2,1,0:T(8,128)(2,1)S(1)}, bf16[256,1024]{1,0:T(8,128)(2,1)S(1)}) custom-call(f32[256,512]{1,0:T(8,128)S(1)} %shard_map.79.ka, f32[256,512]{1,0:T(8,128)S(1)} %collective-permute-done.13.kb, ...), custom_call_target="tpu_custom_call" | custom-call | flops 1 | bytes 1 | tf_op jit(solution)/shard_map/pallas_call | solution.py:176
  105.2 3.2 %shard_map.84 = bf16[8,32,2048]{2,1,0:T(8,128)(2,1)} custom-call(s32[1]{0:T(128)} %bitcast.16.core_ref, bf16[256,1024]{1,0:T(8,128)(2,1)S(1)} %get-tuple-element.26.g, bf16[4096,512]{1,0:T(8,128)(2,1)S(1)} %bitcast.45, bf16[4096,512]{1,0:T(8,128)(2,1)S(1)} %bitcast.50, bf16[4608,512]{1,0:T(8,128)(2,1)S(1)} %collective-permute-done.17.far), custom_call_target="tpu_custom_call" | custom-call | flops 1 | bytes 1 | tf_op jit(solution)/shard_map/pallas_call | solution.py:240
  108.5 2.1 %copy-done.3 = bf16[4608,512]{1,0:T(8,128)(2,1)} copy-done((bf16[4608,512]{1,0:T(8,128)(2,1)}, bf16[4608,512]{1,0:T(8,128)(2,1)S(1)}, u32[]{:S(2)}) %copy-start.3) | copy-done | bytes 4718616
  110.6 7.3 %all-to-all-start.1 = ((bf16[8,32,2048]{2,1,0:T(8,128)(2,1)}), bf16[8,32,2048]{2,1,0:T(8,128)(2,1)}, u32[]{:S(2)}, u32[]{:S(2)}) async-start(bf16[8,32,2048]{2,1,0:T(8,128)(2,1)} %shard_map.84), calls=%async_computation.1 | async-start | bytes 2097152 | tf_op jit(solution)/shard_map/all_to_all | solution.py:358
  118.7 5.9 %shard_map.83 = bf16[8,32,2048]{2,1,0:T(8,128)(2,1)} custom-call(s32[1]{0:T(128)} %bitcast.16.core_ref, bf16[256,1024]{1,0:T(8,128)(2,1)S(1)} %collective-permute-done.15.g, bf16[256,1024]{1,0:T(8,128)(2,1)S(1)} %collective-permute-done.16.h, bf16[4096,512]{1,0:T(8,128)(2,1)} %bitcast.41, bf16[4096,512]{1,0:T(8,128)(2,1)} %bitcast.46, ...), custom_call_target="tpu_custom_call" | custom-call | flops 1 | bytes 1 | tf_op jit(solution)/shard_map/pallas_call | solution.py:294
  124.7 6.6 %all-to-all-done.1 = bf16[8,32,2048]{2,1,0:T(8,128)(2,1)} async-done(((bf16[8,32,2048]{2,1,0:T(8,128)(2,1)}), bf16[8,32,2048]{2,1,0:T(8,128)(2,1)}, u32[]{:S(2)}, u32[]{:S(2)}) %all-to-all-start.1) | async-done | bytes 1048608 | tf_op jit(solution)/shard_map/all_to_all | solution.py:358
  131.3 5.4 %all-to-all-start.2 = ((bf16[8,32,2048]{2,1,0:T(8,128)(2,1)}), bf16[8,32,2048]{2,1,0:T(8,128)(2,1)S(1)}, u32[]{:S(2)}, u32[]{:S(2)}) async-start(bf16[8,32,2048]{2,1,0:T(8,128)(2,1)} %shard_map.83), calls=%async_computation.2 | async-start | bytes 2097152 | tf_op jit(solution)/shard_map/all_to_all | solution.py:358
  136.7 1.4 convert_reduce_fusion.1
  138.3 11.6 %all-to-all-done.2 = bf16[8,32,2048]{2,1,0:T(8,128)(2,1)S(1)} async-done(((bf16[8,32,2048]{2,1,0:T(8,128)(2,1)}), bf16[8,32,2048]{2,1,0:T(8,128)(2,1)S(1)}, u32[]{:S(2)}, u32[]{:S(2)}) %all-to-all-start.2) | async-done | bytes 1048608 | tf_op jit(solution)/shard_map/all_to_all | solution.py:358
  160.9 47.1 %collective-permute-done.26 = bf16[64,1024]{1,0:T(8,128)(2,1)S(1)} collective-permute-done((bf16[64,1024]{1,0:T(8,128)(2,1)S(1)}, bf16[64,1024]{1,0:T(8,128)(2,1)S(1)}, u32[]{:S(2)}, u32[]{:S(2)}) %collective-permute-start.26) | collective-permute-done | bytes 131104 | tf_op jit(solution)/shard_map/ppermute | solution.py:448
  208.0 2.5 %collective-permute-done.25 = bf16[64,1024]{1,0:T(8,128)(2,1)S(1)} collective-permute-done((bf16[64,1024]{1,0:T(8,128)(2,1)S(1)}, bf16[64,1024]{1,0:T(8,128)(2,1)S(1)}, u32[]{:S(2)}, u32[]{:S(2)}) %collective-permute-start.25) | collective-permute-done | bytes 131104 | tf_op jit(solution)/shard_map/ppermute | solution.py:448
  210.5 1.3 collective-permute-done.23
  (77 shorter events, 30.4 us)
Async XLA Ops:
  1.7 9.2 %collective-permute-start.7 = (bf16[32,1024]{1,0:T(8,128)(2,1)S(1)}, bf16[32,1024]{1,0:T(8,128)(2,1)S(1)}, u32[]{:S(2)}, u32[]{:S(2)}) collective-permute-start(bf16[32,1024]{1,0:T(8,128)(2,1)S(1)} %get-tuple-element.35), channel_id=1, source_target_pairs={{112,240},{113,241},{114,242},{115,243},{116,244},{117,245},{118,2... | collective-permute-start | bytes 196616 | tf_op jit(solution)/shard_map/ppermute | solution.py:385
  5.8 6.5 %collective-permute-start.6 = (bf16[32,1024]{1,0:T(8,128)(2,1)S(1)}, bf16[32,1024]{1,0:T(8,128)(2,1)S(1)}, u32[]{:S(2)}, u32[]{:S(2)}) collective-permute-start(bf16[32,1024]{1,0:T(8,128)(2,1)S(1)} %get-tuple-element.36), channel_id=1, source_target_pairs={{112,224},{113,225},{114,226},{115,227},{116,228},{117,229},{118,2... | collective-permute-start | bytes 196616 | tf_op jit(solution)/shard_map/ppermute | solution.py:385
  7.1 6.5 %collective-permute-start.5 = (bf16[32,1024]{1,0:T(8,128)(2,1)S(1)}, bf16[32,1024]{1,0:T(8,128)(2,1)S(1)}, u32[]{:S(2)}, u32[]{:S(2)}) collective-permute-start(bf16[32,1024]{1,0:T(8,128)(2,1)S(1)} %get-tuple-element.30), channel_id=1, source_target_pairs={{112,208},{113,209},{114,210},{115,211},{116,212},{117,213},{118,2... | collective-permute-start | bytes 196616 | tf_op jit(solution)/shard_map/ppermute | solution.py:385
  8.4 6.5 %collective-permute-start.4 = (bf16[32,1024]{1,0:T(8,128)(2,1)S(1)}, bf16[32,1024]{1,0:T(8,128)(2,1)S(1)}, u32[]{:S(2)}, u32[]{:S(2)}) collective-permute-start(bf16[32,1024]{1,0:T(8,128)(2,1)S(1)} %get-tuple-element.31), channel_id=1, source_target_pairs={{112,192},{113,193},{114,194},{115,195},{116,196},{117,197},{118,1... | collective-permute-start | bytes 196616 | tf_op jit(solution)/shard_map/ppermute | solution.py:385
  9.7 5.2 %collective-permute-start.3 = (bf16[32,1024]{1,0:T(8,128)(2,1)S(1)}, bf16[32,1024]{1,0:T(8,128)(2,1)S(1)}, u32[]{:S(2)}, u32[]{:S(2)}) collective-permute-start(bf16[32,1024]{1,0:T(8,128)(2,1)S(1)} %get-tuple-element.32), channel_id=1, source_target_pairs={{112,176},{113,177},{114,178},{115,179},{116,180},{117,181},{118,1... | collective-permute-start | bytes 196616 | tf_op jit(solution)/shard_map/ppermute | solution.py:385
  11.0 3.9 %collective-permute-start.2 = (bf16[32,1024]{1,0:T(8,128)(2,1)S(1)}, bf16[32,1024]{1,0:T(8,128)(2,1)S(1)}, u32[]{:S(2)}, u32[]{:S(2)}) collective-permute-start(bf16[32,1024]{1,0:T(8,128)(2,1)S(1)} %get-tuple-element.33), channel_id=1, source_target_pairs={{112,160},{113,161},{114,162},{115,163},{116,164},{117,165},{118,1... | collective-permute-start | bytes 196616 | tf_op jit(solution)/shard_map/ppermute | solution.py:385
  12.3 3.9 %collective-permute-start = (bf16[32,1024]{1,0:T(8,128)(2,1)S(1)}, bf16[32,1024]{1,0:T(8,128)(2,1)S(1)}, u32[]{:S(2)}, u32[]{:S(2)}) collective-permute-start(bf16[32,1024]{1,0:T(8,128)(2,1)S(1)} %get-tuple-element.34), channel_id=1, source_target_pairs={{112,128},{113,129},{114,130},{115,131},{116,132},{117,133},{118,1... | collective-permute-start | bytes 196616 | tf_op jit(solution)/shard_map/ppermute | solution.py:385
  13.6 3.3 %collective-permute-start.1 = (bf16[32,1024]{1,0:T(8,128)(2,1)S(1)}, bf16[32,1024]{1,0:T(8,128)(2,1)S(1)}, u32[]{:S(2)}, u32[]{:S(2)}) collective-permute-start(bf16[32,1024]{1,0:T(8,128)(2,1)S(1)} %get-tuple-element.29), channel_id=1, source_target_pairs={{112,144},{113,145},{114,146},{115,147},{116,148},{117,149},{118,1... | collective-permute-start | bytes 196616 | tf_op jit(solution)/shard_map/ppermute | solution.py:385
  17.7 1.4 collective-permute-start.9
  48.6 7.7 %collective-permute-start.11 = (bf16[8,32,4096]{2,1,0:T(8,128)(2,1)S(1)}, bf16[8,32,4096]{2,1,0:T(8,128)(2,1)}, u32[]{:S(2)}, u32[]{:S(2)}) collective-permute-start(bf16[8,32,4096]{2,1,0:T(8,128)(2,1)S(1)} %all_to_all.15.x_ref), channel_id=1, source_target_pairs={{128,129},{129,128},{130,131},{131,130},{132,133},{133,132},{134,1... | collective-permute-start | bytes 6291464 | tf_op jit(solution)/shard_map/ppermute | solution.py:336
  61.0 26.1 %collective-permute-start.12 = (bf16[256,512]{1,0:T(8,128)(2,1)S(1)}, bf16[256,512]{1,0:T(8,128)(2,1)S(1)}, u32[]{:S(2)}, u32[]{:S(2)}) collective-permute-start(bf16[256,512]{1,0:T(8,128)(2,1)S(1)} %get-tuple-element.17), channel_id=1, source_target_pairs={{128,64},{129,65},{130,66},{131,67},{132,68},{133,69},{134,70},{13... | collective-permute-start | bytes 786440 | tf_op jit(solution)/shard_map/ppermute | solution.py:349
  62.3 27.1 %collective-permute-start.13 = (f32[256,512]{1,0:T(8,128)S(1)}, f32[256,512]{1,0:T(8,128)S(1)}, u32[]{:S(2)}, u32[]{:S(2)}) collective-permute-start(f32[256,512]{1,0:T(8,128)S(1)} %get-tuple-element.18), channel_id=1, source_target_pairs={{128,136},{129,137},{130,138},{131,139},{132,140},{133,141},{134,1... | collective-permute-start | bytes 1572872 | tf_op jit(solution)/shard_map/ppermute | solution.py:336
  87.0 13.8 %collective-permute-start.14 = (bf16[256,512]{1,0:T(8,128)(2,1)S(1)}, bf16[256,512]{1,0:T(8,128)(2,1)S(1)}, u32[]{:S(2)}, u32[]{:S(2)}) collective-permute-start(bf16[256,512]{1,0:T(8,128)(2,1)S(1)} %collective-permute-done.12.after_ref), channel_id=1, source_target_pairs={{64,136},{65,137},{66,138},{67,139},{68,140},{69,141},{70,142},{71... | collective-permute-start | bytes 786440 | tf_op jit(solution)/shard_map/ppermute | solution.py:353
  103.6 1.7 collective-permute-start.17
  104.5 13.3 %collective-permute-start.15 = (bf16[256,1024]{1,0:T(8,128)(2,1)S(1)}, bf16[256,1024]{1,0:T(8,128)(2,1)S(1)}, u32[]{:S(2)}, u32[]{:S(2)}) collective-permute-start(bf16[256,1024]{1,0:T(8,128)(2,1)S(1)} %get-tuple-element.26.g), channel_id=1, source_target_pairs={{128,136},{129,137},{130,138},{131,139},{132,140},{133,141},{134,1... | collective-permute-start | bytes 1572872 | tf_op jit(solution)/shard_map/ppermute | solution.py:336
  110.6 20.7 %all-to-all-start.1 = ((bf16[8,32,2048]{2,1,0:T(8,128)(2,1)}), bf16[8,32,2048]{2,1,0:T(8,128)(2,1)}, u32[]{:S(2)}, u32[]{:S(2)}) async-start(bf16[8,32,2048]{2,1,0:T(8,128)(2,1)} %shard_map.84), calls=%async_computation.1 | async-start | bytes 2097152 | tf_op jit(solution)/shard_map/all_to_all | solution.py:358
  131.3 18.6 %all-to-all-start.2 = ((bf16[8,32,2048]{2,1,0:T(8,128)(2,1)}), bf16[8,32,2048]{2,1,0:T(8,128)(2,1)S(1)}, u32[]{:S(2)}, u32[]{:S(2)}) async-start(bf16[8,32,2048]{2,1,0:T(8,128)(2,1)} %shard_map.83), calls=%async_computation.2 | async-start | bytes 2097152 | tf_op jit(solution)/shard_map/all_to_all | solution.py:358
  150.9 2.8 %collective-permute-start.21 = (bf16[32,1024]{1,0:T(8,128)(2,1)S(1)}, bf16[32,1024]{1,0:T(8,128)(2,1)S(1)}, u32[]{:S(2)}, u32[]{:S(2)}) collective-permute-start(bf16[32,1024]{1,0:T(8,128)(2,1)S(1)} %bitcast.57), channel_id=1, source_target_pairs={{128,138},{129,139},{130,136},{131,137},{132,130},{133,131},{134,1... | collective-permute-start | bytes 196616 | tf_op jit(solution)/shard_map/ppermute | solution.py:336
  151.6 2.1 collective-permute-start.20
  152.3 1.4 collective-permute-start.19
  154.4 53.5 %collective-permute-start.26 = (bf16[64,1024]{1,0:T(8,128)(2,1)S(1)}, bf16[64,1024]{1,0:T(8,128)(2,1)S(1)}, u32[]{:S(2)}, u32[]{:S(2)}) collective-permute-start(bf16[64,1024]{1,0:T(8,128)(2,1)S(1)} %pad_maximum_fusion.2), channel_id=1, source_target_pairs={{224,112},{225,113},{226,114},{227,115},{228,116},{229,117},{230,1... | collective-permute-start | bytes 393224 | tf_op jit(solution)/shard_map/ppermute | solution.py:448
  155.7 54.8 %collective-permute-start.25 = (bf16[64,1024]{1,0:T(8,128)(2,1)S(1)}, bf16[64,1024]{1,0:T(8,128)(2,1)S(1)}, u32[]{:S(2)}, u32[]{:S(2)}) collective-permute-start(bf16[64,1024]{1,0:T(8,128)(2,1)S(1)} %pad_maximum_fusion.2), channel_id=1, source_target_pairs={{192,112},{193,113},{194,114},{195,115},{196,116},{197,117},{198,1... | collective-permute-start | bytes 393224 | tf_op jit(solution)/shard_map/ppermute | solution.py:448
  157.0 53.5 %collective-permute-start.24 = (bf16[64,1024]{1,0:T(8,128)(2,1)S(1)}, bf16[64,1024]{1,0:T(8,128)(2,1)S(1)}, u32[]{:S(2)}, u32[]{:S(2)}) collective-permute-start(bf16[64,1024]{1,0:T(8,128)(2,1)S(1)} %pad_maximum_fusion.2), channel_id=1, source_target_pairs={{160,112},{161,113},{162,114},{163,115},{164,116},{165,117},{166,1... | collective-permute-start | bytes 393224 | tf_op jit(solution)/shard_map/ppermute | solution.py:448
  158.3 53.5 %collective-permute-start.23 = (bf16[64,1024]{1,0:T(8,128)(2,1)S(1)}, bf16[64,1024]{1,0:T(8,128)(2,1)S(1)}, u32[]{:S(2)}, u32[]{:S(2)}) collective-permute-start(bf16[64,1024]{1,0:T(8,128)(2,1)S(1)} %pad_maximum_fusion.2), channel_id=1, source_target_pairs={{128,112},{129,113},{130,114},{131,115},{132,116},{133,117},{134,1... | collective-permute-start | bytes 393224 | tf_op jit(solution)/shard_map/ppermute | solution.py:448
  (11 other events, 99.8 us)

commit v5 on v4

--- a/solution.py
+++ b/solution.py
@@ -251,37 +251,73 @@
     )(core, mine, key_weight, value_weight, packet)
 
 
-def back_product(core, mine, others, key_weight, value_weight, packet, block, count):
+def back_part(core, mine, key_weight, value_weight, block):
     tokens = mine.shape[0]
     cols = key_weight.shape[1]
-    width = 2 * block
     step = block // 2
-    steps = width // step
-    rows = tokens // count
-
-    def kernel(core_ref, g, h, wk, wv, far, out, held, low, in_sems, out_sems):
+    steps = 2 * block // step
+
+    def kernel(core_ref, g, wk, wv, out, held, sems):
         c = core_ref[0]
         loads = []
         for i in range(steps):
             at = pl.ds(pl.multiple_of(((i // 2 * 2 + c) * 2 + i % 2) * step, step), step)
-            sources = [wk.at[at], wv.at[at]]
-            sources += [far.at[pl.ds(n * width + i * step, step)] for n in range(2)]
             loads.append(
                 [
-                    pltpu.make_async_copy(source, held.at[i, n], in_sems.at[i, n])
-                    for n, source in enumerate(sources)
+                    pltpu.make_async_copy(w.at[at], held.at[i, n], sems.at[i, n])
+                    for n, w in enumerate((wk, wv))
                 ]
             )
         for group in loads:
             for load in group:
                 load.start()
+        for i in range(steps):
+            total = None
+            for n in range(2):
+                loads[i][n].wait()
+                term = dot(g[:, n * cols : (n + 1) * cols], held[i, n], NT)
+                total = term if total is None else total + term
+            out[i] = total
+
+    return pl.pallas_call(
+        kernel,
+        in_specs=scalar() + whole(1) + [pl.BlockSpec(memory_space=pl.ANY)] * 2,
+        out_specs=whole(1)[0],
+        out_shape=like((steps, tokens, step), F32),
+        scratch_shapes=[
+            pltpu.VMEM((steps, 2, step, cols), BF16),
+            pltpu.SemaphoreType.DMA((steps, 2)),
+        ],
+        cost_estimate=cost(),
+        compiler_params=pltpu.CompilerParams(vmem_limit_bytes=VMEM_BACK),
+    )(core, mine, key_weight, value_weight)
+
+
+def back_rest(part, others, packet, block, count):
+    steps, tokens, step = part.shape
+    cols = packet.shape[1]
+    width = 2 * block
+    rows = tokens // count
+
+    def kernel(p, h, far, out, held, low, in_sems, out_sems):
+        loads = [
+            [
+                pltpu.make_async_copy(
+                    far.at[pl.ds(n * width + i * step, step)], held.at[i, n], in_sems.at[i, n]
+                )
+                for n in range(2)
+            ]
+            for i in range(steps)
+        ]
+        for group in loads:
+            for load in group:
+                load.start()
         stores = []
         for i in range(steps):
-            total = None
-            for n, a in enumerate((g, g, h, h)):
+            total = p[i]
+            for n in range(2):
                 loads[i][n].wait()
-                term = dot(a[:, n % 2 * cols : (n % 2 + 1) * cols], held[i, n], NT)
-                total = term if total is None else total + term
+                total = total + dot(h[:, n * cols : (n + 1) * cols], held[i, n], NT)
             low[i] = total.reshape(count, rows, step).astype(BF16)
             store = pltpu.make_async_copy(
                 low.at[i], out.at[:, :, pl.ds(i * step, step)], out_sems.at[i]
@@ -293,18 +329,18 @@
 
     return pl.pallas_call(
         kernel,
-        in_specs=scalar() + whole(2) + [pl.BlockSpec(memory_space=pl.ANY)] * 3,
+        in_specs=whole(2) + [pl.BlockSpec(memory_space=pl.ANY)],
         out_specs=pl.BlockSpec(memory_space=pl.ANY),
         out_shape=like((count, rows, width), BF16),
         scratch_shapes=[
-            pltpu.VMEM((steps, 4, step, cols), BF16),
+            pltpu.VMEM((steps, 2, step, cols), BF16),
             pltpu.VMEM((steps, count, rows, step), BF16),
-            pltpu.SemaphoreType.DMA((steps, 4)),
+            pltpu.SemaphoreType.DMA((steps, 2)),
             pltpu.SemaphoreType.DMA((steps,)),
         ],
         cost_estimate=cost(),
         compiler_params=pltpu.CompilerParams(vmem_limit_bytes=VMEM_BACK),
-    )(core, mine, others, key_weight, value_weight, packet)
+    )(part, others, packet)
 
 
 def body(section_states, key_weight, value_weight, queries, cotangent):
@@ -415,9 +451,8 @@
     own_terms = exchange(
         back_product_near(core_index, grads, *weights, packet, block, count)
     )
-    other_term = back_product(
-        core_index, grads_in, swap_core(grads_in), *weights, packet, block, count
-    )
+    other_part = back_part(core_index, grads_in, *weights, block)
+    other_term = back_rest(other_part, swap_core(grads_in), packet, block, count)
     other_term, own_terms = lax.optimization_barrier((other_term, own_terms))
     own_total, other_total = (
         jnp.sum(terms.astype(F32), axis=0) for terms in (own_terms, exchange(other_term))
@@ -435,18 +470,18 @@
         summed = part if summed is None else summed + part
     summed = summed.astype(BF16)
     pairs = [
-        (place(first + k, d, t), place(first + k - 1, d, t)) for k, d, t in everyone if k % 2
+        (place(first + k, d, t), place(first + k - count // 2, d, t)) for k, d, t in everyone if k >= count // 2
     ]
     summed = jnp.concatenate([summed, lax.ppermute(summed, AXES, pairs)], axis=0)
     out = []
-    for k in range(0, count, 2):
+    for k in range(count // 2):
         pairs = [
             (place(first + k, d, t), place(root, d, t))
             for d in range(replicas)
             for t in range(lanes)
         ]
         out.append(lax.ppermute(summed, AXES, pairs))
-    encoder_grad = jnp.concatenate(out, axis=0)
+    encoder_grad = jnp.concatenate([o[:rows] for o in out] + [o[rows:] for o in out], axis=0)
     encoder_grad = jnp.where(section == root, encoder_grad, jnp.zeros_like(encoder_grad))
     return context[None, None], query_grad[None, None], encoder_grad[None, None]
 

time: 214 us -> 217 us (1.014)
    pallas_call x1 -> x2, Pallas kernels: 5.93 us -> 7.54 us  [the longest x1 4.25 us: back_rest(): pl.pallas_call(kernel, in_specs=whole(2) + [pl.BlockSpec(memory_space=pl....]
    unnamed x17 -> x24, local copies, waits for them, and re-layouts: 6.38 us -> 6.42 us
  transfers between devices with their start and end apart: 29 -> 29, of which waited for: 9 -> 8; matrix products, arithmetic and copies ran while one was open for 1% -> 1% of each run, Pallas kernels for 6% -> 7%
where the time goes in v5:
time: 217 us; the launch traced here: 215 us
  waiting for transfers between devices  108 us (50%)
  starting transfers between devices  44.4 us (20%)
  blocking collectives  29.1 us (13%)
  Pallas kernels  21 us (10%)
  local copies, waits for them, and re-layouts  8.59 us (4%)
  other arithmetic  2.5 us (1%)
    ppermute x4, waiting for transfers between devices, body(): out.append(lax.ppermute(summed, AXES, pairs))  51.7 us
    all_to_all x1, blocking collectives, exchange(): return lax.all_to_all(array, 'pipe', 0, 0, axis_index_groups=groups)  29.1 us
    ppermute x1, waiting for transfers between devices, lend(): return lax.ppermute(array, AXES, pairs)  26.1 us
    all_to_all x2, waiting for transfers between devices, exchange(): return lax.all_to_all(array, 'pipe', 0, 0, axis_index_groups=groups)  16.8 us
    all_to_all x2, starting transfers between devices, exchange(): return lax.all_to_all(array, 'pipe', 0, 0, axis_index_groups=groups)  12.6 us
    ppermute x8, starting transfers between devices, body(): part = lax.ppermute(piece[k * rows:(k + 1) * rows], AXES, pairs)  12.5 us
    ppermute x1, waiting for transfers between devices, swap_replica_lent(): return lax.ppermute(array, AXES, pairs)  10.9 us
    ppermute x12, starting transfers between devices, send(): return lax.ppermute(array, AXES, pairs)  9.9 us
  transfers between devices with their start and end apart: 29, of which 8 were waited for; matrix products, arithmetic and copies ran while one was open for 1% of the time, Pallas kernels for 7%

profile of v5, /device:TPU:122, one launch (start us, length us, event | category | flops | bytes accessed | tf_op | source)
XLA Modules:
  0.0 214.6 jit_solution(7278375433830821095)
XLA Ops:
  1.7 3.1 %collective-permute-start = (bf16[32,1024]{1,0:T(8,128)(2,1)S(1)}, bf16[32,1024]{1,0:T(8,128)(2,1)S(1)}, u32[]{:S(2)}, u32[]{:S(2)}) collective-permute-start(bf16[32,1024]{1,0:T(8,128)(2,1)S(1)} %get-tuple-element.34), channel_id=1, source_target_pairs={{112,128},{113,129},{114,130},{115,131},{116,132},{117,133},{118,1... | collective-permute-start | bytes 196616 | tf_op jit(solution)/shard_map/ppermute | solution.py:421
  4.8 1.7 collective-permute-start.1
  6.5 1.3 collective-permute-start.2
  7.8 1.3 collective-permute-start.3
  11.7 1.3 collective-permute-start.6
  18.9 29.1 %all_to_all.15.x_ref = bf16[8,32,4096]{2,1,0:T(8,128)(2,1)S(1)} all-to-all(bf16[8,32,4096]{2,1,0:T(8,128)(2,1)S(1)} %broadcast_in_dim.16), channel_id=1, replica_groups={{0,16,32,48,64,80,96,112},{128,144,160,176,192,208,224,240},{1,17,33,49..., dimensions={0} | all-to-all | bytes 4194304 | tf_op jit(solution)/shard_map/all_to_all | solution.py:394
  48.0 2.0 collective-permute-start.11
  50.0 2.2 %copy-done = bf16[1,4096,512]{2,1,0:T(8,128)(2,1)S(1)} copy-done((bf16[1,4096,512]{2,1,0:T(8,128)(2,1)S(1)}, bf16[1,4096,512]{2,1,0:T(8,128)(2,1)}, u32[]{:S(2)}) %copy-start) | copy-done | bytes 4194328
  56.6 3.8 %shard_map.78 = (f32[256,512]{1,0:T(8,128)S(1)}, bf16[256,512]{1,0:T(8,128)(2,1)S(1)}, f32[256,512]{1,0:T(8,128)S(1)}, f32[256,512]{1,0:T(8,128)S(1)}) custom-call(s32[1]{0:T(128)} %bitcast.1.same_ref, bf16[8,32,4096]{2,1,0:T(8,128)(2,1)} %collective-permute-done.11.far_ref, bf16[4096,512]{1,0:T(8,128)(2,1)S(1)} %bitcast.71, bf16[4096,512]{1,0:T(8,128)(2,1)S(1)} %bitcast.76, ...), custom_call_target="tpu_custom_call" | custom-call | flops 1 | bytes 1 | tf_op jit(solution)/shard_map/pallas_call | solution.py:99
  62.4 26.1 %collective-permute-done.12.after_ref = bf16[256,512]{1,0:T(8,128)(2,1)S(1)} collective-permute-done((bf16[256,512]{1,0:T(8,128)(2,1)S(1)}, bf16[256,512]{1,0:T(8,128)(2,1)S(1)}, u32[]{:S(2)}, u32[]{:S(2)}) %collective-permute-start.12) | collective-permute-done | bytes 262176 | tf_op jit(solution)/shard_map/ppermute | solution.py:385
  88.5 2.3 %collective-permute-start.14 = (bf16[256,512]{1,0:T(8,128)(2,1)S(1)}, bf16[256,512]{1,0:T(8,128)(2,1)S(1)}, u32[]{:S(2)}, u32[]{:S(2)}) collective-permute-start(bf16[256,512]{1,0:T(8,128)(2,1)S(1)} %collective-permute-done.12.after_ref), channel_id=1, source_target_pairs={{64,136},{65,137},{66,138},{67,139},{68,140},{69,141},{70,142},{71... | collective-permute-start | bytes 786440 | tf_op jit(solution)/shard_map/ppermute | solution.py:389
  90.9 10.9 %collective-permute-done.14.vb = bf16[256,512]{1,0:T(8,128)(2,1)S(1)} collective-permute-done((bf16[256,512]{1,0:T(8,128)(2,1)S(1)}, bf16[256,512]{1,0:T(8,128)(2,1)S(1)}, u32[]{:S(2)}, u32[]{:S(2)}) %collective-permute-start.14) | collective-permute-done | bytes 262176 | tf_op jit(solution)/shard_map/ppermute | solution.py:389
  101.8 2.4 %shard_map.80 = (bf16[256,512]{1,0:T(8,128)(2,1)S(1)}, bf16[256,512]{1,0:T(8,128)(2,1)S(1)}, bf16[4,256,256]{2,1,0:T(8,128)(2,1)S(1)}, bf16[4,256,256]{2,1,0:T(8,128)(2,1)S(1)}, bf16[256,1024]{1,0:T(8,128)(2,1)S(1)}) custom-call(f32[256,512]{1,0:T(8,128)S(1)} %shard_map.79.ka, f32[256,512]{1,0:T(8,128)S(1)} %collective-permute-done.13.kb, ...), custom_call_target="tpu_custom_call" | custom-call | flops 1 | bytes 1 | tf_op jit(solution)/shard_map/pallas_call | solution.py:176
  106.2 3.2 %shard_map.85 = bf16[8,32,2048]{2,1,0:T(8,128)(2,1)} custom-call(s32[1]{0:T(128)} %bitcast.16.core_ref, bf16[256,1024]{1,0:T(8,128)(2,1)S(1)} %get-tuple-element.26.g, bf16[4096,512]{1,0:T(8,128)(2,1)S(1)} %bitcast.73, bf16[4096,512]{1,0:T(8,128)(2,1)S(1)} %bitcast.78, bf16[4608,512]{1,0:T(8,128)(2,1)S(1)} %collective-permute-done.17.far), custom_call_target="tpu_custom_call" | custom-call | flops 1 | bytes 1 | tf_op jit(solution)/shard_map/pallas_call | solution.py:240
  109.4 2.1 copy-done.3
  111.6 7.2 %all-to-all-start.1 = ((bf16[8,32,2048]{2,1,0:T(8,128)(2,1)}), bf16[8,32,2048]{2,1,0:T(8,128)(2,1)}, u32[]{:S(2)}, u32[]{:S(2)}) async-start(bf16[8,32,2048]{2,1,0:T(8,128)(2,1)} %shard_map.85), calls=%async_computation.1 | async-start | bytes 2097152 | tf_op jit(solution)/shard_map/all_to_all | solution.py:394
  119.7 3.3 %shard_map.82.p = f32[4,256,512]{2,1,0:T(8,128)S(1)} custom-call(s32[1]{0:T(128)} %bitcast.16.core_ref, bf16[256,1024]{1,0:T(8,128)(2,1)S(1)} %collective-permute-done.15.g, bf16[4096,512]{1,0:T(8,128)(2,1)} %bitcast.69, bf16[4096,512]{1,0:T(8,128)(2,1)} %bitcast.74), custom_call_target="tpu_custom_call" | custom-call | flops 1 | bytes 1 | tf_op jit(solution)/shard_map/pallas_call | solution.py:282
  123.0 4.3 %shard_map.84 = bf16[8,32,2048]{2,1,0:T(8,128)(2,1)} custom-call(f32[4,256,512]{2,1,0:T(8,128)S(1)} %shard_map.82.p, bf16[256,1024]{1,0:T(8,128)(2,1)S(1)} %collective-permute-done.16.h, bf16[4608,512]{1,0:T(8,128)(2,1)} %copy-done.3), custom_call_target="tpu_custom_call" | custom-call | flops 1 | bytes 1 | tf_op jit(solution)/shard_map/pallas_call | solution.py:330
  127.2 5.1 %all-to-all-done.1 = bf16[8,32,2048]{2,1,0:T(8,128)(2,1)} async-done(((bf16[8,32,2048]{2,1,0:T(8,128)(2,1)}), bf16[8,32,2048]{2,1,0:T(8,128)(2,1)}, u32[]{:S(2)}, u32[]{:S(2)}) %all-to-all-start.1) | async-done | bytes 1048608 | tf_op jit(solution)/shard_map/all_to_all | solution.py:394
  132.4 5.4 %all-to-all-start.2 = ((bf16[8,32,2048]{2,1,0:T(8,128)(2,1)}), bf16[8,32,2048]{2,1,0:T(8,128)(2,1)S(1)}, u32[]{:S(2)}, u32[]{:S(2)}) async-start(bf16[8,32,2048]{2,1,0:T(8,128)(2,1)} %shard_map.84), calls=%async_computation.2 | async-start | bytes 2097152 | tf_op jit(solution)/shard_map/all_to_all | solution.py:394
  137.8 1.4 convert_reduce_fusion.1
  139.3 11.7 %all-to-all-done.2 = bf16[8,32,2048]{2,1,0:T(8,128)(2,1)S(1)} async-done(((bf16[8,32,2048]{2,1,0:T(8,128)(2,1)}), bf16[8,32,2048]{2,1,0:T(8,128)(2,1)S(1)}, u32[]{:S(2)}, u32[]{:S(2)}) %all-to-all-start.2) | async-done | bytes 1048608 | tf_op jit(solution)/shard_map/all_to_all | solution.py:394
  161.9 50.3 %collective-permute-done.23 = bf16[64,1024]{1,0:T(8,128)(2,1)S(1)} collective-permute-done((bf16[64,1024]{1,0:T(8,128)(2,1)S(1)}, bf16[64,1024]{1,0:T(8,128)(2,1)S(1)}, u32[]{:S(2)}, u32[]{:S(2)}) %collective-permute-start.23) | collective-permute-done | bytes 131104 | tf_op jit(solution)/shard_map/ppermute | solution.py:483
  212.2 1.4 collective-permute-done.24
  (86 shorter events, 30.4 us)
Async XLA Ops:
  1.7 8.7 %collective-permute-start = (bf16[32,1024]{1,0:T(8,128)(2,1)S(1)}, bf16[32,1024]{1,0:T(8,128)(2,1)S(1)}, u32[]{:S(2)}, u32[]{:S(2)}) collective-permute-start(bf16[32,1024]{1,0:T(8,128)(2,1)S(1)} %get-tuple-element.34), channel_id=1, source_target_pairs={{112,128},{113,129},{114,130},{115,131},{116,132},{117,133},{118,1... | collective-permute-start | bytes 196616 | tf_op jit(solution)/shard_map/ppermute | solution.py:421
  4.8 6.9 %collective-permute-start.1 = (bf16[32,1024]{1,0:T(8,128)(2,1)S(1)}, bf16[32,1024]{1,0:T(8,128)(2,1)S(1)}, u32[]{:S(2)}, u32[]{:S(2)}) collective-permute-start(bf16[32,1024]{1,0:T(8,128)(2,1)S(1)} %get-tuple-element.29), channel_id=1, source_target_pairs={{112,144},{113,145},{114,146},{115,147},{116,148},{117,149},{118,1... | collective-permute-start | bytes 196616 | tf_op jit(solution)/shard_map/ppermute | solution.py:421
  6.5 6.5 %collective-permute-start.2 = (bf16[32,1024]{1,0:T(8,128)(2,1)S(1)}, bf16[32,1024]{1,0:T(8,128)(2,1)S(1)}, u32[]{:S(2)}, u32[]{:S(2)}) collective-permute-start(bf16[32,1024]{1,0:T(8,128)(2,1)S(1)} %get-tuple-element.33), channel_id=1, source_target_pairs={{112,160},{113,161},{114,162},{115,163},{116,164},{117,165},{118,1... | collective-permute-start | bytes 196616 | tf_op jit(solution)/shard_map/ppermute | solution.py:421
  7.8 6.5 %collective-permute-start.3 = (bf16[32,1024]{1,0:T(8,128)(2,1)S(1)}, bf16[32,1024]{1,0:T(8,128)(2,1)S(1)}, u32[]{:S(2)}, u32[]{:S(2)}) collective-permute-start(bf16[32,1024]{1,0:T(8,128)(2,1)S(1)} %get-tuple-element.32), channel_id=1, source_target_pairs={{112,176},{113,177},{114,178},{115,179},{116,180},{117,181},{118,1... | collective-permute-start | bytes 196616 | tf_op jit(solution)/shard_map/ppermute | solution.py:421
  9.1 5.2 %collective-permute-start.4 = (bf16[32,1024]{1,0:T(8,128)(2,1)S(1)}, bf16[32,1024]{1,0:T(8,128)(2,1)S(1)}, u32[]{:S(2)}, u32[]{:S(2)}) collective-permute-start(bf16[32,1024]{1,0:T(8,128)(2,1)S(1)} %get-tuple-element.31), channel_id=1, source_target_pairs={{112,192},{113,193},{114,194},{115,195},{116,196},{117,197},{118,1... | collective-permute-start | bytes 196616 | tf_op jit(solution)/shard_map/ppermute | solution.py:421
  10.4 3.9 %collective-permute-start.5 = (bf16[32,1024]{1,0:T(8,128)(2,1)S(1)}, bf16[32,1024]{1,0:T(8,128)(2,1)S(1)}, u32[]{:S(2)}, u32[]{:S(2)}) collective-permute-start(bf16[32,1024]{1,0:T(8,128)(2,1)S(1)} %get-tuple-element.30), channel_id=1, source_target_pairs={{112,208},{113,209},{114,210},{115,211},{116,212},{117,213},{118,2... | collective-permute-start | bytes 196616 | tf_op jit(solution)/shard_map/ppermute | solution.py:421
  11.7 3.9 %collective-permute-start.6 = (bf16[32,1024]{1,0:T(8,128)(2,1)S(1)}, bf16[32,1024]{1,0:T(8,128)(2,1)S(1)}, u32[]{:S(2)}, u32[]{:S(2)}) collective-permute-start(bf16[32,1024]{1,0:T(8,128)(2,1)S(1)} %get-tuple-element.36), channel_id=1, source_target_pairs={{112,224},{113,225},{114,226},{115,227},{116,228},{117,229},{118,2... | collective-permute-start | bytes 196616 | tf_op jit(solution)/shard_map/ppermute | solution.py:421
  13.0 3.3 %collective-permute-start.7 = (bf16[32,1024]{1,0:T(8,128)(2,1)S(1)}, bf16[32,1024]{1,0:T(8,128)(2,1)S(1)}, u32[]{:S(2)}, u32[]{:S(2)}) collective-permute-start(bf16[32,1024]{1,0:T(8,128)(2,1)S(1)} %get-tuple-element.35), channel_id=1, source_target_pairs={{112,240},{113,241},{114,242},{115,243},{116,244},{117,245},{118,2... | collective-permute-start | bytes 196616 | tf_op jit(solution)/shard_map/ppermute | solution.py:421
  48.0 7.7 %collective-permute-start.11 = (bf16[8,32,4096]{2,1,0:T(8,128)(2,1)S(1)}, bf16[8,32,4096]{2,1,0:T(8,128)(2,1)}, u32[]{:S(2)}, u32[]{:S(2)}) collective-permute-start(bf16[8,32,4096]{2,1,0:T(8,128)(2,1)S(1)} %all_to_all.15.x_ref), channel_id=1, source_target_pairs={{128,129},{129,128},{130,131},{131,130},{132,133},{133,132},{134,1... | collective-permute-start | bytes 6291464 | tf_op jit(solution)/shard_map/ppermute | solution.py:372
  60.4 28.2 %collective-permute-start.12 = (bf16[256,512]{1,0:T(8,128)(2,1)S(1)}, bf16[256,512]{1,0:T(8,128)(2,1)S(1)}, u32[]{:S(2)}, u32[]{:S(2)}) collective-permute-start(bf16[256,512]{1,0:T(8,128)(2,1)S(1)} %get-tuple-element.17), channel_id=1, source_target_pairs={{128,64},{129,65},{130,66},{131,67},{132,68},{133,69},{134,70},{13... | collective-permute-start | bytes 786440 | tf_op jit(solution)/shard_map/ppermute | solution.py:385
  61.7 29.2 %collective-permute-start.13 = (f32[256,512]{1,0:T(8,128)S(1)}, f32[256,512]{1,0:T(8,128)S(1)}, u32[]{:S(2)}, u32[]{:S(2)}) collective-permute-start(f32[256,512]{1,0:T(8,128)S(1)} %get-tuple-element.18), channel_id=1, source_target_pairs={{128,136},{129,137},{130,138},{131,139},{132,140},{133,141},{134,1... | collective-permute-start | bytes 1572872 | tf_op jit(solution)/shard_map/ppermute | solution.py:372
  88.5 13.3 %collective-permute-start.14 = (bf16[256,512]{1,0:T(8,128)(2,1)S(1)}, bf16[256,512]{1,0:T(8,128)(2,1)S(1)}, u32[]{:S(2)}, u32[]{:S(2)}) collective-permute-start(bf16[256,512]{1,0:T(8,128)(2,1)S(1)} %collective-permute-done.12.after_ref), channel_id=1, source_target_pairs={{64,136},{65,137},{66,138},{67,139},{68,140},{69,141},{70,142},{71... | collective-permute-start | bytes 786440 | tf_op jit(solution)/shard_map/ppermute | solution.py:389
  104.5 1.7 collective-permute-start.17
  105.5 13.3 %collective-permute-start.15 = (bf16[256,1024]{1,0:T(8,128)(2,1)S(1)}, bf16[256,1024]{1,0:T(8,128)(2,1)S(1)}, u32[]{:S(2)}, u32[]{:S(2)}) collective-permute-start(bf16[256,1024]{1,0:T(8,128)(2,1)S(1)} %get-tuple-element.26.g), channel_id=1, source_target_pairs={{128,136},{129,137},{130,138},{131,139},{132,140},{133,141},{134,1... | collective-permute-start | bytes 1572872 | tf_op jit(solution)/shard_map/ppermute | solution.py:372
  111.6 20.8 %all-to-all-start.1 = ((bf16[8,32,2048]{2,1,0:T(8,128)(2,1)}), bf16[8,32,2048]{2,1,0:T(8,128)(2,1)}, u32[]{:S(2)}, u32[]{:S(2)}) async-start(bf16[8,32,2048]{2,1,0:T(8,128)(2,1)} %shard_map.85), calls=%async_computation.1 | async-start | bytes 2097152 | tf_op jit(solution)/shard_map/all_to_all | solution.py:394
  118.8 4.2 %collective-permute-start.16 = (bf16[256,1024]{1,0:T(8,128)(2,1)S(1)}, bf16[256,1024]{1,0:T(8,128)(2,1)S(1)}, u32[]{:S(2)}, u32[]{:S(2)}) collective-permute-start(bf16[256,1024]{1,0:T(8,128)(2,1)S(1)} %collective-permute-done.15.g), channel_id=1, source_target_pairs={{128,129},{129,128},{130,131},{131,130},{132,133},{133,132},{134,1... | collective-permute-start | bytes 1572872 | tf_op jit(solution)/shard_map/ppermute | solution.py:372
  132.4 18.6 %all-to-all-start.2 = ((bf16[8,32,2048]{2,1,0:T(8,128)(2,1)}), bf16[8,32,2048]{2,1,0:T(8,128)(2,1)S(1)}, u32[]{:S(2)}, u32[]{:S(2)}) async-start(bf16[8,32,2048]{2,1,0:T(8,128)(2,1)} %shard_map.84), calls=%async_computation.2 | async-start | bytes 2097152 | tf_op jit(solution)/shard_map/all_to_all | solution.py:394
  151.9 2.8 %collective-permute-start.18 = (bf16[32,1024]{1,0:T(8,128)(2,1)S(1)}, bf16[32,1024]{1,0:T(8,128)(2,1)S(1)}, u32[]{:S(2)}, u32[]{:S(2)}) collective-permute-start(bf16[32,1024]{1,0:T(8,128)(2,1)S(1)} %bitcast.81), channel_id=1, source_target_pairs={{128,128},{129,129},{130,130},{131,131},{132,136},{133,137},{134,1... | collective-permute-start | bytes 196616 | tf_op jit(solution)/shard_map/ppermute | solution.py:372
  152.6 2.1 collective-permute-start.19
  153.4 1.4 collective-permute-start.20
  155.5 56.7 %collective-permute-start.23 = (bf16[64,1024]{1,0:T(8,128)(2,1)S(1)}, bf16[64,1024]{1,0:T(8,128)(2,1)S(1)}, u32[]{:S(2)}, u32[]{:S(2)}) collective-permute-start(bf16[64,1024]{1,0:T(8,128)(2,1)S(1)} %pad_maximum_fusion.2), channel_id=1, source_target_pairs={{128,112},{129,113},{130,114},{131,115},{132,116},{133,117},{134,1... | collective-permute-start | bytes 393224 | tf_op jit(solution)/shard_map/ppermute | solution.py:483
  158.0 55.6 %collective-permute-start.24 = (bf16[64,1024]{1,0:T(8,128)(2,1)S(1)}, bf16[64,1024]{1,0:T(8,128)(2,1)S(1)}, u32[]{:S(2)}, u32[]{:S(2)}) collective-permute-start(bf16[64,1024]{1,0:T(8,128)(2,1)S(1)} %pad_maximum_fusion.2), channel_id=1, source_target_pairs={{144,112},{145,113},{146,114},{147,115},{148,116},{149,117},{150,1... | collective-permute-start | bytes 393224 | tf_op jit(solution)/shard_map/ppermute | solution.py:483
  159.3 54.3 %collective-permute-start.25 = (bf16[64,1024]{1,0:T(8,128)(2,1)S(1)}, bf16[64,1024]{1,0:T(8,128)(2,1)S(1)}, u32[]{:S(2)}, u32[]{:S(2)}) collective-permute-start(bf16[64,1024]{1,0:T(8,128)(2,1)S(1)} %pad_maximum_fusion.2), channel_id=1, source_target_pairs={{160,112},{161,113},{162,114},{163,115},{164,116},{165,117},{166,1... | collective-permute-start | bytes 393224 | tf_op jit(solution)/shard_map/ppermute | solution.py:483
  160.6 53.0 %collective-permute-start.26 = (bf16[64,1024]{1,0:T(8,128)(2,1)S(1)}, bf16[64,1024]{1,0:T(8,128)(2,1)S(1)}, u32[]{:S(2)}, u32[]{:S(2)}) collective-permute-start(bf16[64,1024]{1,0:T(8,128)(2,1)S(1)} %pad_maximum_fusion.2), channel_id=1, source_target_pairs={{176,112},{177,113},{178,114},{179,115},{180,116},{181,117},{182,1... | collective-permute-start | bytes 393224 | tf_op jit(solution)/shard_map/ppermute | solution.py:483
  (11 other events, 103.4 us)

commit v6 on v4

--- a/solution.py
+++ b/solution.py
@@ -435,18 +435,18 @@
         summed = part if summed is None else summed + part
     summed = summed.astype(BF16)
     pairs = [
-        (place(first + k, d, t), place(first + k - 1, d, t)) for k, d, t in everyone if k % 2
+        (place(first + k, d, t), place(first + k - count // 2, d, t)) for k, d, t in everyone if k >= count // 2
     ]
     summed = jnp.concatenate([summed, lax.ppermute(summed, AXES, pairs)], axis=0)
     out = []
-    for k in range(0, count, 2):
+    for k in range(count // 2):
         pairs = [
             (place(first + k, d, t), place(root, d, t))
             for d in range(replicas)
             for t in range(lanes)
         ]
         out.append(lax.ppermute(summed, AXES, pairs))
-    encoder_grad = jnp.concatenate(out, axis=0)
+    encoder_grad = jnp.concatenate([o[:rows] for o in out] + [o[rows:] for o in out], axis=0)
     encoder_grad = jnp.where(section == root, encoder_grad, jnp.zeros_like(encoder_grad))
     return context[None, None], query_grad[None, None], encoder_grad[None, None]
 

time: 214 us -> 213 us (level)
    unnamed x17 -> x24, local copies, waits for them, and re-layouts: 6.38 us -> 6.42 us
where the time goes in v6:
time: 213 us; the launch traced here: 212 us
  waiting for transfers between devices  106 us (50%)
  starting transfers between devices  45.1 us (21%)
  blocking collectives  29.1 us (14%)
  Pallas kernels  19.3 us (9%)
  local copies, waits for them, and re-layouts  8.59 us (4%)
  other arithmetic  2.5 us (1%)
    ppermute x4, waiting for transfers between devices, body(): out.append(lax.ppermute(summed, AXES, pairs))  50.4 us
    all_to_all x1, blocking collectives, exchange(): return lax.all_to_all(array, 'pipe', 0, 0, axis_index_groups=groups)  29.1 us
    ppermute x1, waiting for transfers between devices, lend(): return lax.ppermute(array, AXES, pairs)  24.1 us
    all_to_all x2, waiting for transfers between devices, exchange(): return lax.all_to_all(array, 'pipe', 0, 0, axis_index_groups=groups)  18.3 us
    ppermute x8, starting transfers between devices, body(): part = lax.ppermute(piece[k * rows:(k + 1) * rows], AXES, pairs)  13.1 us
    all_to_all x2, starting transfers between devices, exchange(): return lax.all_to_all(array, 'pipe', 0, 0, axis_index_groups=groups)  12.7 us
    ppermute x1, waiting for transfers between devices, swap_replica_lent(): return lax.ppermute(array, AXES, pairs)  11.5 us
    ppermute x12, starting transfers between devices, send(): return lax.ppermute(array, AXES, pairs)  9.9 us
  transfers between devices with their start and end apart: 29, of which 9 were waited for; matrix products, arithmetic and copies ran while one was open for 1% of the time, Pallas kernels for 6%

profile of v6, /device:TPU:122, one launch (start us, length us, event | category | flops | bytes accessed | tf_op | source)
XLA Modules:
  0.0 212.1 jit_solution(15080320494046393864)
XLA Ops:
  1.7 4.0 %collective-permute-start.7 = (bf16[32,1024]{1,0:T(8,128)(2,1)S(1)}, bf16[32,1024]{1,0:T(8,128)(2,1)S(1)}, u32[]{:S(2)}, u32[]{:S(2)}) collective-permute-start(bf16[32,1024]{1,0:T(8,128)(2,1)S(1)} %get-tuple-element.35), channel_id=1, source_target_pairs={{112,240},{113,241},{114,242},{115,243},{116,244},{117,245},{118,2... | collective-permute-start | bytes 196616 | tf_op jit(solution)/shard_map/ppermute | solution.py:385
  5.8 1.3 collective-permute-start.6
  7.1 1.3 collective-permute-start.5
  9.7 1.3 collective-permute-start.3
  11.0 1.3 collective-permute-start.2
  12.3 1.3 collective-permute-start
  19.4 29.1 %all_to_all.15.x_ref = bf16[8,32,4096]{2,1,0:T(8,128)(2,1)S(1)} all-to-all(bf16[8,32,4096]{2,1,0:T(8,128)(2,1)S(1)} %broadcast_in_dim.16), channel_id=1, replica_groups={{0,16,32,48,64,80,96,112},{128,144,160,176,192,208,224,240},{1,17,33,49..., dimensions={0} | all-to-all | bytes 4194304 | tf_op jit(solution)/shard_map/all_to_all | solution.py:358
  48.6 2.0 collective-permute-start.11
  50.6 2.2 %copy-done = bf16[1,4096,512]{2,1,0:T(8,128)(2,1)S(1)} copy-done((bf16[1,4096,512]{2,1,0:T(8,128)(2,1)S(1)}, bf16[1,4096,512]{2,1,0:T(8,128)(2,1)}, u32[]{:S(2)}) %copy-start) | copy-done | bytes 4194328
  57.2 3.8 %shard_map.78 = (f32[256,512]{1,0:T(8,128)S(1)}, bf16[256,512]{1,0:T(8,128)(2,1)S(1)}, f32[256,512]{1,0:T(8,128)S(1)}, f32[256,512]{1,0:T(8,128)S(1)}) custom-call(s32[1]{0:T(128)} %bitcast.1.same_ref, bf16[8,32,4096]{2,1,0:T(8,128)(2,1)} %collective-permute-done.11.far_ref, bf16[4096,512]{1,0:T(8,128)(2,1)S(1)} %bitcast.71, bf16[4096,512]{1,0:T(8,128)(2,1)S(1)} %bitcast.76, ...), custom_call_target="tpu_custom_call" | custom-call | flops 1 | bytes 1 | tf_op jit(solution)/shard_map/pallas_call | solution.py:99
  63.0 24.1 %collective-permute-done.12.after_ref = bf16[256,512]{1,0:T(8,128)(2,1)S(1)} collective-permute-done((bf16[256,512]{1,0:T(8,128)(2,1)S(1)}, bf16[256,512]{1,0:T(8,128)(2,1)S(1)}, u32[]{:S(2)}, u32[]{:S(2)}) %collective-permute-start.12) | collective-permute-done | bytes 262176 | tf_op jit(solution)/shard_map/ppermute | solution.py:349
  87.0 2.3 %collective-permute-start.14 = (bf16[256,512]{1,0:T(8,128)(2,1)S(1)}, bf16[256,512]{1,0:T(8,128)(2,1)S(1)}, u32[]{:S(2)}, u32[]{:S(2)}) collective-permute-start(bf16[256,512]{1,0:T(8,128)(2,1)S(1)} %collective-permute-done.12.after_ref), channel_id=1, source_target_pairs={{64,136},{65,137},{66,138},{67,139},{68,140},{69,141},{70,142},{71... | collective-permute-start | bytes 786440 | tf_op jit(solution)/shard_map/ppermute | solution.py:353
  89.4 11.5 %collective-permute-done.14.vb = bf16[256,512]{1,0:T(8,128)(2,1)S(1)} collective-permute-done((bf16[256,512]{1,0:T(8,128)(2,1)S(1)}, bf16[256,512]{1,0:T(8,128)(2,1)S(1)}, u32[]{:S(2)}, u32[]{:S(2)}) %collective-permute-start.14) | collective-permute-done | bytes 262176 | tf_op jit(solution)/shard_map/ppermute | solution.py:353
  100.9 2.4 %shard_map.80 = (bf16[256,512]{1,0:T(8,128)(2,1)S(1)}, bf16[256,512]{1,0:T(8,128)(2,1)S(1)}, bf16[4,256,256]{2,1,0:T(8,128)(2,1)S(1)}, bf16[4,256,256]{2,1,0:T(8,128)(2,1)S(1)}, bf16[256,1024]{1,0:T(8,128)(2,1)S(1)}) custom-call(f32[256,512]{1,0:T(8,128)S(1)} %shard_map.79.ka, f32[256,512]{1,0:T(8,128)S(1)} %collective-permute-done.13.kb, ...), custom_call_target="tpu_custom_call" | custom-call | flops 1 | bytes 1 | tf_op jit(solution)/shard_map/pallas_call | solution.py:176
  105.2 3.2 %shard_map.84 = bf16[8,32,2048]{2,1,0:T(8,128)(2,1)} custom-call(s32[1]{0:T(128)} %bitcast.16.core_ref, bf16[256,1024]{1,0:T(8,128)(2,1)S(1)} %get-tuple-element.26.g, bf16[4096,512]{1,0:T(8,128)(2,1)S(1)} %bitcast.73, bf16[4096,512]{1,0:T(8,128)(2,1)S(1)} %bitcast.78, bf16[4608,512]{1,0:T(8,128)(2,1)S(1)} %collective-permute-done.17.far), custom_call_target="tpu_custom_call" | custom-call | flops 1 | bytes 1 | tf_op jit(solution)/shard_map/pallas_call | solution.py:240
  108.5 2.1 %copy-done.3 = bf16[4608,512]{1,0:T(8,128)(2,1)} copy-done((bf16[4608,512]{1,0:T(8,128)(2,1)}, bf16[4608,512]{1,0:T(8,128)(2,1)S(1)}, u32[]{:S(2)}) %copy-start.3) | copy-done | bytes 4718616
  110.6 7.3 %all-to-all-start.1 = ((bf16[8,32,2048]{2,1,0:T(8,128)(2,1)}), bf16[8,32,2048]{2,1,0:T(8,128)(2,1)}, u32[]{:S(2)}, u32[]{:S(2)}) async-start(bf16[8,32,2048]{2,1,0:T(8,128)(2,1)} %shard_map.84), calls=%async_computation.1 | async-start | bytes 2097152 | tf_op jit(solution)/shard_map/all_to_all | solution.py:358
  118.7 5.9 %shard_map.83 = bf16[8,32,2048]{2,1,0:T(8,128)(2,1)} custom-call(s32[1]{0:T(128)} %bitcast.16.core_ref, bf16[256,1024]{1,0:T(8,128)(2,1)S(1)} %collective-permute-done.15.g, bf16[256,1024]{1,0:T(8,128)(2,1)S(1)} %collective-permute-done.16.h, bf16[4096,512]{1,0:T(8,128)(2,1)} %bitcast.69, bf16[4096,512]{1,0:T(8,128)(2,1)} %bitcast.74, ...), custom_call_target="tpu_custom_call" | custom-call | flops 1 | bytes 1 | tf_op jit(solution)/shard_map/pallas_call | solution.py:294
  124.7 6.6 %all-to-all-done.1 = bf16[8,32,2048]{2,1,0:T(8,128)(2,1)} async-done(((bf16[8,32,2048]{2,1,0:T(8,128)(2,1)}), bf16[8,32,2048]{2,1,0:T(8,128)(2,1)}, u32[]{:S(2)}, u32[]{:S(2)}) %all-to-all-start.1) | async-done | bytes 1048608 | tf_op jit(solution)/shard_map/all_to_all | solution.py:358
  131.3 5.4 %all-to-all-start.2 = ((bf16[8,32,2048]{2,1,0:T(8,128)(2,1)}), bf16[8,32,2048]{2,1,0:T(8,128)(2,1)S(1)}, u32[]{:S(2)}, u32[]{:S(2)}) async-start(bf16[8,32,2048]{2,1,0:T(8,128)(2,1)} %shard_map.83), calls=%async_computation.2 | async-start | bytes 2097152 | tf_op jit(solution)/shard_map/all_to_all | solution.py:358
  136.7 1.4 convert_reduce_fusion.1
  138.3 11.6 %all-to-all-done.2 = bf16[8,32,2048]{2,1,0:T(8,128)(2,1)S(1)} async-done(((bf16[8,32,2048]{2,1,0:T(8,128)(2,1)}), bf16[8,32,2048]{2,1,0:T(8,128)(2,1)S(1)}, u32[]{:S(2)}, u32[]{:S(2)}) %all-to-all-start.2) | async-done | bytes 1048608 | tf_op jit(solution)/shard_map/all_to_all | solution.py:358
  160.8 48.0 %collective-permute-done.23 = bf16[64,1024]{1,0:T(8,128)(2,1)S(1)} collective-permute-done((bf16[64,1024]{1,0:T(8,128)(2,1)S(1)}, bf16[64,1024]{1,0:T(8,128)(2,1)S(1)}, u32[]{:S(2)}, u32[]{:S(2)}) %collective-permute-start.23) | collective-permute-done | bytes 131104 | tf_op jit(solution)/shard_map/ppermute | solution.py:448
  208.8 2.2 %collective-permute-done.24 = bf16[64,1024]{1,0:T(8,128)(2,1)S(1)} collective-permute-done((bf16[64,1024]{1,0:T(8,128)(2,1)S(1)}, bf16[64,1024]{1,0:T(8,128)(2,1)S(1)}, u32[]{:S(2)}, u32[]{:S(2)}) %collective-permute-start.24) | collective-permute-done | bytes 131104 | tf_op jit(solution)/shard_map/ppermute | solution.py:448
  (85 shorter events, 29.3 us)
Async XLA Ops:
  1.7 9.2 %collective-permute-start.7 = (bf16[32,1024]{1,0:T(8,128)(2,1)S(1)}, bf16[32,1024]{1,0:T(8,128)(2,1)S(1)}, u32[]{:S(2)}, u32[]{:S(2)}) collective-permute-start(bf16[32,1024]{1,0:T(8,128)(2,1)S(1)} %get-tuple-element.35), channel_id=1, source_target_pairs={{112,240},{113,241},{114,242},{115,243},{116,244},{117,245},{118,2... | collective-permute-start | bytes 196616 | tf_op jit(solution)/shard_map/ppermute | solution.py:385
  5.8 6.5 %collective-permute-start.6 = (bf16[32,1024]{1,0:T(8,128)(2,1)S(1)}, bf16[32,1024]{1,0:T(8,128)(2,1)S(1)}, u32[]{:S(2)}, u32[]{:S(2)}) collective-permute-start(bf16[32,1024]{1,0:T(8,128)(2,1)S(1)} %get-tuple-element.36), channel_id=1, source_target_pairs={{112,224},{113,225},{114,226},{115,227},{116,228},{117,229},{118,2... | collective-permute-start | bytes 196616 | tf_op jit(solution)/shard_map/ppermute | solution.py:385
  7.1 6.5 %collective-permute-start.5 = (bf16[32,1024]{1,0:T(8,128)(2,1)S(1)}, bf16[32,1024]{1,0:T(8,128)(2,1)S(1)}, u32[]{:S(2)}, u32[]{:S(2)}) collective-permute-start(bf16[32,1024]{1,0:T(8,128)(2,1)S(1)} %get-tuple-element.30), channel_id=1, source_target_pairs={{112,208},{113,209},{114,210},{115,211},{116,212},{117,213},{118,2... | collective-permute-start | bytes 196616 | tf_op jit(solution)/shard_map/ppermute | solution.py:385
  8.4 6.5 %collective-permute-start.4 = (bf16[32,1024]{1,0:T(8,128)(2,1)S(1)}, bf16[32,1024]{1,0:T(8,128)(2,1)S(1)}, u32[]{:S(2)}, u32[]{:S(2)}) collective-permute-start(bf16[32,1024]{1,0:T(8,128)(2,1)S(1)} %get-tuple-element.31), channel_id=1, source_target_pairs={{112,192},{113,193},{114,194},{115,195},{116,196},{117,197},{118,1... | collective-permute-start | bytes 196616 | tf_op jit(solution)/shard_map/ppermute | solution.py:385
  9.7 5.2 %collective-permute-start.3 = (bf16[32,1024]{1,0:T(8,128)(2,1)S(1)}, bf16[32,1024]{1,0:T(8,128)(2,1)S(1)}, u32[]{:S(2)}, u32[]{:S(2)}) collective-permute-start(bf16[32,1024]{1,0:T(8,128)(2,1)S(1)} %get-tuple-element.32), channel_id=1, source_target_pairs={{112,176},{113,177},{114,178},{115,179},{116,180},{117,181},{118,1... | collective-permute-start | bytes 196616 | tf_op jit(solution)/shard_map/ppermute | solution.py:385
  11.0 3.9 %collective-permute-start.2 = (bf16[32,1024]{1,0:T(8,128)(2,1)S(1)}, bf16[32,1024]{1,0:T(8,128)(2,1)S(1)}, u32[]{:S(2)}, u32[]{:S(2)}) collective-permute-start(bf16[32,1024]{1,0:T(8,128)(2,1)S(1)} %get-tuple-element.33), channel_id=1, source_target_pairs={{112,160},{113,161},{114,162},{115,163},{116,164},{117,165},{118,1... | collective-permute-start | bytes 196616 | tf_op jit(solution)/shard_map/ppermute | solution.py:385
  12.3 3.9 %collective-permute-start = (bf16[32,1024]{1,0:T(8,128)(2,1)S(1)}, bf16[32,1024]{1,0:T(8,128)(2,1)S(1)}, u32[]{:S(2)}, u32[]{:S(2)}) collective-permute-start(bf16[32,1024]{1,0:T(8,128)(2,1)S(1)} %get-tuple-element.34), channel_id=1, source_target_pairs={{112,128},{113,129},{114,130},{115,131},{116,132},{117,133},{118,1... | collective-permute-start | bytes 196616 | tf_op jit(solution)/shard_map/ppermute | solution.py:385
  13.6 3.3 %collective-permute-start.1 = (bf16[32,1024]{1,0:T(8,128)(2,1)S(1)}, bf16[32,1024]{1,0:T(8,128)(2,1)S(1)}, u32[]{:S(2)}, u32[]{:S(2)}) collective-permute-start(bf16[32,1024]{1,0:T(8,128)(2,1)S(1)} %get-tuple-element.29), channel_id=1, source_target_pairs={{112,144},{113,145},{114,146},{115,147},{116,148},{117,149},{118,1... | collective-permute-start | bytes 196616 | tf_op jit(solution)/shard_map/ppermute | solution.py:385
  17.7 1.4 collective-permute-start.9
  48.6 7.7 %collective-permute-start.11 = (bf16[8,32,4096]{2,1,0:T(8,128)(2,1)S(1)}, bf16[8,32,4096]{2,1,0:T(8,128)(2,1)}, u32[]{:S(2)}, u32[]{:S(2)}) collective-permute-start(bf16[8,32,4096]{2,1,0:T(8,128)(2,1)S(1)} %all_to_all.15.x_ref), channel_id=1, source_target_pairs={{128,129},{129,128},{130,131},{131,130},{132,133},{133,132},{134,1... | collective-permute-start | bytes 6291464 | tf_op jit(solution)/shard_map/ppermute | solution.py:336
  61.0 26.1 %collective-permute-start.12 = (bf16[256,512]{1,0:T(8,128)(2,1)S(1)}, bf16[256,512]{1,0:T(8,128)(2,1)S(1)}, u32[]{:S(2)}, u32[]{:S(2)}) collective-permute-start(bf16[256,512]{1,0:T(8,128)(2,1)S(1)} %get-tuple-element.17), channel_id=1, source_target_pairs={{128,64},{129,65},{130,66},{131,67},{132,68},{133,69},{134,70},{13... | collective-permute-start | bytes 786440 | tf_op jit(solution)/shard_map/ppermute | solution.py:349
  62.3 27.1 %collective-permute-start.13 = (f32[256,512]{1,0:T(8,128)S(1)}, f32[256,512]{1,0:T(8,128)S(1)}, u32[]{:S(2)}, u32[]{:S(2)}) collective-permute-start(f32[256,512]{1,0:T(8,128)S(1)} %get-tuple-element.18), channel_id=1, source_target_pairs={{128,136},{129,137},{130,138},{131,139},{132,140},{133,141},{134,1... | collective-permute-start | bytes 1572872 | tf_op jit(solution)/shard_map/ppermute | solution.py:336
  87.0 13.8 %collective-permute-start.14 = (bf16[256,512]{1,0:T(8,128)(2,1)S(1)}, bf16[256,512]{1,0:T(8,128)(2,1)S(1)}, u32[]{:S(2)}, u32[]{:S(2)}) collective-permute-start(bf16[256,512]{1,0:T(8,128)(2,1)S(1)} %collective-permute-done.12.after_ref), channel_id=1, source_target_pairs={{64,136},{65,137},{66,138},{67,139},{68,140},{69,141},{70,142},{71... | collective-permute-start | bytes 786440 | tf_op jit(solution)/shard_map/ppermute | solution.py:353
  103.6 1.7 collective-permute-start.17
  104.5 13.3 %collective-permute-start.15 = (bf16[256,1024]{1,0:T(8,128)(2,1)S(1)}, bf16[256,1024]{1,0:T(8,128)(2,1)S(1)}, u32[]{:S(2)}, u32[]{:S(2)}) collective-permute-start(bf16[256,1024]{1,0:T(8,128)(2,1)S(1)} %get-tuple-element.26.g), channel_id=1, source_target_pairs={{128,136},{129,137},{130,138},{131,139},{132,140},{133,141},{134,1... | collective-permute-start | bytes 1572872 | tf_op jit(solution)/shard_map/ppermute | solution.py:336
  110.6 20.7 %all-to-all-start.1 = ((bf16[8,32,2048]{2,1,0:T(8,128)(2,1)}), bf16[8,32,2048]{2,1,0:T(8,128)(2,1)}, u32[]{:S(2)}, u32[]{:S(2)}) async-start(bf16[8,32,2048]{2,1,0:T(8,128)(2,1)} %shard_map.84), calls=%async_computation.1 | async-start | bytes 2097152 | tf_op jit(solution)/shard_map/all_to_all | solution.py:358
  131.3 18.6 %all-to-all-start.2 = ((bf16[8,32,2048]{2,1,0:T(8,128)(2,1)}), bf16[8,32,2048]{2,1,0:T(8,128)(2,1)S(1)}, u32[]{:S(2)}, u32[]{:S(2)}) async-start(bf16[8,32,2048]{2,1,0:T(8,128)(2,1)} %shard_map.83), calls=%async_computation.2 | async-start | bytes 2097152 | tf_op jit(solution)/shard_map/all_to_all | solution.py:358
  150.9 2.8 %collective-permute-start.21 = (bf16[32,1024]{1,0:T(8,128)(2,1)S(1)}, bf16[32,1024]{1,0:T(8,128)(2,1)S(1)}, u32[]{:S(2)}, u32[]{:S(2)}) collective-permute-start(bf16[32,1024]{1,0:T(8,128)(2,1)S(1)} %bitcast.81), channel_id=1, source_target_pairs={{128,138},{129,139},{130,136},{131,137},{132,130},{133,131},{134,1... | collective-permute-start | bytes 196616 | tf_op jit(solution)/shard_map/ppermute | solution.py:336
  151.6 2.1 collective-permute-start.20
  152.3 1.4 collective-permute-start.19
  154.4 54.4 %collective-permute-start.23 = (bf16[64,1024]{1,0:T(8,128)(2,1)S(1)}, bf16[64,1024]{1,0:T(8,128)(2,1)S(1)}, u32[]{:S(2)}, u32[]{:S(2)}) collective-permute-start(bf16[64,1024]{1,0:T(8,128)(2,1)S(1)} %pad_maximum_fusion.2), channel_id=1, source_target_pairs={{128,112},{129,113},{130,114},{131,115},{132,116},{133,117},{134,1... | collective-permute-start | bytes 393224 | tf_op jit(solution)/shard_map/ppermute | solution.py:448
  157.0 54.0 %collective-permute-start.24 = (bf16[64,1024]{1,0:T(8,128)(2,1)S(1)}, bf16[64,1024]{1,0:T(8,128)(2,1)S(1)}, u32[]{:S(2)}, u32[]{:S(2)}) collective-permute-start(bf16[64,1024]{1,0:T(8,128)(2,1)S(1)} %pad_maximum_fusion.2), channel_id=1, source_target_pairs={{144,112},{145,113},{146,114},{147,115},{148,116},{149,117},{150,1... | collective-permute-start | bytes 393224 | tf_op jit(solution)/shard_map/ppermute | solution.py:448
  158.2 52.7 %collective-permute-start.25 = (bf16[64,1024]{1,0:T(8,128)(2,1)S(1)}, bf16[64,1024]{1,0:T(8,128)(2,1)S(1)}, u32[]{:S(2)}, u32[]{:S(2)}) collective-permute-start(bf16[64,1024]{1,0:T(8,128)(2,1)S(1)} %pad_maximum_fusion.2), channel_id=1, source_target_pairs={{160,112},{161,113},{162,114},{163,115},{164,116},{165,117},{166,1... | collective-permute-start | bytes 393224 | tf_op jit(solution)/shard_map/ppermute | solution.py:448
  159.5 51.7 %collective-permute-start.26 = (bf16[64,1024]{1,0:T(8,128)(2,1)S(1)}, bf16[64,1024]{1,0:T(8,128)(2,1)S(1)}, u32[]{:S(2)}, u32[]{:S(2)}) collective-permute-start(bf16[64,1024]{1,0:T(8,128)(2,1)S(1)} %pad_maximum_fusion.2), channel_id=1, source_target_pairs={{176,112},{177,113},{178,114},{179,115},{180,116},{181,117},{182,1... | collective-permute-start | bytes 393224 | tf_op jit(solution)/shard_map/ppermute | solution.py:448
  (11 other events, 99.8 us)
